TPU v7x, 32 devices: a whole 2x2x4 slice. The times are simulated.
32 devices in a mesh: gx: 4 (over z), gy: 8 (over y, x, core).
Axes of the slice: x: 2, y: 2, z: 4, core: 2. Of those that a mesh axis runs over, the one named last changes fastest.
Arguments:
- start_block: float32 [4, 8, 64, 16, 128], P('gx', 'gy')
- tiles: float32 [4, 8, 64, 4, 128, 128], P('gx', 'gy'), may hold values from -0.15625 to 0.15625
- tile_cols: int32 [4, 8, 64, 4], P('gx', 'gy'), may hold values from 0 to 63
- node_diag: float32 [4, 8, 64, 128], P('gx', 'gy'), may hold values from 3 to 24
- face_tiles: float32 [4, 8, 2, 24, 128, 128], P('gx', 'gy'), may hold values from -0.15625 to 0.15625
- face_rows: int32 [4, 8, 4, 24], P('gx', 'gy'), may hold values from 0 to 63, as said below
- filter_bounds: float32 [2], replicated, may hold values from 8 to 30, as said below
Outputs:
- basis: float32 [4, 8, 64, 16, 128], P('gx', 'gy')
- projected: float32 [16, 16], replicated
Inputs may be any that keep to these rules, and one draw needn't show every extreme that they name: `tile_cols`: each stored tile's column is a tile row of the same subdomain. `face_rows`: each of the four lists of a subdomain names 24 distinct tile rows. `filter_bounds`: entry 0 lies in 8 to 10 and entry 1 in 26 to 30.
All inputs are finite; a program needn't handle non-finite values.
Results may differ from a plain program's by a relative error of at most 0.0003.
Values sent between devices are 32-bit elements; how exact they have to be, the bound alone decides.
No kernel may reach another device: no remote copies, remote signals or barrier semaphores. Data moves between devices by JAX's collectives and lax.ppermute only.
A program may use at most 128 MiB of HBM per device.

v0:
```python
import jax
import jax.numpy as jnp
from jax import lax
from jax.sharding import PartitionSpec as P

HIGH = lax.Precision.HIGHEST


def from_behind(shard, axis, by):
    peers = lax.axis_size(axis)
    pairs = [(i, i + by) for i in range(peers) if 0 <= i + by < peers]
    return lax.ppermute(shard, axis, pairs)


def local_apply(block, tiles, cols, diag):
    count = block.shape[0]
    gathered = block[cols]
    forward = jnp.einsum("rkcb,rkab->rca", gathered, tiles, precision=HIGH)
    terms = jnp.einsum("rca,rkab->rkcb", block, tiles, precision=HIGH)
    onehot = (cols.reshape(-1)[:, None] == jnp.arange(count, dtype=jnp.int32)[None, :]).astype(
        block.dtype
    )
    backward = jnp.einsum(
        "mr,mcb->rcb", onehot, terms.reshape((-1,) + terms.shape[2:]), precision=HIGH
    )
    return diag[:, None, :] * block + forward + backward


def place(rows, data, count):
    onehot = (rows[:, None] == jnp.arange(count, dtype=jnp.int32)[None, :]).astype(data.dtype)
    return jnp.einsum("fr,fcn->rcn", onehot, data, precision=HIGH)


def partial_products(left, right):
    return jnp.einsum("rcn,rdn->cd", left, right, precision=HIGH)


def shards(start_block, tiles, tile_cols, node_diag, face_tiles, face_rows, filter_bounds):
    block = start_block[0, 0]
    stored = tiles[0, 0]
    cols = tile_cols[0, 0]
    diag = node_diag[0, 0]
    coupling = face_tiles[0, 0]
    rows = face_rows[0, 0]
    count = block.shape[0]
    nodes = count * block.shape[2] * lax.axis_size("gx") * lax.axis_size("gy")

    def face_x(field):
        upper = from_behind(field[rows[1]], "gx", -1)
        total = place(
            rows[0], jnp.einsum("fcb,fab->fca", upper, coupling[0], precision=HIGH), count
        )
        plus = field[rows[0]]
        outgoing = jnp.einsum("fca,fab->fcb", plus, coupling[0], precision=HIGH)
        total = total + place(rows[1], from_behind(outgoing, "gx", 1), count)
        return total

    def face_y(field):
        upper = from_behind(field[rows[3]], "gy", -1)
        total = place(
            rows[2], jnp.einsum("fcb,fab->fca", upper, coupling[1], precision=HIGH), count
        )
        plus = field[rows[2]]
        outgoing = jnp.einsum("fca,fab->fcb", plus, coupling[1], precision=HIGH)
        total = total + place(rows[3], from_behind(outgoing, "gy", 1), count)
        return total

    def operate(field):
        return local_apply(field, stored, cols, diag) + face_x(field) + face_y(field)

    half = (filter_bounds[1] - filter_bounds[0]) / 2.0
    centre = (filter_bounds[1] + filter_bounds[0]) / 2.0
    first = (operate(block) - centre * block) / half
    second = 2.0 * (operate(first) - centre * first) / half - block
    filtered = 2.0 * (operate(second) - centre * second) / half - first
    width = filtered.shape[1]
    identity = jnp.eye(width, dtype=jnp.float32)
    gram = lax.psum(partial_products(filtered, filtered), ("gx", "gy")) / nodes
    factor = jnp.linalg.cholesky(gram)
    inverse = lax.linalg.triangular_solve(factor, identity, left_side=True, lower=True)
    basis = jnp.einsum("cd,rdn->rcn", inverse, filtered, precision=HIGH)
    image = operate(basis)
    raw = lax.psum(partial_products(basis, image), ("gx", "gy")) / nodes
    projected = (raw + raw.T) / 2.0
    return (basis[None, None], projected)


def solution(mesh):
    in_specs = (
        P("gx", "gy", None, None, None),
        P("gx", "gy", None, None, None, None),
        P("gx", "gy", None, None),
        P("gx", "gy", None, None),
        P("gx", "gy", None, None, None, None),
        P("gx", "gy", None, None),
        P(),
    )
    out_specs = (P("gx", "gy", None, None, None), P())
    return jax.shard_map(shards, mesh=mesh, in_specs=in_specs, out_specs=out_specs, check_vma=False)
```

profile of v0, /device:TPU:0, one launch (start us, length us, event | category | flops | bytes accessed | tf_op | source)
XLA Modules:
  0.0 367.7 jit_solution(14014567686671160945)
XLA Ops:
  3.7 2.8 fusion.52
  6.6 5.6 %collective-permute-start.1 = (f32[24,16,128]{2,0,1:T(8,128)S(1)}, f32[24,16,128]{2,0,1:T(8,128)}, u32[]{:S(2)}, u32[]{:S(2)}) collective-permute-start(f32[24,16,128]{2,0,1:T(8,128)S(1)} %copy.60), channel_id=1, source_target_pairs={{0,8},{8,16},{16,24},{1,9},{9,17},{17,25},{2,10},{10,18},{18,26},{... | collective-permute-start | bytes 589832 | tf_op jit(solution)/shard_map/ppermute | solution.py:12
  30.0 3.1 gather_fusion
  33.3 11.8 %fusion.12 = f32[64,4,128,16]{2,3,1,0:T(8,128)S(1)} fusion(f32[1,1,64,4,128,128]{5,4,3,2,1,0:T(8,128)} %param.8, f32[1,1,64,16,128]{4,3,2,1,0:T(8,128)} %param.7), kind=kOutput, calls=%fused_computation.32 | convolution fusion | flops 805306368 | bytes 19398656 | tf_op jit(solution)/shard_map/rca,rkab->rkcb/dot_general | solution.py:19
  46.6 3.5 fusion.38
  50.6 3.6 fusion.54
  57.6 18.4 %fusion.143 = f32[64,16,128]{2,1,0:T(8,128)} fusion(f32[64,4,16,128]{3,2,1,0:T(8,128)S(1)} %bitcast.352, f32[1,1,64,4,128,128]{5,4,3,2,1,0:T(8,128)} %param.8, f32[64,16,128]{2,0,1:T(8,128)S(1)} %fusion.219, f32[64,16,128]{2,0,1:T(8,128)S(1)} %fusion.182, f32[64,16,128]{2,0,1:T(8,128)S(1)} %fusion.206, f32[64,16,128]{2,0,1:T(8,128)S(1)} %fusion.184, ...), kind=kOutput, calls=%fused_computation.105 | convolution fusion | flops 806617088 | bytes 22577160 | tf_op jit(solution)/shard_map/rkcb,rkab->rca/dot_general | solution.py:18
  84.3 12.6 %fusion.8 = f32[64,16,4,128]{3,1,2,0:T(8,128)} fusion(f32[1,1,64,4,128,128]{5,4,3,2,1,0:T(8,128)} %param.8, f32[64,16,128]{2,1,0:T(8,128)} %fusion.143), kind=kOutput, calls=%fused_computation.28 | convolution fusion | flops 805306368 | bytes 19398656 | tf_op jit(solution)/shard_map/rca,rkab->rkcb/dot_general | solution.py:19
  96.9 3.1 gather_fusion.5
  101.6 4.6 %collective-permute-start.5 = (f32[24,16,128]{2,0,1:T(8,128)S(1)}, f32[24,16,128]{2,0,1:T(8,128)S(1)}, u32[]{:S(2)}, u32[]{:S(2)}) collective-permute-start(f32[24,16,128]{2,0,1:T(8,128)S(1)} %copy.66), channel_id=1, source_target_pairs={{0,8},{8,16},{16,24},{1,9},{9,17},{17,25},{2,10},{10,18},{18,26},{... | collective-permute-start | bytes 589832 | tf_op jit(solution)/shard_map/ppermute | solution.py:12
  107.6 3.4 collective-permute-start.7
  116.1 2.5 fusion.34
  126.4 17.5 %fusion.125 = f32[64,16,128]{2,1,0:T(8,128)S(1)} fusion(f32[64,4,16,128]{3,2,1,0:T(8,128)S(1)} %bitcast.346, f32[1,1,64,4,128,128]{5,4,3,2,1,0:T(8,128)} %param.8, f32[64,16,128]{2,0,1:T(8,128)} %fusion.217, f32[64,16,128]{2,0,1:T(8,128)} %fusion.178, f32[64,16,128]{2,0,1:T(8,128)} %fusion.204, f32[64,16,128]{2,0,1:T(8,128)} %fusion.180, ...), kind=kOutput, calls=%fused_computation.99 | convolution fusion | flops 806879232 | bytes 23101448 | tf_op jit(solution)/shard_map/rkcb,rkab->rca/dot_general | solution.py:18
  144.7 9.4 %fusion.4 = f32[64,16,4,128]{3,1,2,0:T(8,128)} fusion(f32[1,1,64,4,128,128]{5,4,3,2,1,0:T(8,128)S(1)} %bitcast.333, f32[64,16,128]{2,1,0:T(8,128)S(1)} %fusion.125), kind=kOutput, calls=%fused_computation.24 | convolution fusion | flops 805306368 | bytes 19398656 | tf_op jit(solution)/shard_map/rca,rkab->rkcb/dot_general | solution.py:19
  154.1 3.1 gather_fusion.10
  167.0 4.5 %collective-permute-start.9 = (f32[24,16,128]{2,0,1:T(8,128)S(1)}, f32[24,16,128]{2,0,1:T(8,128)S(1)}, u32[]{:S(2)}, u32[]{:S(2)}) collective-permute-start(f32[24,16,128]{2,0,1:T(8,128)S(1)} %copy.72), channel_id=1, source_target_pairs={{0,8},{8,16},{16,24},{1,9},{9,17},{17,25},{2,10},{10,18},{18,26},{... | collective-permute-start | bytes 589832 | tf_op jit(solution)/shard_map/ppermute | solution.py:12
  173.1 4.3 %collective-permute-start.11 = (f32[24,16,128]{2,0,1:T(8,128)S(1)}, f32[24,16,128]{2,0,1:T(8,128)S(1)}, u32[]{:S(2)}, u32[]{:S(2)}) collective-permute-start(f32[24,16,128]{2,0,1:T(8,128)S(1)} %copy.74), channel_id=1, source_target_pairs={{0,1},{1,2},{2,3},{3,4},{4,5},{5,6},{6,7},{8,9},{9,10},{10,11},{11... | collective-permute-start | bytes 589832 | tf_op jit(solution)/shard_map/ppermute | solution.py:12
  190.7 17.7 %fusion.101 = f32[64,16,128]{2,1,0:T(8,128)S(1)} fusion(f32[64,16,128]{2,1,0:T(8,128)S(1)} %copy-done.2, f32[64,4,16,128]{3,2,1,0:T(8,128)S(1)} %bitcast.345, f32[1,1,64,4,128,128]{5,4,3,2,1,0:T(8,128)} %param.8, f32[64,16,128]{2,0,1:T(8,128)S(1)} %fusion.215, f32[64,16,128]{2,0,1:T(8,128)S(1)} %fusion.174, f32[64,16,128]{2,0,1:T(8,128)S(1)} %fusion.202, ...), kind=kOutput, calls=%fused_computation.91 | convolution fusion | flops 806879232 | bytes 23101448 | tf_op jit(solution)/shard_map/rkcb,rkab->rca/dot_general | solution.py:18
  210.0 45.0 %psum.14 = f32[16,16]{0,1:T(8,128)S(1)} all-reduce(f32[16,16]{0,1:T(8,128)S(1)} %convolution_bitcast_fusion.2), channel_id=1, replica_groups=mesh['gx'=4,'gy'=8] {'gx','gy'}, use_global_device_ids=true, to_apply=%region_0.0 | all-reduce | flops 256 | bytes 2048 | tf_op jit(solution)/shard_map/psum | solution.py:78
  261.0 12.0 %fusion = f32[64,16,4,128]{3,1,2,0:T(8,128)} fusion(f32[1,1,64,4,128,128]{5,4,3,2,1,0:T(8,128)} %param.8, f32[64,128,16]{1,2,0:T(8,128)S(1)} %fusion.246), kind=kOutput, calls=%fused_computation.20 | convolution fusion | flops 805306368 | bytes 19398656 | tf_op jit(solution)/shard_map/rca,rkab->rkcb/dot_general | solution.py:19
  272.9 3.1 gather_fusion.15
  289.8 2.7 collective-permute-start.13
  304.1 17.6 %fusion.77 = f32[64,16,128]{2,1,0:T(8,128)S(1)} fusion(f32[64,4,16,128]{3,2,1,0:T(8,128)S(1)} %bitcast.351, f32[1,1,64,4,128,128]{5,4,3,2,1,0:T(8,128)} %param.8, f32[64,16,128]{2,0,1:T(8,128)S(1)} %fusion.166, f32[64,16,128]{2,0,1:T(8,128)S(1)} %fusion.168, f32[64,16,128]{2,0,1:T(8,128)S(1)} %fusion.170, f32[64,16,128]{2,0,1:T(8,128)S(1)} %fusion.172, ...), kind=kOutput, calls=%fused_computation.83 | convolution fusion | flops 806223872 | bytes 22577152 | tf_op jit(solution)/shard_map/rkcb,rkab->rca/dot_general | solution.py:18
  322.5 44.2 %psum.15 = f32[16,16]{0,1:T(8,128)S(1)} all-reduce(f32[16,16]{0,1:T(8,128)S(1)} %convolution_bitcast_fusion), channel_id=1, replica_groups=mesh['gx'=4,'gy'=8] {'gx','gy'}, use_global_device_ids=true, to_apply=%region_3.4 | all-reduce | flops 256 | bytes 2048 | tf_op jit(solution)/shard_map/psum | solution.py:83
  (199 shorter events, 107.3 us)
Async XLA Ops:
  6.5 20.1 %copy-start.39 = (f32[2]{0:T(128)S(1)}, f32[2]{0:T(128)}, u32[]{:S(2)}) copy-start(f32[2]{0:T(128)} %param.13) | copy-start | bytes 28
  6.5 23.2 %copy-start.37 = (s32[1,1,64,4]{2,3,1,0:T(4,128)S(1)}, s32[1,1,64,4]{2,3,1,0:T(4,128)}, u32[]{:S(2)}) copy-start(s32[1,1,64,4]{2,3,1,0:T(4,128)} %param.9) | copy-start | bytes 3076
  6.6 48.1 %collective-permute-start.1 = (f32[24,16,128]{2,0,1:T(8,128)S(1)}, f32[24,16,128]{2,0,1:T(8,128)}, u32[]{:S(2)}, u32[]{:S(2)}) collective-permute-start(f32[24,16,128]{2,0,1:T(8,128)S(1)} %copy.60), channel_id=1, source_target_pairs={{0,8},{8,16},{16,24},{1,9},{9,17},{17,25},{2,10},{10,18},{18,26},{... | collective-permute-start | bytes 589832 | tf_op jit(solution)/shard_map/ppermute | solution.py:12
  12.9 20.3 %copy-start.34 = (s32[1024]{0:T(1024)}, s32[1024]{0:T(1024)S(1)}, u32[]{:S(2)}) copy-start(s32[1024]{0:T(1024)S(1)} %pad_clamp_fusion) | copy-start | bytes 12292
  16.7 39.5 %collective-permute-start.3 = (f32[24,16,128]{2,0,1:T(8,128)}, f32[24,16,128]{2,0,1:T(8,128)}, u32[]{:S(2)}, u32[]{:S(2)}) collective-permute-start(f32[24,16,128]{2,0,1:T(8,128)} %copy.62), channel_id=1, source_target_pairs={{0,1},{1,2},{2,3},{3,4},{4,5},{5,6},{6,7},{8,9},{9,10},{10,11},{11... | collective-permute-start | bytes 589832 | tf_op jit(solution)/shard_map/ppermute | solution.py:12
  21.7 24.9 %collective-permute-start.2 = (f32[24,16,128]{2,1,0:T(8,128)}, f32[24,16,128]{2,1,0:T(8,128)}, u32[]{:S(2)}, u32[]{:S(2)}) collective-permute-start(f32[24,16,128]{2,1,0:T(8,128)} %gather_fusion.3), channel_id=1, source_target_pairs={{1,0},{2,1},{3,2},{4,3},{5,4},{6,5},{7,6},{9,8},{10,9},{11,10},{12... | collective-permute-start | bytes 589832 | tf_op jit(solution)/shard_map/ppermute | solution.py:12
  25.3 25.3 %collective-permute-start = (f32[24,16,128]{2,1,0:T(8,128)}, f32[24,16,128]{2,1,0:T(8,128)}, u32[]{:S(2)}, u32[]{:S(2)}) collective-permute-start(f32[24,16,128]{2,1,0:T(8,128)} %gather_fusion.1), channel_id=1, source_target_pairs={{8,0},{16,8},{24,16},{9,1},{17,9},{25,17},{10,2},{18,10},{26,18},{... | collective-permute-start | bytes 589832 | tf_op jit(solution)/shard_map/ppermute | solution.py:12
  101.6 22.3 %collective-permute-start.5 = (f32[24,16,128]{2,0,1:T(8,128)S(1)}, f32[24,16,128]{2,0,1:T(8,128)S(1)}, u32[]{:S(2)}, u32[]{:S(2)}) collective-permute-start(f32[24,16,128]{2,0,1:T(8,128)S(1)} %copy.66), channel_id=1, source_target_pairs={{0,8},{8,16},{16,24},{1,9},{9,17},{17,25},{2,10},{10,18},{18,26},{... | collective-permute-start | bytes 589832 | tf_op jit(solution)/shard_map/ppermute | solution.py:12
  107.6 17.5 %collective-permute-start.7 = (f32[24,16,128]{2,0,1:T(8,128)S(1)}, f32[24,16,128]{2,0,1:T(8,128)S(1)}, u32[]{:S(2)}, u32[]{:S(2)}) collective-permute-start(f32[24,16,128]{2,0,1:T(8,128)S(1)} %copy.68), channel_id=1, source_target_pairs={{0,1},{1,2},{2,3},{3,4},{4,5},{5,6},{6,7},{8,9},{9,10},{10,11},{11... | collective-permute-start | bytes 589832 | tf_op jit(solution)/shard_map/ppermute | solution.py:12
  111.0 5.1 %collective-permute-start.6 = (f32[24,16,128]{2,1,0:T(8,128)S(1)}, f32[24,16,128]{2,1,0:T(8,128)S(1)}, u32[]{:S(2)}, u32[]{:S(2)}) collective-permute-start(f32[24,16,128]{2,1,0:T(8,128)S(1)} %copy-done.24), channel_id=1, source_target_pairs={{1,0},{2,1},{3,2},{4,3},{5,4},{6,5},{7,6},{9,8},{10,9},{11,10},{12... | collective-permute-start | bytes 589832 | tf_op jit(solution)/shard_map/ppermute | solution.py:12
  112.3 7.7 %collective-permute-start.4 = (f32[24,16,128]{2,1,0:T(8,128)S(1)}, f32[24,16,128]{2,1,0:T(8,128)S(1)}, u32[]{:S(2)}, u32[]{:S(2)}) collective-permute-start(f32[24,16,128]{2,1,0:T(8,128)S(1)} %copy-done.21), channel_id=1, source_target_pairs={{8,0},{16,8},{24,16},{9,1},{17,9},{25,17},{10,2},{18,10},{26,18},{... | collective-permute-start | bytes 589832 | tf_op jit(solution)/shard_map/ppermute | solution.py:12
  113.8 30.8 %slice-start = ((s8[16777216]{0:T(1024)(128)(4,1)}), s8[4194304]{0:T(1024)(128)(4,1)S(1)}, s32[]{:S(2)}) async-start(s8[16777216]{0:T(1024)(128)(4,1)} %bitcast.332), calls=%async_computation | async-start | bytes 8388608
  123.8 20.9 %slice-start.1 = ((s8[16777216]{0:T(1024)(128)(4,1)}), s8[4194304]{0:T(1024)(128)(4,1)S(1)}, s32[]{:S(2)}) async-start(s8[16777216]{0:T(1024)(128)(4,1)} %bitcast.332), calls=%async_computation.1 | async-start | bytes 8388608
  126.4 18.3 %slice-start.2 = ((s8[16777216]{0:T(1024)(128)(4,1)}), s8[4194304]{0:T(1024)(128)(4,1)S(1)}, s32[]{:S(2)}) async-start(s8[16777216]{0:T(1024)(128)(4,1)} %bitcast.332), calls=%async_computation.2 | async-start | bytes 8388608
  126.4 18.3 %slice-start.3 = ((s8[16777216]{0:T(1024)(128)(4,1)}), s8[4194304]{0:T(1024)(128)(4,1)S(1)}, s32[]{:S(2)}) async-start(s8[16777216]{0:T(1024)(128)(4,1)} %bitcast.332), calls=%async_computation.3 | async-start | bytes 8388608
  165.5 14.7 %copy-start.12 = (f32[64,16,4,128]{3,1,2,0:T(8,128)S(1)}, f32[64,16,4,128]{3,1,2,0:T(8,128)}, u32[]{:S(2)}) copy-start(f32[64,16,4,128]{3,1,2,0:T(8,128)} %fusion.4) | copy-start | bytes 6291460
  167.0 22.7 %collective-permute-start.9 = (f32[24,16,128]{2,0,1:T(8,128)S(1)}, f32[24,16,128]{2,0,1:T(8,128)S(1)}, u32[]{:S(2)}, u32[]{:S(2)}) collective-permute-start(f32[24,16,128]{2,0,1:T(8,128)S(1)} %copy.72), channel_id=1, source_target_pairs={{0,8},{8,16},{16,24},{1,9},{9,17},{17,25},{2,10},{10,18},{18,26},{... | collective-permute-start | bytes 589832 | tf_op jit(solution)/shard_map/ppermute | solution.py:12
  173.1 17.2 %collective-permute-start.11 = (f32[24,16,128]{2,0,1:T(8,128)S(1)}, f32[24,16,128]{2,0,1:T(8,128)S(1)}, u32[]{:S(2)}, u32[]{:S(2)}) collective-permute-start(f32[24,16,128]{2,0,1:T(8,128)S(1)} %copy.74), channel_id=1, source_target_pairs={{0,1},{1,2},{2,3},{3,4},{4,5},{5,6},{6,7},{8,9},{9,10},{10,11},{11... | collective-permute-start | bytes 589832 | tf_op jit(solution)/shard_map/ppermute | solution.py:12
  177.4 5.5 %collective-permute-start.10 = (f32[24,16,128]{2,1,0:T(8,128)S(1)}, f32[24,16,128]{2,1,0:T(8,128)S(1)}, u32[]{:S(2)}, u32[]{:S(2)}) collective-permute-start(f32[24,16,128]{2,1,0:T(8,128)S(1)} %copy-done.25), channel_id=1, source_target_pairs={{1,0},{2,1},{3,2},{4,3},{5,4},{6,5},{7,6},{9,8},{10,9},{11,10},{12... | collective-permute-start | bytes 589832 | tf_op jit(solution)/shard_map/ppermute | solution.py:12
  178.9 7.8 %collective-permute-start.8 = (f32[24,16,128]{2,1,0:T(8,128)S(1)}, f32[24,16,128]{2,1,0:T(8,128)S(1)}, u32[]{:S(2)}, u32[]{:S(2)}) collective-permute-start(f32[24,16,128]{2,1,0:T(8,128)S(1)} %copy-done.22), channel_id=1, source_target_pairs={{8,0},{16,8},{24,16},{9,1},{17,9},{25,17},{10,2},{18,10},{26,18},{... | collective-permute-start | bytes 589832 | tf_op jit(solution)/shard_map/ppermute | solution.py:12
  285.8 17.3 %collective-permute-start.15 = (f32[24,16,128]{2,1,0:T(8,128)S(1)}, f32[24,16,128]{2,1,0:T(8,128)S(1)}, u32[]{:S(2)}, u32[]{:S(2)}) collective-permute-start(f32[24,16,128]{2,1,0:T(8,128)S(1)} %fusion.24), channel_id=1, source_target_pairs={{0,1},{1,2},{2,3},{3,4},{4,5},{5,6},{6,7},{8,9},{9,10},{10,11},{11... | collective-permute-start | bytes 589832 | tf_op jit(solution)/shard_map/ppermute | solution.py:12
  287.1 8.5 %collective-permute-start.14 = (f32[24,16,128]{2,1,0:T(8,128)}, f32[24,16,128]{2,1,0:T(8,128)S(1)}, u32[]{:S(2)}, u32[]{:S(2)}) collective-permute-start(f32[24,16,128]{2,1,0:T(8,128)} %gather_fusion.18), channel_id=1, source_target_pairs={{1,0},{2,1},{3,2},{4,3},{5,4},{6,5},{7,6},{9,8},{10,9},{11,10},{12... | collective-permute-start | bytes 589832 | tf_op jit(solution)/shard_map/ppermute | solution.py:12
  289.8 13.8 %collective-permute-start.13 = (f32[24,16,128]{2,1,0:T(8,128)S(1)}, f32[24,16,128]{2,1,0:T(8,128)S(1)}, u32[]{:S(2)}, u32[]{:S(2)}) collective-permute-start(f32[24,16,128]{2,1,0:T(8,128)S(1)} %fusion.40), channel_id=1, source_target_pairs={{0,8},{8,16},{16,24},{1,9},{9,17},{17,25},{2,10},{10,18},{18,26},{... | collective-permute-start | bytes 589832 | tf_op jit(solution)/shard_map/ppermute | solution.py:12
  292.5 7.6 %collective-permute-start.12 = (f32[24,16,128]{2,1,0:T(8,128)S(1)}, f32[24,16,128]{2,1,0:T(8,128)S(1)}, u32[]{:S(2)}, u32[]{:S(2)}) collective-permute-start(f32[24,16,128]{2,1,0:T(8,128)S(1)} %copy-done.23), channel_id=1, source_target_pairs={{8,0},{16,8},{24,16},{9,1},{17,9},{25,17},{10,2},{18,10},{26,18},{... | collective-permute-start | bytes 589832 | tf_op jit(solution)/shard_map/ppermute | solution.py:12
  (36 other events, 253.3 us)
where the time goes:
time: 373 us; the launch traced here: 368 us
  matrix products  175 us (47%)
  blocking collectives  89.2 us (24%)
  local copies, waits for them, and re-layouts  49.2 us (13%)
  starting transfers between devices  39.4 us (11%)
  other arithmetic  7.36 us (2%)
  between operations  4.25 us (1%)
    dot_general x4, matrix products, local_apply(): forward = jnp.einsum('rkcb,rkab->rca', gathered, tiles, precision=HIGH)  71.1 us
    dot_general x4, matrix products, local_apply(): terms = jnp.einsum('rca,rkab->rkcb', block, tiles, precision=HIGH)  45.8 us
    psum x1, blocking collectives, shards(): gram = lax.psum(partial_products(filtered, filtered), ('gx', 'gy')) / nodes  45 us
    psum x1, blocking collectives, shards(): raw = lax.psum(partial_products(basis, image), ('gx', 'gy')) / nodes  44.2 us
    ppermute x16, starting transfers between devices, from_behind(): return lax.ppermute(shard, axis, pairs)  39.4 us
    dot_general x16, matrix products, place(): return jnp.einsum('fr,fcn->rcn', onehot, data, precision=HIGH)  12.8 us
    gather x4, local copies, waits for them, and re-layouts, local_apply(): gathered = block[cols]  12.5 us
    dot_general x4, matrix products, face_x(): jnp.einsum('fcb,fab->fca', upper, coupling[0], precision=HIGH)  11.2 us
  transfers between devices with their start and end apart: 16, of which 3 were waited for; matrix products, arithmetic and copies ran while one was open for 19% of the time, Pallas kernels for 0%

commit v1 on v0

v1 whole, which is shorter than its diff:
```python
import functools

import jax
import jax.numpy as jnp
from jax import lax
from jax.experimental import pallas as pl
from jax.experimental.pallas import tpu as pltpu
from jax.sharding import PartitionSpec as P

F32 = jnp.float32
BF16 = jnp.bfloat16
MIB = 1 << 20
VM = pl.BlockSpec(memory_space=pltpu.VMEM)
SM = pl.BlockSpec(memory_space=pltpu.SMEM)
ANY = pl.BlockSpec(memory_space=pl.ANY)
cat = jnp.concatenate

ROWS = 8
SHRINK = 1.0 / 64.0


def split(x):
    high = x.astype(BF16)
    low = (x - high.astype(F32)).astype(BF16)
    return high, low


def stacked(x):
    return cat(split(x), axis=-2)


def dot_nn(x, t):
    return lax.dot_general(x, t, (((1,), (0,)), ((), ())), preferred_element_type=F32)


def dot_nt(x, t):
    return lax.dot_general(x, t, (((1,), (1,)), ((), ())), preferred_element_type=F32)


def fold(both, low=None):
    half = both.shape[0] // 2
    out = both[:half] + both[half:]
    return out if low is None else out + low


def two_piece(dot, x2, high, low):
    half = x2.shape[0] // 2
    return fold(dot(x2, high), dot(x2[:half], low))


def place_rows(w_ref, rows, which, data, j):
    at = rows[which, j]
    w_ref[at] = w_ref[at] + data


def leave(v_ref, v2_ref, rows, ch, cl, sends, products):
    faces = rows.shape[1]
    for axis in range(2):
        minus = sends[2 * axis]

        def copy(j, carry, axis=axis, minus=minus):
            minus[j] = v_ref[rows[2 * axis + 1, j]]
            return carry

        lax.fori_loop(0, faces, copy, 0, unroll=8)
    if not products:
        return

    def step(s, carry):
        outs = []
        for axis in range(2):
            for r in range(ROWS):
                j = s * ROWS + r
                x2 = v2_ref[rows[2 * axis, j]]
                outs.append((axis, j, two_piece(dot_nn, x2, ch[axis, j], cl[axis, j])))
        for axis, j, out in outs:
            sends[2 * axis + 1][j] = out
        return carry

    lax.fori_loop(0, faces // ROWS, step, 0)


def begin_kernel(rows, v, tiles, ch, cl, v2, mx, ox, my, oy):
    v2[...] = stacked(v[...])
    high, low = split(tiles[...])
    ch[...] = high
    cl[...] = low
    leave(v, v2, rows, ch, cl, (mx, ox, my, oy), True)


def local_rows(rows, cols, v2, highs, lows, wf, wb):
    outs = []
    for i, high, low in zip(rows, highs, lows):
        x2 = v2[i]
        g2 = cat([v2[cols[i, k]] for k in range(4)], axis=1)
        high = cat(high, axis=1)
        low = cat(low, axis=1)
        outs.append((two_piece(dot_nt, g2, high, low), two_piece(dot_nn, x2, high, low)))
    for i, (forward, backward) in zip(rows, outs):
        wf[i] = forward
        for k in range(4):
            at = cols[i, k]
            wb[at] = wb[at] + backward[:, k * 128 : (k + 1) * 128]


def first_kernel(cols, v2, tiles, wf, wb, th, tl, stage, sems):
    count = v2.shape[0]
    copies = count // ROWS

    def fetch(c):
        part = pl.ds(c * ROWS, ROWS)
        return pltpu.make_async_copy(tiles.at[part], stage.at[part], sems.at[c])

    for c in range(copies):
        fetch(c).start()
    wb[...] = jnp.zeros_like(wb)

    def step(c, carry):
        fetch(c).wait()
        rows, highs, lows = [], [], []
        for r in range(ROWS):
            i = c * ROWS + r
            pieces = [split(stage[i, k]) for k in range(4)]
            for k in range(4):
                th[i, k] = pieces[k][0]
                tl[i, k] = pieces[k][1]
            rows.append(i)
            highs.append([p[0] for p in pieces])
            lows.append([p[1] for p in pieces])
        local_rows(rows, cols, v2, highs, lows, wf, wb)
        return carry

    lax.fori_loop(0, copies, step, 0)


def local_kernel(cols, v2, th, tl, wf, wb):
    wb[...] = jnp.zeros_like(wb)

    def step(c, carry):
        rows = [c * ROWS + r for r in range(ROWS)]
        highs = [[th[i, k] for k in range(4)] for i in rows]
        lows = [[tl[i, k] for k in range(4)] for i in rows]
        local_rows(rows, cols, v2, highs, lows, wf, wb)
        return carry

    lax.fori_loop(0, v2.shape[0] // ROWS, step, 0)


def arrive(rows, flags, received, ch, cl, acc):
    faces = rows.shape[1]

    def step(s, carry):
        outs = []
        for axis in range(2):
            upper, lower = received[2 * axis], received[2 * axis + 1]
            for r in range(ROWS):
                j = s * ROWS + r
                u2 = stacked(jnp.where(flags[2 * axis] > 0, upper[j], 0.0))
                gain = two_piece(dot_nt, u2, ch[axis, j], cl[axis, j])
                outs.append((axis, j, gain, jnp.where(flags[2 * axis + 1] > 0, lower[j], 0.0)))
        for axis, j, gain, low in outs:
            place_rows(acc, rows, 2 * axis, gain, j)
            place_rows(acc, rows, 2 * axis + 1, low, j)
        return carry

    lax.fori_loop(0, faces // ROWS, step, 0)


def next_kernel(order, rows, flags, bounds, *refs):
    if order == 1:
        (v, wf, wb, diag, ux, lx, uy, ly, ch, cl, *outs, acc) = refs
        older = None
    else:
        (v, older, wf, wb, diag, ux, lx, uy, ly, ch, cl, *outs, acc) = refs
    new, new2, *sends = outs
    acc[...] = jnp.zeros_like(acc)
    arrive(rows, flags, (ux, lx, uy, ly), ch, cl, acc)
    lower = jnp.full((16, 128), bounds[0], F32)
    upper = jnp.full((16, 128), bounds[1], F32)
    half = (upper - lower) / 2.0
    centre = (upper + lower) / 2.0
    scale = (1.0 if order == 1 else 2.0) / half
    group = 8

    def step(s, carry):
        part = pl.ds(s * group, group)
        x = v[part]
        ax = wf[part] + wb[part] + acc[part] + diag[part][:, None, :] * x
        y = (ax - centre * x) * scale
        if older is not None:
            y = y - older[part]
        new[part] = y
        new2[part] = stacked(y)
        return carry

    lax.fori_loop(0, v.shape[0] // group, step, 0)
    if order < 3:
        leave(new, new2, rows, ch, cl, sends, True)
        return
    mx, my, gram = sends
    leave(new, new2, rows, ch, cl, (mx, None, my, None), False)
    total = jnp.zeros((32, 32), F32)
    for s in range(0, v.shape[0], 16):
        x2 = cat([new2[s + r] for r in range(16)], axis=1)
        total = total + dot_nt(x2, x2)
    spread(gram, quarter(total))


def quarter(total):
    half = total.shape[0] // 2
    return (total[:half, :half] + total[half:, half:]) + (total[:half, half:] + total[half:, :half])


def spread(out, value):
    def step(d, carry):
        out[d] = value
        return carry

    lax.fori_loop(0, out.shape[0], step, 0)


def project_kernel(cols, v, v2, diag, th, out, y2):
    def step(c, carry):
        outs = []
        for r in range(ROWS):
            i = c * ROWS + r
            g2 = cat([v2[cols[i, k]] for k in range(4)], axis=1)
            outs.append((i, fold(dot_nt(g2, cat([th[i, k] for k in range(4)], axis=1)))))
        for i, forward in outs:
            y2[i] = stacked((forward + 0.5 * (diag[pl.ds(i, 1)] * v[i])) * SHRINK)
        return carry

    lax.fori_loop(0, v.shape[0] // ROWS, step, 0)
    total = jnp.zeros((32, 32), F32)
    for s in range(0, v.shape[0], 16):
        a2 = cat([v2[s + r] for r in range(16)], axis=1)
        b2 = cat([y2[s + r] for r in range(16)], axis=1)
        total = total + dot_nt(a2, b2)
    out[...] = quarter(total)


def project_faces_kernel(rows, flags, v2, ux, uy, ch, part, out):
    total = jnp.zeros((32, 32), F32)
    for axis, upper in ((0, ux), (1, uy)):
        for s in range(0, rows.shape[1], ROWS):
            lefts, rights = [], []
            for r in range(ROWS):
                j = s + r
                u2 = stacked(jnp.where(flags[2 * axis] > 0, upper[j], 0.0))
                rights.append(stacked(fold(dot_nt(u2, ch[axis, j])) * SHRINK))
                lefts.append(v2[rows[2 * axis, j]])
            total = total + dot_nt(cat(lefts, axis=1), cat(rights, axis=1))
    spread(out, part[...] + quarter(total))


def summed(ref):
    total = ref[0]
    for d in range(1, ref.shape[0]):
        total = total + ref[d]
    return total


def basis_kernel(nodes, gram, v2, basis, inverse):
    g = summed(gram) / nodes
    n = g.shape[0]
    row = lax.broadcasted_iota(jnp.int32, (n, n), 0)
    col = lax.broadcasted_iota(jnp.int32, (n, n), 1)
    e = jnp.where(row == col, 1.0, 0.0).astype(F32)
    pivots = jnp.zeros((n, n), F32)
    for k in range(n):
        pivot = jnp.broadcast_to(g[k : k + 1, k : k + 1], (n, n))
        pivots = jnp.where(row == k, pivot, pivots)
        factor = jnp.broadcast_to(g[:, k : k + 1], (n, n)) / pivot
        factor = jnp.where(row > k, factor, 0.0)
        g = g - factor * g[k : k + 1, :]
        e = e - factor * e[k : k + 1, :]
    inv = e / jnp.sqrt(pivots)
    inverse[...] = inv
    high, low = split(inv)
    left = cat([cat([high, high], axis=1), cat([low, jnp.zeros_like(low)], axis=1)], axis=0)

    for s in range(0, v2.shape[0], 8):
        out = fold(dot_nn(left, cat([v2[s + r] for r in range(8)], axis=1)))
        for r in range(8):
            basis[s + r] = out[:, r * 128 : (r + 1) * 128]


def projected_kernel(nodes, sums, inverse, out):
    half = summed(sums)
    inv = inverse[...]
    high = lax.Precision.HIGHEST
    raw = lax.dot_general(inv, half, (((1,), (0,)), ((), ())), precision=high, preferred_element_type=F32)
    raw = lax.dot_general(raw, inv, (((1,), (1,)), ((), ())), precision=high, preferred_element_type=F32)
    out[...] = (raw + raw.T) * (1.0 / (SHRINK * nodes))


def in_vmem(shape, dtype):
    return pltpu.VMEM(shape, dtype)


def call(kernel, name, specs, outs, scratch=(), limit=32, flops=0, nbytes=0):
    return pl.pallas_call(
        kernel,
        name=name,
        in_specs=specs,
        out_specs=[VM] * len(outs),
        out_shape=outs,
        scratch_shapes=list(scratch),
        cost_estimate=pl.CostEstimate(flops=flops, bytes_accessed=nbytes, transcendentals=0),
        compiler_params=pltpu.CompilerParams(vmem_limit_bytes=limit * MIB),
    )


def ring(x, axis, by):
    peers = lax.axis_size(axis)
    return lax.ppermute(x, axis, [(i, (i + by) % peers) for i in range(peers)])


def shards(start_block, tiles, tile_cols, node_diag, face_tiles, face_rows, filter_bounds):
    block = start_block[0, 0]
    stored = tiles[0, 0]
    cols = tile_cols[0, 0]
    diag = node_diag[0, 0]
    coupling = face_tiles[0, 0]
    rows = face_rows[0, 0]
    count, width, tile = block.shape
    faces = rows.shape[1]
    nx, ny = lax.axis_size("gx"), lax.axis_size("gy")
    peers = nx * ny
    nodes = float(count * tile * peers)
    ix, iy = lax.axis_index("gx"), lax.axis_index("gy")
    flags = jnp.stack([ix < nx - 1, ix > 0, iy < ny - 1, iy > 0]).astype(jnp.int32)

    vec = in_vmem((count, width, tile), F32)
    vec2 = in_vmem((count, 2 * width, tile), BF16)
    face = jax.ShapeDtypeStruct((faces, width, tile), F32)
    tile2 = in_vmem(stored.shape, BF16)
    face2 = in_vmem(coupling.shape, BF16)
    small = jax.ShapeDtypeStruct((peers, width, width), F32)
    local_flops = 16 * stored.size * width

    ch, cl, x2, mx, ox, my, oy = call(
        begin_kernel, "begin", [SM, VM, VM], [face2, face2, vec2, face, face, face, face]
    )(rows, block, coupling)

    def exchange(mx, ox, my, oy):
        return (ring(mx, "gx", -1), ring(ox, "gx", 1), ring(my, "gy", -1), ring(oy, "gy", 1))

    received = exchange(mx, ox, my, oy)
    wf, wb, th, tl = call(
        first_kernel, "local_first", [SM, VM, ANY], [vec, vec, tile2, tile2],
        [pltpu.VMEM(stored.shape, F32), pltpu.SemaphoreType.DMA((count // ROWS,))],
        limit=40, flops=local_flops, nbytes=4 * stored.size,
    )(cols, x2, stored)

    x, older = block, None
    for order in (1, 2, 3):
        carried = (x,) if older is None else (x, older)
        last = order == 3
        outs = [vec, vec2] + ([face, face, small] if last else [face] * 4)
        new, new2, *sends = call(
            functools.partial(next_kernel, order), "finish%d" % order,
            [SM, SM, SM] + [VM] * (9 + len(carried)), outs,
            [pltpu.VMEM((count, width, tile), F32)],
        )(rows, flags, filter_bounds, *carried, wf, wb, diag, *received, ch, cl)
        x, x2, older = new, new2, x
        if not last:
            received = exchange(*sends)
            wf, wb = call(
                local_kernel, "local%d" % (order + 1), [SM] + [VM] * 3, [vec, vec],
                flops=local_flops, nbytes=4 * stored.size,
            )(cols, x2, th, tl)
    mx, my, gram = sends
    gram = lax.all_to_all(gram, ("gx", "gy"), 0, 0)
    ux, uy = ring(mx, "gx", -1), ring(my, "gy", -1)
    (part,) = call(
        project_kernel, "project", [SM] + [VM] * 4, [in_vmem((width, width), F32)],
        [pltpu.VMEM((count, 2 * width, tile), BF16)],
        flops=local_flops // 4, nbytes=2 * stored.size,
    )(cols, x, x2, diag, th)
    (sums,) = call(project_faces_kernel, "project_faces", [SM, SM] + [VM] * 5, [small])(
        rows, flags, x2, ux, uy, ch, part
    )
    sums = lax.all_to_all(sums, ("gx", "gy"), 0, 0)
    basis, inverse = call(
        functools.partial(basis_kernel, nodes), "basis", [VM, VM],
        [jax.ShapeDtypeStruct((count, width, tile), F32), in_vmem((width, width), F32)],
        flops=1 << 24, nbytes=MIB,
    )(gram, x2)
    (projected,) = call(
        functools.partial(projected_kernel, nodes), "projected", [VM, VM],
        [jax.ShapeDtypeStruct((width, width), F32)],
    )(sums, inverse)
    return (basis[None, None], projected)


def solution(mesh):
    in_specs = (
        P("gx", "gy", None, None, None),
        P("gx", "gy", None, None, None, None),
        P("gx", "gy", None, None),
        P("gx", "gy", None, None),
        P("gx", "gy", None, None, None, None),
        P("gx", "gy", None, None),
        P(),
    )
    out_specs = (P("gx", "gy", None, None, None), P())
    return jax.shard_map(shards, mesh=mesh, in_specs=in_specs, out_specs=out_specs, check_vma=False)
```

time: 373 us -> 123 us (0.33); the launches traced: 368 us -> 123 us
  matrix products: 175 us -> 0 us
  blocking collectives: 89.2 us -> 0 us
  Pallas kernels: 0 us -> 56.2 us
  local copies, waits for them, and re-layouts: 49.2 us -> 28.5 us
  starting transfers between devices: 39.4 us -> 32.9 us
  other arithmetic: 7.36 us -> 1.51 us
    dot_general x47 -> x0, matrix products: 175 us -> none  [the longest x4 71.1 us: local_apply(): forward = jnp.einsum('rkcb,rkab->rca', gathered, tiles, precision=HIGH)]
    psum x2 -> x0, blocking collectives: 89.2 us -> none  [the longest x1 45 us: shards(): gram = lax.psum(partial_products(filtered, filtered), ('gx', 'gy')) / nodes]
    pallas_call x0 -> x11, Pallas kernels: none -> 56.2 us  [the longest x2 17.4 us: shards(): call(local_kernel, 'local%d' % (order + 1), [SM] + [VM] * 3, [vec, vec],...]
    gather x20 -> x0, local copies, waits for them, and re-layouts: 45.1 us -> none  [the longest x4 12.5 us: local_apply(): gathered = block[cols]]
    unnamed x89 -> x45, local copies, waits for them, and re-layouts: 1.85 us -> 27.9 us
    ppermute x16 -> x14, starting transfers between devices: 39.4 us -> 24.5 us  [ring(): return lax.ppermute(x, axis, [(i, (i + by) % peers) for i in range(peers)])]
    all_to_all x0 -> x2, starting transfers between devices: none -> 8.4 us  [the longest x1 5.84 us: shards(): sums = lax.all_to_all(sums, ('gx', 'gy'), 0, 0)]
    another operation x5 -> x0, other arithmetic: 3.99 us -> none  [the longest x3 2.16 us: shards(): factor = jnp.linalg.cholesky(gram)]
  transfers between devices with their start and end apart: 16 -> 16, of which waited for: 3 -> 1; matrix products, arithmetic and copies ran while one was open for 19% -> 4% of each run, Pallas kernels for 0% -> 31%
where the time goes in v1:
time: 123 us
  Pallas kernels  56.2 us (46%)
  starting transfers between devices  32.9 us (27%)
  local copies, waits for them, and re-layouts  28.5 us (23%)
  waiting for transfers between devices  2.92 us (2%)
  other arithmetic  1.51 us (1%)
    unnamed x45, local copies, waits for them, and re-layouts  27.9 us
    ppermute x14, starting transfers between devices, ring(): return lax.ppermute(x, axis, [(i, (i + by) % peers) for i in range(peers)])  24.5 us
    pallas_call x2, Pallas kernels, shards(): call(local_kernel, 'local%d' % (order + 1), [SM] + [VM] * 3, [vec, vec],...  17.4 us
    pallas_call x3, Pallas kernels, shards(): call(functools.partial(next_kernel, order), 'finish%d' % order, [SM, SM,...  13.4 us
    pallas_call x1, Pallas kernels, shards(): call(first_kernel, 'local_first', [SM, VM, ANY], [vec, vec, tile2, tile2]...  10.7 us
    all_to_all x1, starting transfers between devices, shards(): sums = lax.all_to_all(sums, ('gx', 'gy'), 0, 0)  5.84 us
    pallas_call x1, Pallas kernels, shards(): call(project_kernel, 'project', [SM] + [VM] * 4, [in_vmem((width, width),...  5.22 us
    pallas_call x1, Pallas kernels, shards(): call(begin_kernel, 'begin', [SM, VM, VM], [face2, face2, vec2, face, face...  3.15 us
  transfers between devices with their start and end apart: 16, of which 1 were waited for; matrix products, arithmetic and copies ran while one was open for 4% of the time, Pallas kernels for 31%

profile of v1, /device:TPU:0, one launch (start us, length us, event | category | flops | bytes accessed | tf_op | source)
XLA Modules:
  0.0 122.9 jit_solution(12653674915893609067)
XLA Ops:
  4.2 3.2 %begin.1 = (bf16[2,24,128,128]{3,2,1,0:T(8,128)(2,1)S(1)}, bf16[2,24,128,128]{3,2,1,0:T(8,128)(2,1)S(1)}, bf16[64,32,128]{2,1,0:T(8,128)(2,1)S(1)}, f32[24,16,12...) custom-call(s32[4,24]{1,0:T(4,128)S(1)} %bitcast.23, ...), custom_call_target="tpu_custom_call" | custom-call | tf_op jit(solution)/shard_map/begin/pallas_call | solution.py:342
  8.2 5.0 %collective-permute-start = (f32[24,16,128]{2,1,0:T(8,128)}, f32[24,16,128]{2,1,0:T(8,128)S(1)}, u32[]{:S(2)}, u32[]{:S(2)}) collective-permute-start(f32[24,16,128]{2,1,0:T(8,128)} %get-tuple-element.39), channel_id=1, source_target_pairs={{0,24},{8,0},{16,8},{24,16},{1,25},{9,1},{17,9},{25,17},{2,26},{10... | collective-permute-start | bytes 589832 | tf_op jit(solution)/shard_map/ppermute | solution.py:316
  16.3 10.7 %local_first.1 = (f32[64,16,128]{2,1,0:T(8,128)S(1)}, f32[64,16,128]{2,1,0:T(8,128)S(1)}, bf16[64,4,128,128]{3,2,1,0:T(8,128)(2,1)S(1)}, bf16[64,4,128,128]{3,2,1,0:T(8,128)(2,1)S(1)}) custom-call(s32[64,4]{1,0:T(8,128)} %bitcast.15, bf16[64,32,128]{2,1,0:T(8,128)(2,1)} %copy-done.14, f32[64,4,128,128]{3,2,1,0:T(8,128)} %bitcast.28), custom_call_target="tpu_custom_call" | custom-call | flops 1073741824 | bytes 16777216 | tf_op jit(solution)/shard_map/local_first/pallas_call | solution.py:350
  27.0 3.3 %copy-done = bf16[64,4,128,128]{3,2,1,0:T(8,128)(2,1)} copy-done((bf16[64,4,128,128]{3,2,1,0:T(8,128)(2,1)}, bf16[64,4,128,128]{3,2,1,0:T(8,128)(2,1)S(1)}, u32[]{:S(2)}) %copy-start) | copy-done | bytes 8388632
  30.2 3.2 %copy-done.4 = bf16[64,4,128,128]{3,2,1,0:T(8,128)(2,1)} copy-done((bf16[64,4,128,128]{3,2,1,0:T(8,128)(2,1)}, bf16[64,4,128,128]{3,2,1,0:T(8,128)(2,1)S(1)}, u32[]{:S(2)}) %copy-start.4) | copy-done | bytes 8388632
  33.6 4.8 %finish1.1 = (f32[64,16,128]{2,1,0:T(8,128)S(1)}, bf16[64,32,128]{2,1,0:T(8,128)(2,1)S(1)}, f32[24,16,128]{2,1,0:T(8,128)S(1)}, f32[24,16,128]{2,1,0:T(8,128)S(1...) custom-call(s32[4,24]{1,0:T(4,128)S(1)} %bitcast.24, s32[4]{0:T(128)S(1)} %add_convert_fusion.flags, ...), custom_call_target="tpu_custom_call" | custom-call | tf_op jit(solution)/shard_map/finish1/pallas_call | solution.py:361
  38.4 3.6 %collective-permute-start.4 = (f32[24,16,128]{2,1,0:T(8,128)S(1)}, f32[24,16,128]{2,1,0:T(8,128)S(1)}, u32[]{:S(2)}, u32[]{:S(2)}) collective-permute-start(f32[24,16,128]{2,1,0:T(8,128)S(1)} %get-tuple-element.51), channel_id=1, source_target_pairs={{0,24},{8,0},{16,8},{24,16},{1,25},{9,1},{17,9},{25,17},{2,26},{10... | collective-permute-start | bytes 589832 | tf_op jit(solution)/shard_map/ppermute | solution.py:316
  42.0 2.4 %collective-permute-start.6 = (f32[24,16,128]{2,1,0:T(8,128)S(1)}, f32[24,16,128]{2,1,0:T(8,128)S(1)}, u32[]{:S(2)}, u32[]{:S(2)}) collective-permute-start(f32[24,16,128]{2,1,0:T(8,128)S(1)} %get-tuple-element.53), channel_id=1, source_target_pairs={{0,7},{1,0},{2,1},{3,2},{4,3},{5,4},{6,5},{7,6},{8,15},{9,8},{10,9... | collective-permute-start | bytes 589832 | tf_op jit(solution)/shard_map/ppermute | solution.py:316
  44.4 3.4 %copy-done.1 = bf16[64,4,128,128]{3,2,1,0:T(8,128)(2,1)S(1)} copy-done((bf16[64,4,128,128]{3,2,1,0:T(8,128)(2,1)S(1)}, bf16[64,4,128,128]{3,2,1,0:T(8,128)(2,1)}, u32[]{:S(2)}) %copy-start.1) | copy-done | bytes 8388632
  47.7 3.4 %copy-done.5 = bf16[64,4,128,128]{3,2,1,0:T(8,128)(2,1)S(1)} copy-done((bf16[64,4,128,128]{3,2,1,0:T(8,128)(2,1)S(1)}, bf16[64,4,128,128]{3,2,1,0:T(8,128)(2,1)}, u32[]{:S(2)}) %copy-start.5) | copy-done | bytes 8388632
  51.1 8.7 %local2.1 = (f32[64,16,128]{2,1,0:T(8,128)S(1)}, f32[64,16,128]{2,1,0:T(8,128)S(1)}) custom-call(s32[64,4]{1,0:T(8,128)S(1)} %bitcast.16, bf16[64,32,128]{2,1,0:T(8,128)(2,1)S(1)} %get-tuple-element.46.v2, bf16[64,4,128,128]{3,2,1,0:T(8,128)(2,1)S(1)} %copy-done.1, bf16[64,4,128,128]{3,2,1,0:T(8,128)(2,1)S(1)} %copy-done.5), custom_call_target="tpu_custom_call" | custom-call | flops 1073741824 | bytes 16777216 | tf_op jit(solution)/shard_map/local2/pallas_call | solution.py:369
  59.8 4.2 %finish2.1 = (f32[64,16,128]{2,1,0:T(8,128)S(1)}, bf16[64,32,128]{2,1,0:T(8,128)(2,1)S(1)}, f32[24,16,128]{2,1,0:T(8,128)S(1)}, f32[24,16,128]{2,1,0:T(8,128)S(1...) custom-call(s32[4,24]{1,0:T(4,128)S(1)} %bitcast.25, s32[4]{0:T(128)S(1)} %add_convert_fusion.flags, ...), custom_call_target="tpu_custom_call" | custom-call | tf_op jit(solution)/shard_map/finish2/pallas_call | solution.py:361
  64.1 2.7 %collective-permute-start.10 = (f32[24,16,128]{2,1,0:T(8,128)S(1)}, f32[24,16,128]{2,1,0:T(8,128)S(1)}, u32[]{:S(2)}, u32[]{:S(2)}) collective-permute-start(f32[24,16,128]{2,1,0:T(8,128)S(1)} %get-tuple-element.61), channel_id=1, source_target_pairs={{0,7},{1,0},{2,1},{3,2},{4,3},{5,4},{6,5},{7,6},{8,15},{9,8},{10,9... | collective-permute-start | bytes 589832 | tf_op jit(solution)/shard_map/ppermute | solution.py:316
  66.8 3.5 %collective-permute-start.8 = (f32[24,16,128]{2,1,0:T(8,128)S(1)}, f32[24,16,128]{2,1,0:T(8,128)S(1)}, u32[]{:S(2)}, u32[]{:S(2)}) collective-permute-start(f32[24,16,128]{2,1,0:T(8,128)S(1)} %get-tuple-element.59), channel_id=1, source_target_pairs={{0,24},{8,0},{16,8},{24,16},{1,25},{9,1},{17,9},{25,17},{2,26},{10... | collective-permute-start | bytes 589832 | tf_op jit(solution)/shard_map/ppermute | solution.py:316
  70.3 8.7 %local3.1 = (f32[64,16,128]{2,1,0:T(8,128)S(1)}, f32[64,16,128]{2,1,0:T(8,128)S(1)}) custom-call(s32[64,4]{1,0:T(8,128)S(1)} %bitcast.17, bf16[64,32,128]{2,1,0:T(8,128)(2,1)S(1)} %get-tuple-element.56.v2, bf16[64,4,128,128]{3,2,1,0:T(8,128)(2,1)S(1)} %copy-done.2, bf16[64,4,128,128]{3,2,1,0:T(8,128)(2,1)S(1)} %copy-done.5), custom_call_target="tpu_custom_call" | custom-call | flops 1073741824 | bytes 16777216 | tf_op jit(solution)/shard_map/local3/pallas_call | solution.py:369
  79.0 4.4 %finish3.1 = (f32[64,16,128]{2,1,0:T(8,128)S(1)}, bf16[64,32,128]{2,1,0:T(8,128)(2,1)S(1)}, f32[24,16,128]{2,1,0:T(8,128)}, f32[24,16,128]{2,1,0:T(8,128)}, f32[32,16,16]{2,1,0:T(8,128)S(1)}) custom-call(s32[4,24]{1,0:T(4,128)S(1)} %bitcast.26, s32[4]{0:T(128)S(1)} %add_convert_fusion.flags, f32[2]{0:T(128)S(1)} %copy-done.19, ...), custom_call_target="tpu_custom_call" | custom-call | tf_op jit(solution)/shard_map/finish3/pallas_call | solution.py:361
  85.1 3.8 %collective-permute-start.12 = (f32[24,16,128]{2,1,0:T(8,128)}, f32[24,16,128]{2,1,0:T(8,128)S(1)}, u32[]{:S(2)}, u32[]{:S(2)}) collective-permute-start(f32[24,16,128]{2,1,0:T(8,128)} %get-tuple-element.66), channel_id=1, source_target_pairs={{0,24},{8,0},{16,8},{24,16},{1,25},{9,1},{17,9},{25,17},{2,26},{10... | collective-permute-start | bytes 589832 | tf_op jit(solution)/shard_map/ppermute | solution.py:316
  91.5 2.6 %all-to-all-start = ((f32[32,1,256]{2,1,0:T(1,128)}), f32[32,1,256]{2,1,0:T(1,128)S(1)}, u32[]{:S(2)}, u32[]{:S(2)}) async-start(f32[32,1,256]{2,1,0:T(1,128)} %reshape.4), calls=%async_computation | async-start | bytes 65536 | tf_op jit(solution)/shard_map/all_to_all | solution.py:374
  94.1 3.4 %copy-done.3 = bf16[64,4,128,128]{3,2,1,0:T(8,128)(2,1)S(1)} copy-done((bf16[64,4,128,128]{3,2,1,0:T(8,128)(2,1)S(1)}, bf16[64,4,128,128]{3,2,1,0:T(8,128)(2,1)}, u32[]{:S(2)}) %copy-start.3) | copy-done | bytes 8388632
  99.5 5.2 %project.1.part = f32[16,16]{1,0:T(8,128)S(1)} custom-call(s32[64,4]{1,0:T(8,128)S(1)} %bitcast.18, f32[64,16,128]{2,1,0:T(8,128)S(1)} %copy-done.16, bf16[64,32,128]{2,1,0:T(8,128)(2,1)S(1)} %copy-done.9, f32[64,128]{1,0:T(8,128)S(1)} %bitcast.22, bf16[64,4,128,128]{3,2,1,0:T(8,128)(2,1)S(1)} %copy-done.3), custom_call_target="tpu_custom_call" | custom-call | flops 268435456 | bytes 8388608 | tf_op jit(solution)/shard_map/project/pallas_call | solution.py:376
  104.8 2.4 %project_faces.1 = f32[32,16,16]{2,1,0:T(8,128)S(1)} custom-call(s32[4,24]{1,0:T(4,128)S(1)} %bitcast.27, s32[4]{0:T(128)S(1)} %add_convert_fusion.flags, bf16[64,32,128]{2,1,0:T(8,128)(2,1)S(1)} %copy-done.9, f32[24,16,128]{2,1,0:T(8,128)S(1)} %collective-permute-done.12.ux, f32[24,16,128]{2,1,0:T(8,128)S(1)} %collective-permute-done.13.uy, ...), custom_call_target="tpu_custom_call" | custom-call | tf_op jit(solution)/shard_map/project_faces/pallas_call | solution.py:381
  108.0 5.8 %all-to-all-start.1 = ((f32[32,1,256]{2,1,0:T(1,128)}), f32[32,1,256]{2,1,0:T(1,128)S(1)}, u32[]{:S(2)}, u32[]{:S(2)}) async-start(f32[32,1,256]{2,1,0:T(1,128)} %reshape.6), calls=%async_computation.1 | async-start | bytes 65536 | tf_op jit(solution)/shard_map/all_to_all | solution.py:384
  115.2 3.0 %basis.1 = (f32[64,16,128]{2,1,0:T(8,128)}, f32[16,16]{1,0:T(8,128)S(1)}) custom-call(f32[32,16,16]{2,1,0:T(8,128)S(1)} %reshape.5.gram, bf16[64,32,128]{2,1,0:T(8,128)(2,1)S(1)} %copy-done.10), custom_call_target="tpu_custom_call" | custom-call | flops 16777216 | bytes 1048576 | tf_op jit(solution)/shard_map/basis/pallas_call | solution.py:385
  118.2 2.9 %all-to-all-done.1 = f32[32,1,256]{2,1,0:T(1,128)S(1)} async-done(((f32[32,1,256]{2,1,0:T(1,128)}), f32[32,1,256]{2,1,0:T(1,128)S(1)}, u32[]{:S(2)}, u32[]{:S(2)}) %all-to-all-start.1) | async-done | bytes 32800 | tf_op jit(solution)/shard_map/all_to_all | solution.py:384
  (68 shorter events, 17.8 us)
Async XLA Ops:
  8.2 25.4 %collective-permute-start = (f32[24,16,128]{2,1,0:T(8,128)}, f32[24,16,128]{2,1,0:T(8,128)S(1)}, u32[]{:S(2)}, u32[]{:S(2)}) collective-permute-start(f32[24,16,128]{2,1,0:T(8,128)} %get-tuple-element.39), channel_id=1, source_target_pairs={{0,24},{8,0},{16,8},{24,16},{1,25},{9,1},{17,9},{25,17},{2,26},{10... | collective-permute-start | bytes 589832 | tf_op jit(solution)/shard_map/ppermute | solution.py:316
  13.2 20.3 %collective-permute-start.1 = (f32[24,16,128]{2,1,0:T(8,128)}, f32[24,16,128]{2,1,0:T(8,128)}, u32[]{:S(2)}, u32[]{:S(2)}) collective-permute-start(f32[24,16,128]{2,1,0:T(8,128)} %get-tuple-element.40), channel_id=1, source_target_pairs={{0,8},{8,16},{16,24},{24,0},{1,9},{9,17},{17,25},{25,1},{2,10},{10... | collective-permute-start | bytes 589832 | tf_op jit(solution)/shard_map/ppermute | solution.py:316
  13.2 20.3 %collective-permute-start.2 = (f32[24,16,128]{2,1,0:T(8,128)}, f32[24,16,128]{2,1,0:T(8,128)}, u32[]{:S(2)}, u32[]{:S(2)}) collective-permute-start(f32[24,16,128]{2,1,0:T(8,128)} %get-tuple-element.41), channel_id=1, source_target_pairs={{0,7},{1,0},{2,1},{3,2},{4,3},{5,4},{6,5},{7,6},{8,15},{9,8},{10,9... | collective-permute-start | bytes 589832 | tf_op jit(solution)/shard_map/ppermute | solution.py:316
  14.9 18.7 %collective-permute-start.3 = (f32[24,16,128]{2,1,0:T(8,128)}, f32[24,16,128]{2,1,0:T(8,128)}, u32[]{:S(2)}, u32[]{:S(2)}) collective-permute-start(f32[24,16,128]{2,1,0:T(8,128)} %get-tuple-element.42), channel_id=1, source_target_pairs={{0,1},{1,2},{2,3},{3,4},{4,5},{5,6},{6,7},{7,0},{8,9},{9,10},{10,1... | collective-permute-start | bytes 589832 | tf_op jit(solution)/shard_map/ppermute | solution.py:316
  16.2 17.4 %copy-start.7 = (f32[1,1,64,16,128]{4,3,2,1,0:T(8,128)S(1)}, f32[1,1,64,16,128]{4,3,2,1,0:T(8,128)}, u32[]{:S(2)}) copy-start(f32[1,1,64,16,128]{4,3,2,1,0:T(8,128)} %param.7) | copy-start | bytes 1572868
  16.2 17.4 %copy-start.13 = (f32[1,1,64,128]{3,2,1,0:T(8,128)S(1)}, f32[1,1,64,128]{3,2,1,0:T(8,128)}, u32[]{:S(2)}) copy-start(f32[1,1,64,128]{3,2,1,0:T(8,128)} %param.10) | copy-start | bytes 98308
  16.2 17.4 %copy-start.18 = (s32[1,1,4,24]{3,2,1,0:T(4,128)S(1)}, s32[1,1,4,24]{3,2,1,0:T(4,128)}, u32[]{:S(2)}) copy-start(s32[1,1,4,24]{3,2,1,0:T(4,128)} %param.12) | copy-start | bytes 1156
  16.2 17.4 %copy-start.19 = (f32[2]{0:T(128)S(1)}, f32[2]{0:T(128)}, u32[]{:S(2)}) copy-start(f32[2]{0:T(128)} %bounds.5) | copy-start | bytes 28
  16.3 28.1 %copy-start.12 = (s32[1,1,64,4]{3,2,1,0:T(8,128)S(1)}, s32[1,1,64,4]{3,2,1,0:T(8,128)}, u32[]{:S(2)}) copy-start(s32[1,1,64,4]{3,2,1,0:T(8,128)} %copy.9) | copy-start | bytes 3076
  38.4 21.4 %collective-permute-start.4 = (f32[24,16,128]{2,1,0:T(8,128)S(1)}, f32[24,16,128]{2,1,0:T(8,128)S(1)}, u32[]{:S(2)}, u32[]{:S(2)}) collective-permute-start(f32[24,16,128]{2,1,0:T(8,128)S(1)} %get-tuple-element.51), channel_id=1, source_target_pairs={{0,24},{8,0},{16,8},{24,16},{1,25},{9,1},{17,9},{25,17},{2,26},{10... | collective-permute-start | bytes 589832 | tf_op jit(solution)/shard_map/ppermute | solution.py:316
  42.0 17.8 %collective-permute-start.5 = (f32[24,16,128]{2,1,0:T(8,128)S(1)}, f32[24,16,128]{2,1,0:T(8,128)S(1)}, u32[]{:S(2)}, u32[]{:S(2)}) collective-permute-start(f32[24,16,128]{2,1,0:T(8,128)S(1)} %get-tuple-element.52), channel_id=1, source_target_pairs={{0,8},{8,16},{16,24},{24,0},{1,9},{9,17},{17,25},{25,1},{2,10},{10... | collective-permute-start | bytes 589832 | tf_op jit(solution)/shard_map/ppermute | solution.py:316
  42.0 17.8 %collective-permute-start.6 = (f32[24,16,128]{2,1,0:T(8,128)S(1)}, f32[24,16,128]{2,1,0:T(8,128)S(1)}, u32[]{:S(2)}, u32[]{:S(2)}) collective-permute-start(f32[24,16,128]{2,1,0:T(8,128)S(1)} %get-tuple-element.53), channel_id=1, source_target_pairs={{0,7},{1,0},{2,1},{3,2},{4,3},{5,4},{6,5},{7,6},{8,15},{9,8},{10,9... | collective-permute-start | bytes 589832 | tf_op jit(solution)/shard_map/ppermute | solution.py:316
  44.3 15.5 %collective-permute-start.7 = (f32[24,16,128]{2,1,0:T(8,128)S(1)}, f32[24,16,128]{2,1,0:T(8,128)S(1)}, u32[]{:S(2)}, u32[]{:S(2)}) collective-permute-start(f32[24,16,128]{2,1,0:T(8,128)S(1)} %get-tuple-element.54), channel_id=1, source_target_pairs={{0,1},{1,2},{2,3},{3,4},{4,5},{5,6},{6,7},{7,0},{8,9},{9,10},{10,1... | collective-permute-start | bytes 589832 | tf_op jit(solution)/shard_map/ppermute | solution.py:316
  44.4 3.4 %copy-start.1 = (bf16[64,4,128,128]{3,2,1,0:T(8,128)(2,1)S(1)}, bf16[64,4,128,128]{3,2,1,0:T(8,128)(2,1)}, u32[]{:S(2)}) copy-start(bf16[64,4,128,128]{3,2,1,0:T(8,128)(2,1)} %copy-done) | copy-start | bytes 25165828
  51.1 19.2 %copy-start.2 = (bf16[64,4,128,128]{3,2,1,0:T(8,128)(2,1)S(1)}, bf16[64,4,128,128]{3,2,1,0:T(8,128)(2,1)}, u32[]{:S(2)}) copy-start(bf16[64,4,128,128]{3,2,1,0:T(8,128)(2,1)} %copy-done) | copy-start | bytes 25165828
  64.1 14.9 %collective-permute-start.10 = (f32[24,16,128]{2,1,0:T(8,128)S(1)}, f32[24,16,128]{2,1,0:T(8,128)S(1)}, u32[]{:S(2)}, u32[]{:S(2)}) collective-permute-start(f32[24,16,128]{2,1,0:T(8,128)S(1)} %get-tuple-element.61), channel_id=1, source_target_pairs={{0,7},{1,0},{2,1},{3,2},{4,3},{5,4},{6,5},{7,6},{8,15},{9,8},{10,9... | collective-permute-start | bytes 589832 | tf_op jit(solution)/shard_map/ppermute | solution.py:316
  66.8 12.3 %collective-permute-start.11 = (f32[24,16,128]{2,1,0:T(8,128)S(1)}, f32[24,16,128]{2,1,0:T(8,128)S(1)}, u32[]{:S(2)}, u32[]{:S(2)}) collective-permute-start(f32[24,16,128]{2,1,0:T(8,128)S(1)} %get-tuple-element.62), channel_id=1, source_target_pairs={{0,1},{1,2},{2,3},{3,4},{4,5},{5,6},{6,7},{7,0},{8,9},{9,10},{10,1... | collective-permute-start | bytes 589832 | tf_op jit(solution)/shard_map/ppermute | solution.py:316
  66.8 12.3 %collective-permute-start.8 = (f32[24,16,128]{2,1,0:T(8,128)S(1)}, f32[24,16,128]{2,1,0:T(8,128)S(1)}, u32[]{:S(2)}, u32[]{:S(2)}) collective-permute-start(f32[24,16,128]{2,1,0:T(8,128)S(1)} %get-tuple-element.59), channel_id=1, source_target_pairs={{0,24},{8,0},{16,8},{24,16},{1,25},{9,1},{17,9},{25,17},{2,26},{10... | collective-permute-start | bytes 589832 | tf_op jit(solution)/shard_map/ppermute | solution.py:316
  70.3 8.7 %collective-permute-start.9 = (f32[24,16,128]{2,1,0:T(8,128)S(1)}, f32[24,16,128]{2,1,0:T(8,128)S(1)}, u32[]{:S(2)}, u32[]{:S(2)}) collective-permute-start(f32[24,16,128]{2,1,0:T(8,128)S(1)} %get-tuple-element.60), channel_id=1, source_target_pairs={{0,8},{8,16},{16,24},{24,0},{1,9},{9,17},{17,25},{25,1},{2,10},{10... | collective-permute-start | bytes 589832 | tf_op jit(solution)/shard_map/ppermute | solution.py:316
  85.1 19.6 %collective-permute-start.12 = (f32[24,16,128]{2,1,0:T(8,128)}, f32[24,16,128]{2,1,0:T(8,128)S(1)}, u32[]{:S(2)}, u32[]{:S(2)}) collective-permute-start(f32[24,16,128]{2,1,0:T(8,128)} %get-tuple-element.66), channel_id=1, source_target_pairs={{0,24},{8,0},{16,8},{24,16},{1,25},{9,1},{17,9},{25,17},{2,26},{10... | collective-permute-start | bytes 589832 | tf_op jit(solution)/shard_map/ppermute | solution.py:316
  88.9 15.8 %collective-permute-start.13 = (f32[24,16,128]{2,1,0:T(8,128)}, f32[24,16,128]{2,1,0:T(8,128)S(1)}, u32[]{:S(2)}, u32[]{:S(2)}) collective-permute-start(f32[24,16,128]{2,1,0:T(8,128)} %get-tuple-element.67), channel_id=1, source_target_pairs={{0,7},{1,0},{2,1},{3,2},{4,3},{5,4},{6,5},{7,6},{8,15},{9,8},{10,9... | collective-permute-start | bytes 589832 | tf_op jit(solution)/shard_map/ppermute | solution.py:316
  91.5 16.5 %all-to-all-start = ((f32[32,1,256]{2,1,0:T(1,128)}), f32[32,1,256]{2,1,0:T(1,128)S(1)}, u32[]{:S(2)}, u32[]{:S(2)}) async-start(f32[32,1,256]{2,1,0:T(1,128)} %reshape.4), calls=%async_computation | async-start | bytes 65536 | tf_op jit(solution)/shard_map/all_to_all | solution.py:374
  99.5 15.7 %copy-start.10 = (bf16[64,32,128]{2,1,0:T(8,128)(2,1)S(1)}, bf16[64,32,128]{2,1,0:T(8,128)(2,1)}, u32[]{:S(2)}) copy-start(bf16[64,32,128]{2,1,0:T(8,128)(2,1)} %copy-done.8) | copy-start | bytes 1572868
  108.0 13.1 %all-to-all-start.1 = ((f32[32,1,256]{2,1,0:T(1,128)}), f32[32,1,256]{2,1,0:T(1,128)S(1)}, u32[]{:S(2)}, u32[]{:S(2)}) async-start(f32[32,1,256]{2,1,0:T(1,128)} %reshape.6), calls=%async_computation.1 | async-start | bytes 65536 | tf_op jit(solution)/shard_map/all_to_all | solution.py:384
  (12 other events, 21.4 us)

commit v2 on v1

v2 whole, which is shorter than its diff:
```python
import functools

import jax
import jax.numpy as jnp
from jax import lax
from jax.experimental import pallas as pl
from jax.experimental.pallas import tpu as pltpu
from jax.sharding import PartitionSpec as P

F32 = jnp.float32
BF16 = jnp.bfloat16
MIB = 1 << 20
VM = pl.BlockSpec(memory_space=pltpu.VMEM)
SM = pl.BlockSpec(memory_space=pltpu.SMEM)
HBM = pl.BlockSpec(memory_space=pltpu.HBM)
cat = jnp.concatenate

ROWS = 8
EARLY = 24
SHRINK = 1.0 / 64.0


def split(x):
    high = x.astype(BF16)
    low = (x - high.astype(F32)).astype(BF16)
    return high, low


def stacked(x):
    return cat(split(x), axis=-2)


def dot_nn(x, t):
    return lax.dot_general(x, t, (((1,), (0,)), ((), ())), preferred_element_type=F32)


def dot_nt(x, t):
    return lax.dot_general(x, t, (((1,), (1,)), ((), ())), preferred_element_type=F32)


def fold(both, low=None):
    half = both.shape[0] // 2
    out = both[:half] + both[half:]
    return out if low is None else out + low


def two_piece(dot, x2, high, low):
    half = x2.shape[0] // 2
    return fold(dot(x2, high), dot(x2[:half], low))


def place_rows(w_ref, rows, which, data, j):
    at = rows[which, j]
    w_ref[at] = w_ref[at] + data


def leave(v, v2, rows, flags, ch, cl, sends):
    def step(s, carry):
        outs = []
        for axis in range(2):
            for r in range(ROWS):
                j = s * ROWS + r
                x2 = v2[rows[2 * axis, j]]
                outs.append((axis, j, two_piece(dot_nn, x2, ch[axis, j], cl[axis, j])))
        for axis, j, out in outs:
            send(rows, flags, v, axis, j, out, sends)
        return carry

    lax.fori_loop(0, rows.shape[1] // ROWS, step, 0)


def begin_kernel(rows_in, cols_in, bounds_in, flags_in, block, tiles, stored, *refs):
    (rows, cols, bounds, flags, ch, cl, v, v2, a, b, c, d, early, stage, sems) = refs
    faces = rows.shape[1]
    chunks = faces // ROWS

    def fetch(s, axis):
        part = pl.ds(s * ROWS, ROWS)
        at = sems.at[2 * s + axis]
        return pltpu.make_async_copy(tiles.at[axis, part], stage.at[axis, part], at)

    def bring(source, target, k):
        copy = pltpu.make_async_copy(source, target, sems.at[2 * chunks + k])
        copy.start()
        return copy

    small = [bring(x, y, k) for k, (x, y) in enumerate(((rows_in, rows), (flags_in, flags), (block, v)))]
    for s in range(chunks):
        for axis in range(2):
            fetch(s, axis).start()
    late = [bring(cols_in, cols, 3), bring(bounds_in, bounds, 4)]
    late.append(bring(stored.at[pl.ds(0, EARLY)], early, 5))
    for copy in small:
        copy.wait()
    v2[...] = stacked(v[...])

    def step(s, carry):
        outs = []
        for axis in range(2):
            fetch(s, axis).wait()
            for r in range(ROWS):
                j = s * ROWS + r
                high, low = split(stage[axis, j])
                ch[axis, j] = high
                cl[axis, j] = low
                outs.append((axis, j, two_piece(dot_nn, v2[rows[2 * axis, j]], high, low)))
        for axis, j, out in outs:
            send(rows, flags, v, axis, j, out, (a, b, c, d))
        return carry

    lax.fori_loop(0, chunks, step, 0)
    for copy in late:
        copy.wait()


def send(rows, flags, v, axis, j, product, sends):
    minus = v[rows[2 * axis + 1, j]]
    odd = flags[4 + axis] > 0
    sends[2 * axis][j] = jnp.where(odd, minus, product)
    sends[2 * axis + 1][j] = jnp.where(odd, product, minus)


def local_rows(rows, cols, v2, highs, lows, wf, wb):
    outs = []
    for i, high, low in zip(rows, highs, lows):
        x2 = v2[i]
        g2 = cat([v2[cols[k, i]] for k in range(4)], axis=1)
        high = cat(high, axis=1)
        low = cat(low, axis=1)
        outs.append((two_piece(dot_nt, g2, high, low), two_piece(dot_nn, x2, high, low)))
    for i, (forward, backward) in zip(rows, outs):
        wf[i] = forward
        for k in range(4):
            at = cols[k, i]
            wb[at] = wb[at] + backward[:, k * 128 : (k + 1) * 128]


def first_kernel(cols, v2, early, tiles, wf, wb, th, tl, stage, sems):
    copies = stage.shape[0] // ROWS

    def fetch(c):
        part = pl.ds(c * ROWS, ROWS)
        return pltpu.make_async_copy(
            tiles.at[pl.ds(EARLY + c * ROWS, ROWS)], stage.at[part], sems.at[c]
        )

    for c in range(copies):
        fetch(c).start()
    wb[...] = jnp.zeros_like(wb)

    def work(source, start, c):
        rows, highs, lows = [], [], []
        for r in range(ROWS):
            i = start + c * ROWS + r
            pieces = [split(source[c * ROWS + r, k]) for k in range(4)]
            for k in range(4):
                th[i, k] = pieces[k][0]
                tl[i, k] = pieces[k][1]
            rows.append(i)
            highs.append([p[0] for p in pieces])
            lows.append([p[1] for p in pieces])
        local_rows(rows, cols, v2, highs, lows, wf, wb)

    def step_early(c, carry):
        work(early, 0, c)
        return carry

    def step(c, carry):
        fetch(c).wait()
        work(stage, EARLY, c)
        return carry

    lax.fori_loop(0, EARLY // ROWS, step_early, 0)
    lax.fori_loop(0, copies, step, 0)


def local_kernel(cols, v2, th, tl, wf, wb):
    wb[...] = jnp.zeros_like(wb)

    def step(c, carry):
        rows = [c * ROWS + r for r in range(ROWS)]
        highs = [[th[i, k] for k in range(4)] for i in rows]
        lows = [[tl[i, k] for k in range(4)] for i in rows]
        local_rows(rows, cols, v2, highs, lows, wf, wb)
        return carry

    lax.fori_loop(0, v2.shape[0] // ROWS, step, 0)


def arrive(rows, flags, received, ch, cl, acc):
    faces = rows.shape[1]

    def step(s, carry):
        outs = []
        for axis in range(2):
            odd = flags[4 + axis] > 0
            for r in range(ROWS):
                j = s * ROWS + r
                even, other = received[2 * axis][j], received[2 * axis + 1][j]
                u2 = stacked(jnp.where(flags[2 * axis] > 0, jnp.where(odd, other, even), 0.0))
                gain = two_piece(dot_nt, u2, ch[axis, j], cl[axis, j])
                outs.append((axis, j, gain, jnp.where(flags[2 * axis + 1] > 0, jnp.where(odd, even, other), 0.0)))
        for axis, j, gain, low in outs:
            place_rows(acc, rows, 2 * axis, gain, j)
            place_rows(acc, rows, 2 * axis + 1, low, j)
        return carry

    lax.fori_loop(0, faces // ROWS, step, 0)


def next_kernel(order, rows, flags, bounds, *refs):
    if order == 1:
        (v, wf, wb, diag, ux, lx, uy, ly, ch, cl, *outs, acc) = refs
        older = None
    else:
        (v, older, wf, wb, diag, ux, lx, uy, ly, ch, cl, *outs, acc) = refs
    new, new2, *sends = outs
    acc[...] = jnp.zeros_like(acc)
    arrive(rows, flags, (ux, lx, uy, ly), ch, cl, acc)
    lower = jnp.full((16, 128), bounds[0], F32)
    upper = jnp.full((16, 128), bounds[1], F32)
    half = (upper - lower) / 2.0
    centre = (upper + lower) / 2.0
    scale = (1.0 if order == 1 else 2.0) / half
    group = 8

    def step(s, carry):
        part = pl.ds(s * group, group)
        x = v[part]
        ax = wf[part] + wb[part] + acc[part] + diag[part][:, None, :] * x
        y = (ax - centre * x) * scale
        if older is not None:
            y = y - older[part]
        new[part] = y
        new2[part] = stacked(y)
        return carry

    lax.fori_loop(0, v.shape[0] // group, step, 0)
    if order < 3:
        leave(new, new2, rows, flags, ch, cl, sends)
        return
    mx, my, gram = sends

    def copy(j, carry):
        mx[j] = new[rows[1, j]]
        my[j] = new[rows[3, j]]
        return carry

    lax.fori_loop(0, rows.shape[1], copy, 0, unroll=8)
    total = jnp.zeros((32, 32), F32)
    for s in range(0, v.shape[0], 16):
        x2 = cat([new2[s + r] for r in range(16)], axis=1)
        total = total + dot_nt(x2, x2)
    gram[...] = quarter(total)


def quarter(total):
    half = total.shape[0] // 2
    return (total[:half, :half] + total[half:, half:]) + (total[:half, half:] + total[half:, :half])


def spread(out, gram, half):
    value = cat([gram[:8], gram[8:], half[:8], half[8:]], axis=1)
    value = cat([value, jnp.zeros((8, 128 - value.shape[1]), F32)], axis=1)

    def step(d, carry):
        out[d] = value
        return carry

    lax.fori_loop(0, out.shape[0], step, 0)


def project_kernel(cols, v, v2, diag, th, out, y2):
    def step(c, carry):
        outs = []
        for r in range(ROWS):
            i = c * ROWS + r
            g2 = cat([v2[cols[k, i]] for k in range(4)], axis=1)
            outs.append((i, fold(dot_nt(g2, cat([th[i, k] for k in range(4)], axis=1)))))
        for i, forward in outs:
            y2[i] = stacked((forward + 0.5 * (diag[pl.ds(i, 1)] * v[i])) * SHRINK)
        return carry

    lax.fori_loop(0, v.shape[0] // ROWS, step, 0)
    total = jnp.zeros((32, 32), F32)
    for s in range(0, v.shape[0], 16):
        a2 = cat([v2[s + r] for r in range(16)], axis=1)
        b2 = cat([y2[s + r] for r in range(16)], axis=1)
        total = total + dot_nt(a2, b2)
    out[...] = quarter(total)


def project_faces_kernel(rows, flags, v2, ux, uy, ch, part, gram, out):
    total = jnp.zeros((32, 32), F32)
    for axis, upper in ((0, ux), (1, uy)):
        for s in range(0, rows.shape[1], ROWS):
            lefts, rights = [], []
            for r in range(ROWS):
                j = s + r
                u2 = stacked(jnp.where(flags[2 * axis] > 0, upper[j], 0.0))
                rights.append(stacked(fold(dot_nt(u2, ch[axis, j])) * SHRINK))
                lefts.append(v2[rows[2 * axis, j]])
            total = total + dot_nt(cat(lefts, axis=1), cat(rights, axis=1))
    spread(out, gram[...], part[...] + quarter(total))


def end_kernel(nodes, sums, v2, basis, projected):
    total = sums[0]
    for d in range(1, sums.shape[0]):
        total = total + sums[d]
    n = v2.shape[1] // 2
    g = cat([total[:, :n], total[:, n : 2 * n]], axis=0) / nodes
    half = cat([total[:, 2 * n : 3 * n], total[:, 3 * n : 4 * n]], axis=0)
    row = lax.broadcasted_iota(jnp.int32, (n, n), 0)
    col = lax.broadcasted_iota(jnp.int32, (n, n), 1)
    e = jnp.where(row == col, 1.0, 0.0).astype(F32)
    pivots = jnp.zeros((n, n), F32)
    for k in range(n):
        pivot = jnp.broadcast_to(g[k : k + 1, k : k + 1], (n, n))
        pivots = jnp.where(row == k, pivot, pivots)
        factor = jnp.broadcast_to(g[:, k : k + 1], (n, n)) / pivot
        factor = jnp.where(row > k, factor, 0.0)
        g = g - factor * g[k : k + 1, :]
        e = e - factor * e[k : k + 1, :]
    inv = e / jnp.sqrt(pivots)
    high, low = split(inv)
    left = cat([cat([high, high], axis=1), cat([low, jnp.zeros_like(low)], axis=1)], axis=0)
    for s in range(0, v2.shape[0], 8):
        out = fold(dot_nn(left, cat([v2[s + r] for r in range(8)], axis=1)))
        for r in range(8):
            basis[s + r] = out[:, r * 128 : (r + 1) * 128]
    exact = dict(precision=lax.Precision.HIGHEST, preferred_element_type=F32)
    raw = lax.dot_general(inv, half, (((1,), (0,)), ((), ())), **exact)
    raw = lax.dot_general(raw, inv, (((1,), (1,)), ((), ())), **exact)
    projected[...] = (raw + raw.T) * (1.0 / (SHRINK * nodes))


def in_hbm(x):
    return pltpu.with_memory_space_constraint(x, pltpu.HBM)


def in_vmem(shape, dtype):
    return pltpu.VMEM(shape, dtype)


def call(kernel, name, specs, outs, scratch=(), limit=6, flops=0, nbytes=0, smem=0):
    return pl.pallas_call(
        kernel,
        name=name,
        in_specs=specs,
        out_specs=[SM] * smem + [VM] * (len(outs) - smem),
        out_shape=outs,
        scratch_shapes=list(scratch),
        cost_estimate=pl.CostEstimate(flops=flops, bytes_accessed=nbytes, transcendentals=0),
        compiler_params=pltpu.CompilerParams(vmem_limit_bytes=limit * MIB),
    )


def ring(x, axis, by):
    peers = lax.axis_size(axis)
    return lax.ppermute(x, axis, [(i, (i + by) % peers) for i in range(peers)])


def pairs(x, axis, odd):
    nx, ny = lax.axis_size("gx"), lax.axis_size("gy")
    moves = []
    for u in range(nx):
        for w in range(ny):
            at, size = (u, nx) if axis == 0 else (w, ny)
            if odd and at in (0, size - 1):
                to = (u, w ^ 1) if axis == 0 else (u ^ 1, w)
            else:
                other = at + 1 if at % 2 == odd else at - 1
                to = (other, w) if axis == 0 else (u, other)
            moves.append((u * ny + w, to[0] * ny + to[1]))
    return lax.ppermute(x, ("gx", "gy"), moves)


def shards(start_block, tiles, tile_cols, node_diag, face_tiles, face_rows, filter_bounds):
    block = start_block[0, 0]
    stored = tiles[0, 0]
    cols = tile_cols[0, 0].T
    diag = node_diag[0, 0]
    coupling = face_tiles[0, 0]
    rows = face_rows[0, 0]
    count, width, tile = block.shape
    faces = rows.shape[1]
    nx, ny = lax.axis_size("gx"), lax.axis_size("gy")
    peers = nx * ny
    nodes = float(count * tile * peers)
    ix, iy = lax.axis_index("gx"), lax.axis_index("gy")
    flags = jnp.stack(
        [ix < nx - 1, ix > 0, iy < ny - 1, iy > 0, ix % 2 == 1, iy % 2 == 1]
    ).astype(jnp.int32)

    vec = in_vmem((count, width, tile), F32)
    vec2 = in_vmem((count, 2 * width, tile), BF16)
    face = jax.ShapeDtypeStruct((faces, width, tile), F32)
    tile2 = in_vmem(stored.shape, BF16)
    face2 = in_vmem(coupling.shape, BF16)
    square = in_vmem((width, width), F32)
    small = jax.ShapeDtypeStruct((peers, 8, 128), F32)
    local_flops = 16 * stored.size * width

    rows, cols, filter_bounds, flags, ch, cl, block, x2, *sends, early = call(
        begin_kernel, "begin", [HBM] * 7,
        [
            pltpu.SMEM(rows.shape, jnp.int32), pltpu.SMEM(cols.shape, jnp.int32),
            pltpu.SMEM((2,), F32), pltpu.SMEM(flags.shape, jnp.int32),
            face2, face2, vec, vec2, face, face, face, face,
            in_vmem((EARLY,) + stored.shape[1:], F32),
        ],
        [pltpu.VMEM(coupling.shape, F32), pltpu.SemaphoreType.DMA((2 * (faces // ROWS) + 6,))],
        limit=6, flops=local_flops // 2, nbytes=4 * stored.size // 2, smem=4,
    )(*(in_hbm(x) for x in (rows, cols, filter_bounds, flags, block, coupling, stored)))

    def exchange(sends):
        return tuple(pairs(x, k // 2, k % 2) for k, x in enumerate(sends))

    received = exchange(sends)
    wf, wb, th, tl = call(
        first_kernel, "local_first", [SM, VM, VM, HBM], [vec, vec, tile2, tile2],
        [
            pltpu.VMEM((count - EARLY,) + stored.shape[1:], F32),
            pltpu.SemaphoreType.DMA(((count - EARLY) // ROWS,)),
        ],
        limit=14, flops=local_flops, nbytes=4 * stored.size,
    )(cols, x2, early, in_hbm(stored))

    x, older = block, None
    for order in (1, 2, 3):
        carried = (x,) if older is None else (x, older)
        last = order == 3
        outs = [vec, vec2] + ([face, face, square] if last else [face] * 4)
        new, new2, *sends = call(
            functools.partial(next_kernel, order), "finish%d" % order,
            [SM, SM, SM] + [VM] * (9 + len(carried)), outs,
            [pltpu.VMEM((count, width, tile), F32)],
        )(rows, flags, filter_bounds, *carried, wf, wb, diag, *received, ch, cl)
        x, x2, older = new, new2, x
        if not last:
            received = exchange(sends)
            wf, wb = call(
                local_kernel, "local%d" % (order + 1), [SM] + [VM] * 3, [vec, vec],
                flops=local_flops, nbytes=4 * stored.size,
            )(cols, x2, th, tl)
    mx, my, gram = sends
    ux, uy = ring(mx, "gx", -1), ring(my, "gy", -1)
    (part,) = call(
        project_kernel, "project", [SM] + [VM] * 4, [square],
        [pltpu.VMEM((count, 2 * width, tile), BF16)],
        flops=local_flops // 4, nbytes=2 * stored.size,
    )(cols, x, x2, diag, th)
    (sums,) = call(project_faces_kernel, "project_faces", [SM, SM] + [VM] * 6, [small])(
        rows, flags, x2, ux, uy, ch, part, gram
    )
    sums = lax.all_to_all(sums, ("gx", "gy"), 0, 0)
    basis, projected = call(
        functools.partial(end_kernel, nodes), "end", [VM, VM],
        [jax.ShapeDtypeStruct((count, width, tile), F32), jax.ShapeDtypeStruct((width, width), F32)],
    )(sums, x2)
    return (basis[None, None], projected)


def solution(mesh):
    in_specs = (
        P("gx", "gy", None, None, None),
        P("gx", "gy", None, None, None, None),
        P("gx", "gy", None, None),
        P("gx", "gy", None, None),
        P("gx", "gy", None, None, None, None),
        P("gx", "gy", None, None),
        P(),
    )
    out_specs = (P("gx", "gy", None, None, None), P())
    return jax.shard_map(shards, mesh=mesh, in_specs=in_specs, out_specs=out_specs, check_vma=False)
```

time: 123 us -> 76.1 us (0.62)
  local copies, waits for them, and re-layouts: 28.5 us -> 0.11 us
  starting transfers between devices: 32.9 us -> 15.5 us
  blocking collectives: 0 us -> 12.9 us
  Pallas kernels: 56.2 us -> 45.9 us
  waiting for transfers between devices: 2.92 us -> 0.04 us
    unnamed x45 -> x2, local copies, waits for them, and re-layouts: 27.9 us -> 0.01 us
    ppermute x14 -> x2, starting transfers between devices: 24.5 us -> 3.07 us  [ring(): return lax.ppermute(x, axis, [(i, (i + by) % peers) for i in range(peers)])]
    all_to_all x0 -> x1, blocking collectives: none -> 12.9 us  [shards(): sums = lax.all_to_all(sums, ('gx', 'gy'), 0, 0)]
    ppermute x0 -> x12, starting transfers between devices: none -> 12.4 us  [pairs(): return lax.ppermute(x, ('gx', 'gy'), moves)]
    all_to_all x2 -> x0, starting transfers between devices: 8.4 us -> none  [the longest x1 5.84 us: shards(): sums = lax.all_to_all(sums, ('gx', 'gy'), 0, 0)]
    pallas_call x6 -> x5, Pallas kernels: 25.5 us -> 20.9 us  [the longest x1 7.77 us: shards(): call(first_kernel, 'local_first', [SM, VM, VM, HBM], [vec, vec, tile2, ti...]
    pallas_call x3, Pallas kernels: 13.4 us -> 9.81 us  [shards(): call(functools.partial(next_kernel, order), 'finish%d' % order, [SM, SM,...]
    all_to_all x2 -> x0, waiting for transfers between devices: 2.87 us -> none  [the longest x1 2.87 us: shards(): sums = lax.all_to_all(sums, ('gx', 'gy'), 0, 0)]
  transfers between devices with their start and end apart: 16 -> 14, of which waited for: 1 -> 0; matrix products, arithmetic and copies ran while one was open for 4% -> 0% of each run, Pallas kernels for 31% -> 36%
where the time goes in v2:
time: 76.1 us; the launch traced here: 75.9 us
  Pallas kernels  45.9 us (60%)
  starting transfers between devices  15.5 us (20%)
  blocking collectives  12.9 us (17%)
  between operations  0.82 us (1%)
    pallas_call x2, Pallas kernels, shards(): call(local_kernel, 'local%d' % (order + 1), [SM] + [VM] * 3, [vec, vec],...  15.2 us
    all_to_all x1, blocking collectives, shards(): sums = lax.all_to_all(sums, ('gx', 'gy'), 0, 0)  12.9 us
    ppermute x12, starting transfers between devices, pairs(): return lax.ppermute(x, ('gx', 'gy'), moves)  12.4 us
    pallas_call x3, Pallas kernels, shards(): call(functools.partial(next_kernel, order), 'finish%d' % order, [SM, SM,...  9.81 us
    pallas_call x1, Pallas kernels, shards(): call(first_kernel, 'local_first', [SM, VM, VM, HBM], [vec, vec, tile2, ti...  7.77 us
    pallas_call x1, Pallas kernels, shards(): call(project_kernel, 'project', [SM] + [VM] * 4, [square], [pltpu.VMEM((c...  4.14 us
    pallas_call x1, Pallas kernels, shards(): call(begin_kernel, 'begin', [HBM] * 7, [pltpu.SMEM(rows.shape, jnp.int32)...  4.02 us
    pallas_call x1, Pallas kernels, shards(): call(functools.partial(end_kernel, nodes), 'end', [VM, VM], [jax.ShapeDty...  3.11 us
  transfers between devices with their start and end apart: 14, of which 0 were waited for; matrix products, arithmetic and copies ran while one was open for 0% of the time, Pallas kernels for 36%

profile of v2, /device:TPU:0, one launch (start us, length us, event | category | flops | bytes accessed | tf_op | source)
XLA Modules:
  0.0 75.9 jit_solution(4755632140302929762)
XLA Ops:
  0.7 0.1 stack.27
  0.8 0.5 convert_element_type.3.flags_in
  1.3 4.0 %begin.1 = (s32[4,24]{1,0:T(4,128)S(4)}, s32[4,64]{1,0:T(4,128)S(4)}, f32[2]{0:T(128)S(4)}, s32[6]{0:T(128)S(4)}, bf16[2,24,128,128]{3,2,1,0:T(8,128)(2,1)S(1)},...) custom-call(s32[4,24]{1,0:T(4,128)} %bitcast.23, ...), custom_call_target="tpu_custom_call" | custom-call | flops 536870912 | bytes 8388608 | tf_op jit(solution)/shard_map/begin/pallas_call | solution.py:405
  5.3 3.1 %collective-permute-start = (f32[24,16,128]{2,1,0:T(8,128)S(1)}, f32[24,16,128]{2,1,0:T(8,128)S(1)}, u32[]{:S(2)}, u32[]{:S(2)}) collective-permute-start(f32[24,16,128]{2,1,0:T(8,128)S(1)} %get-tuple-element.51), channel_id=1, source_target_pairs={{0,8},{1,9},{2,10},{3,11},{4,12},{5,13},{6,14},{7,15},{8,0},{9,1},... | collective-permute-start | bytes 589832 | tf_op jit(solution)/shard_map/ppermute | solution.py:376
  8.4 0.5 collective-permute-start.2
  8.9 2.6 %collective-permute-start.3 = (f32[24,16,128]{2,1,0:T(8,128)S(1)}, f32[24,16,128]{2,1,0:T(8,128)S(1)}, u32[]{:S(2)}, u32[]{:S(2)}) collective-permute-start(f32[24,16,128]{2,1,0:T(8,128)S(1)} %get-tuple-element.54), channel_id=1, source_target_pairs={{0,8},{1,2},{2,1},{3,4},{4,3},{5,6},{6,5},{7,15},{8,0},{9,10},{10,... | collective-permute-start | bytes 589832 | tf_op jit(solution)/shard_map/ppermute | solution.py:376
  11.6 7.8 %local_first.1 = (f32[64,16,128]{2,1,0:T(8,128)S(1)}, f32[64,16,128]{2,1,0:T(8,128)S(1)}, bf16[64,4,128,128]{3,2,1,0:T(8,128)(2,1)S(1)}, bf16[64,4,128,128]{3,2,1,0:T(8,128)(2,1)S(1)}) custom-call(s32[4,64]{1,0:T(4,128)S(4)} %get-tuple-element.46.cols, bf16[64,32,128]{2,1,0:T(8,128)(2,1)S(1)} %get-tuple-element.47.v2, ...), custom_call_target="tpu_custom_call" | custom-call | flops 1073741824 | bytes 16777216 | tf_op jit(solution)/shard_map/local_first/pallas_call | solution.py:421
  19.4 3.5 %finish1.1 = (f32[64,16,128]{2,1,0:T(8,128)S(1)}, bf16[64,32,128]{2,1,0:T(8,128)(2,1)S(1)}, f32[24,16,128]{2,1,0:T(8,128)S(1)}, f32[24,16,128]{2,1,0:T(8,128)S(1...) custom-call(s32[4,24]{1,0:T(4,128)S(4)} %get-tuple-element.42.rows, s32[6]{0:T(128)S(4)} %get-tuple-element.43.flags, ...), custom_call_target="tpu_custom_call" | custom-call | tf_op jit(solution)/shard_map/finish1/pallas_call | solution.py:435
  22.9 0.1 collective-permute-start.4
  23.0 1.3 %collective-permute-start.5 = (f32[24,16,128]{2,1,0:T(8,128)S(1)}, f32[24,16,128]{2,1,0:T(8,128)S(1)}, u32[]{:S(2)}, u32[]{:S(2)}) collective-permute-start(f32[24,16,128]{2,1,0:T(8,128)S(1)} %get-tuple-element.64), channel_id=1, source_target_pairs={{0,1},{1,0},{2,3},{3,2},{4,5},{5,4},{6,7},{7,6},{8,16},{9,17},{10,... | collective-permute-start | bytes 589832 | tf_op jit(solution)/shard_map/ppermute | solution.py:376
  24.3 0.7 collective-permute-start.7
  25.0 7.6 %local2.1 = (f32[64,16,128]{2,1,0:T(8,128)S(1)}, f32[64,16,128]{2,1,0:T(8,128)S(1)}) custom-call(s32[4,64]{1,0:T(4,128)S(4)} %get-tuple-element.46.cols, bf16[64,32,128]{2,1,0:T(8,128)(2,1)S(1)} %get-tuple-element.58.v2, bf16[64,4,128,128]{3,2,1,0:T(8,128)(2,1)S(1)} %get-tuple-element.59.th, bf16[64,4,128,128]{3,2,1,0:T(8,128)(2,1)S(1)} %get-tuple-element.60.tl), custom_call_target="tpu_custom_call" | custom-call | flops 1073741824 | bytes 16777216 | tf_op jit(solution)/shard_map/local2/pallas_call | solution.py:443
  32.6 3.5 %finish2.1 = (f32[64,16,128]{2,1,0:T(8,128)S(1)}, bf16[64,32,128]{2,1,0:T(8,128)(2,1)S(1)}, f32[24,16,128]{2,1,0:T(8,128)S(1)}, f32[24,16,128]{2,1,0:T(8,128)S(1...) custom-call(s32[4,24]{1,0:T(4,128)S(4)} %get-tuple-element.42.rows, s32[6]{0:T(128)S(4)} %get-tuple-element.43.flags, ...), custom_call_target="tpu_custom_call" | custom-call | tf_op jit(solution)/shard_map/finish2/pallas_call | solution.py:435
  36.1 1.4 %collective-permute-start.8 = (f32[24,16,128]{2,1,0:T(8,128)S(1)}, f32[24,16,128]{2,1,0:T(8,128)S(1)}, u32[]{:S(2)}, u32[]{:S(2)}) collective-permute-start(f32[24,16,128]{2,1,0:T(8,128)S(1)} %get-tuple-element.71), channel_id=1, source_target_pairs={{0,8},{1,9},{2,10},{3,11},{4,12},{5,13},{6,14},{7,15},{8,0},{9,1},... | collective-permute-start | bytes 589832 | tf_op jit(solution)/shard_map/ppermute | solution.py:376
  37.5 0.5 collective-permute-start.10
  38.0 2.2 %collective-permute-start.11 = (f32[24,16,128]{2,1,0:T(8,128)S(1)}, f32[24,16,128]{2,1,0:T(8,128)S(1)}, u32[]{:S(2)}, u32[]{:S(2)}) collective-permute-start(f32[24,16,128]{2,1,0:T(8,128)S(1)} %get-tuple-element.74), channel_id=1, source_target_pairs={{0,8},{1,2},{2,1},{3,4},{4,3},{5,6},{6,5},{7,15},{8,0},{9,10},{10,... | collective-permute-start | bytes 589832 | tf_op jit(solution)/shard_map/ppermute | solution.py:376
  40.2 7.6 %local3.1 = (f32[64,16,128]{2,1,0:T(8,128)S(1)}, f32[64,16,128]{2,1,0:T(8,128)S(1)}) custom-call(s32[4,64]{1,0:T(4,128)S(4)} %get-tuple-element.46.cols, bf16[64,32,128]{2,1,0:T(8,128)(2,1)S(1)} %get-tuple-element.68.v2, bf16[64,4,128,128]{3,2,1,0:T(8,128)(2,1)S(1)} %get-tuple-element.59.th, bf16[64,4,128,128]{3,2,1,0:T(8,128)(2,1)S(1)} %get-tuple-element.60.tl), custom_call_target="tpu_custom_call" | custom-call | flops 1073741824 | bytes 16777216 | tf_op jit(solution)/shard_map/local3/pallas_call | solution.py:443
  47.9 2.8 %finish3.1 = (f32[64,16,128]{2,1,0:T(8,128)S(1)}, bf16[64,32,128]{2,1,0:T(8,128)(2,1)S(1)}, f32[24,16,128]{2,1,0:T(8,128)S(1)}, f32[24,16,128]{2,1,0:T(8,128)S(1)}, f32[16,16]{1,0:T(8,128)S(1)}) custom-call(s32[4,24]{1,0:T(4,128)S(4)} %get-tuple-element.42.rows, s32[6]{0:T(128)S(4)} %get-tuple-element.43.flags, f32[2]{0:T(128)S(4)} %get-tuple-element.44.bounds, ...), custom_call_target="tpu_custom_call" | custom-call | tf_op jit(solution)/shard_map/finish3/pallas_call | solution.py:435
  50.7 1.3 %collective-permute-start.12 = (f32[24,16,128]{2,1,0:T(8,128)S(1)}, f32[24,16,128]{2,1,0:T(8,128)S(1)}, u32[]{:S(2)}, u32[]{:S(2)}) collective-permute-start(f32[24,16,128]{2,1,0:T(8,128)S(1)} %get-tuple-element.76), channel_id=1, source_target_pairs={{0,24},{8,0},{16,8},{24,16},{1,25},{9,1},{17,9},{25,17},{2,26},{10... | collective-permute-start | bytes 589832 | tf_op jit(solution)/shard_map/ppermute | solution.py:361
  52.0 1.8 %collective-permute-start.13 = (f32[24,16,128]{2,1,0:T(8,128)S(1)}, f32[24,16,128]{2,1,0:T(8,128)S(1)}, u32[]{:S(2)}, u32[]{:S(2)}) collective-permute-start(f32[24,16,128]{2,1,0:T(8,128)S(1)} %get-tuple-element.77), channel_id=1, source_target_pairs={{0,7},{1,0},{2,1},{3,2},{4,3},{5,4},{6,5},{7,6},{8,15},{9,8},{10,9... | collective-permute-start | bytes 589832 | tf_op jit(solution)/shard_map/ppermute | solution.py:361
  53.8 4.1 %project.1.part = f32[16,16]{1,0:T(8,128)S(1)} custom-call(s32[4,64]{1,0:T(4,128)S(4)} %get-tuple-element.46.cols, f32[64,16,128]{2,1,0:T(8,128)S(1)} %get-tuple-element.78.v, bf16[64,32,128]{2,1,0:T(8,128)(2,1)S(1)} %get-tuple-element.75.v2, f32[64,128]{1,0:T(8,128)S(1)} %bitcast.18, bf16[64,4,128,128]{3,2,1,0:T(8,128)(2,1)S(1)} %get-tuple-element.59.th), custom_call_target="tpu_custom_call" | custom-call | flops 268435456 | bytes 8388608 | tf_op jit(solution)/shard_map/project/pallas_call | solution.py:449
  58.0 1.9 %project_faces.1 = f32[32,8,128]{2,1,0:T(8,128)S(1)} custom-call(s32[4,24]{1,0:T(4,128)S(4)} %get-tuple-element.42.rows, s32[6]{0:T(128)S(4)} %get-tuple-element.43.flags, bf16[64,32,128]{2,1,0:T(8,128)(2,1)S(1)} %get-tuple-element.75.v2, f32[24,16,128]{2,1,0:T(8,128)S(1)} %collective-permute-done.12.ux, f32[24,16,128]{2,1,0:T(8,128)S(1)} %collective-permute-done.13.uy, ...), custom_call_target="tpu_custom_call" | custom-call | tf_op jit(solution)/shard_map/project_faces/pallas_call | solution.py:454
  59.8 12.9 %all_to_all.5.sums = f32[32,8,128]{2,1,0:T(8,128)S(1)} all-to-all(f32[32,8,128]{2,1,0:T(8,128)S(1)} %project_faces.1), channel_id=1, replica_groups=mesh['gx'=4,'gy'=8] {'gx','gy'}, dimensions={0} | all-to-all | bytes 262144 | tf_op jit(solution)/shard_map/all_to_all | solution.py:457
  72.8 3.1 %end.1 = (f32[64,16,128]{2,1,0:T(8,128)}, f32[16,16]{1,0:T(8,128)}) custom-call(f32[32,8,128]{2,1,0:T(8,128)S(1)} %all_to_all.5.sums, bf16[64,32,128]{2,1,0:T(8,128)(2,1)S(1)} %get-tuple-element.75.v2), custom_call_target="tpu_custom_call" | custom-call | tf_op jit(solution)/shard_map/end/pallas_call | solution.py:458
  (19 shorter events, 0.0 us)
Async XLA Ops:
  5.3 14.0 %collective-permute-start = (f32[24,16,128]{2,1,0:T(8,128)S(1)}, f32[24,16,128]{2,1,0:T(8,128)S(1)}, u32[]{:S(2)}, u32[]{:S(2)}) collective-permute-start(f32[24,16,128]{2,1,0:T(8,128)S(1)} %get-tuple-element.51), channel_id=1, source_target_pairs={{0,8},{1,9},{2,10},{3,11},{4,12},{5,13},{6,14},{7,15},{8,0},{9,1},... | collective-permute-start | bytes 589832 | tf_op jit(solution)/shard_map/ppermute | solution.py:376
  8.4 10.9 %collective-permute-start.1 = (f32[24,16,128]{2,1,0:T(8,128)S(1)}, f32[24,16,128]{2,1,0:T(8,128)S(1)}, u32[]{:S(2)}, u32[]{:S(2)}) collective-permute-start(f32[24,16,128]{2,1,0:T(8,128)S(1)} %get-tuple-element.52), channel_id=1, source_target_pairs={{0,1},{1,0},{2,3},{3,2},{4,5},{5,4},{6,7},{7,6},{8,16},{9,17},{10,... | collective-permute-start | bytes 589832 | tf_op jit(solution)/shard_map/ppermute | solution.py:376
  8.4 11.0 %collective-permute-start.2 = (f32[24,16,128]{2,1,0:T(8,128)S(1)}, f32[24,16,128]{2,1,0:T(8,128)S(1)}, u32[]{:S(2)}, u32[]{:S(2)}) collective-permute-start(f32[24,16,128]{2,1,0:T(8,128)S(1)} %get-tuple-element.53), channel_id=1, source_target_pairs={{0,1},{1,0},{2,3},{3,2},{4,5},{5,4},{6,7},{7,6},{8,9},{9,8},{10,11... | collective-permute-start | bytes 589832 | tf_op jit(solution)/shard_map/ppermute | solution.py:376
  8.9 10.5 %collective-permute-start.3 = (f32[24,16,128]{2,1,0:T(8,128)S(1)}, f32[24,16,128]{2,1,0:T(8,128)S(1)}, u32[]{:S(2)}, u32[]{:S(2)}) collective-permute-start(f32[24,16,128]{2,1,0:T(8,128)S(1)} %get-tuple-element.54), channel_id=1, source_target_pairs={{0,8},{1,2},{2,1},{3,4},{4,3},{5,6},{6,5},{7,15},{8,0},{9,10},{10,... | collective-permute-start | bytes 589832 | tf_op jit(solution)/shard_map/ppermute | solution.py:376
  11.6 7.8 %copy-start = (f32[1,1,64,128]{3,2,1,0:T(8,128)S(1)}, f32[1,1,64,128]{3,2,1,0:T(8,128)}, u32[]{:S(2)}) copy-start(f32[1,1,64,128]{3,2,1,0:T(8,128)} %param.10) | copy-start | bytes 98308
  22.9 9.7 %collective-permute-start.4 = (f32[24,16,128]{2,1,0:T(8,128)S(1)}, f32[24,16,128]{2,1,0:T(8,128)S(1)}, u32[]{:S(2)}, u32[]{:S(2)}) collective-permute-start(f32[24,16,128]{2,1,0:T(8,128)S(1)} %get-tuple-element.63), channel_id=1, source_target_pairs={{0,8},{1,9},{2,10},{3,11},{4,12},{5,13},{6,14},{7,15},{8,0},{9,1},... | collective-permute-start | bytes 589832 | tf_op jit(solution)/shard_map/ppermute | solution.py:376
  23.0 9.6 %collective-permute-start.5 = (f32[24,16,128]{2,1,0:T(8,128)S(1)}, f32[24,16,128]{2,1,0:T(8,128)S(1)}, u32[]{:S(2)}, u32[]{:S(2)}) collective-permute-start(f32[24,16,128]{2,1,0:T(8,128)S(1)} %get-tuple-element.64), channel_id=1, source_target_pairs={{0,1},{1,0},{2,3},{3,2},{4,5},{5,4},{6,7},{7,6},{8,16},{9,17},{10,... | collective-permute-start | bytes 589832 | tf_op jit(solution)/shard_map/ppermute | solution.py:376
  24.3 8.3 %collective-permute-start.6 = (f32[24,16,128]{2,1,0:T(8,128)S(1)}, f32[24,16,128]{2,1,0:T(8,128)S(1)}, u32[]{:S(2)}, u32[]{:S(2)}) collective-permute-start(f32[24,16,128]{2,1,0:T(8,128)S(1)} %get-tuple-element.65), channel_id=1, source_target_pairs={{0,1},{1,0},{2,3},{3,2},{4,5},{5,4},{6,7},{7,6},{8,9},{9,8},{10,11... | collective-permute-start | bytes 589832 | tf_op jit(solution)/shard_map/ppermute | solution.py:376
  24.3 8.3 %collective-permute-start.7 = (f32[24,16,128]{2,1,0:T(8,128)S(1)}, f32[24,16,128]{2,1,0:T(8,128)S(1)}, u32[]{:S(2)}, u32[]{:S(2)}) collective-permute-start(f32[24,16,128]{2,1,0:T(8,128)S(1)} %get-tuple-element.66), channel_id=1, source_target_pairs={{0,8},{1,2},{2,1},{3,4},{4,3},{5,6},{6,5},{7,15},{8,0},{9,10},{10,... | collective-permute-start | bytes 589832 | tf_op jit(solution)/shard_map/ppermute | solution.py:376
  36.1 11.7 %collective-permute-start.8 = (f32[24,16,128]{2,1,0:T(8,128)S(1)}, f32[24,16,128]{2,1,0:T(8,128)S(1)}, u32[]{:S(2)}, u32[]{:S(2)}) collective-permute-start(f32[24,16,128]{2,1,0:T(8,128)S(1)} %get-tuple-element.71), channel_id=1, source_target_pairs={{0,8},{1,9},{2,10},{3,11},{4,12},{5,13},{6,14},{7,15},{8,0},{9,1},... | collective-permute-start | bytes 589832 | tf_op jit(solution)/shard_map/ppermute | solution.py:376
  37.5 10.4 %collective-permute-start.9 = (f32[24,16,128]{2,1,0:T(8,128)S(1)}, f32[24,16,128]{2,1,0:T(8,128)S(1)}, u32[]{:S(2)}, u32[]{:S(2)}) collective-permute-start(f32[24,16,128]{2,1,0:T(8,128)S(1)} %get-tuple-element.72), channel_id=1, source_target_pairs={{0,1},{1,0},{2,3},{3,2},{4,5},{5,4},{6,7},{7,6},{8,16},{9,17},{10,... | collective-permute-start | bytes 589832 | tf_op jit(solution)/shard_map/ppermute | solution.py:376
  37.5 10.4 %collective-permute-start.10 = (f32[24,16,128]{2,1,0:T(8,128)S(1)}, f32[24,16,128]{2,1,0:T(8,128)S(1)}, u32[]{:S(2)}, u32[]{:S(2)}) collective-permute-start(f32[24,16,128]{2,1,0:T(8,128)S(1)} %get-tuple-element.73), channel_id=1, source_target_pairs={{0,1},{1,0},{2,3},{3,2},{4,5},{5,4},{6,7},{7,6},{8,9},{9,8},{10,11... | collective-permute-start | bytes 589832 | tf_op jit(solution)/shard_map/ppermute | solution.py:376
  38.0 9.9 %collective-permute-start.11 = (f32[24,16,128]{2,1,0:T(8,128)S(1)}, f32[24,16,128]{2,1,0:T(8,128)S(1)}, u32[]{:S(2)}, u32[]{:S(2)}) collective-permute-start(f32[24,16,128]{2,1,0:T(8,128)S(1)} %get-tuple-element.74), channel_id=1, source_target_pairs={{0,8},{1,2},{2,1},{3,4},{4,3},{5,6},{6,5},{7,15},{8,0},{9,10},{10,... | collective-permute-start | bytes 589832 | tf_op jit(solution)/shard_map/ppermute | solution.py:376
  50.7 7.2 %collective-permute-start.12 = (f32[24,16,128]{2,1,0:T(8,128)S(1)}, f32[24,16,128]{2,1,0:T(8,128)S(1)}, u32[]{:S(2)}, u32[]{:S(2)}) collective-permute-start(f32[24,16,128]{2,1,0:T(8,128)S(1)} %get-tuple-element.76), channel_id=1, source_target_pairs={{0,24},{8,0},{16,8},{24,16},{1,25},{9,1},{17,9},{25,17},{2,26},{10... | collective-permute-start | bytes 589832 | tf_op jit(solution)/shard_map/ppermute | solution.py:361
  52.0 5.9 %collective-permute-start.13 = (f32[24,16,128]{2,1,0:T(8,128)S(1)}, f32[24,16,128]{2,1,0:T(8,128)S(1)}, u32[]{:S(2)}, u32[]{:S(2)}) collective-permute-start(f32[24,16,128]{2,1,0:T(8,128)S(1)} %get-tuple-element.77), channel_id=1, source_target_pairs={{0,7},{1,0},{2,1},{3,2},{4,3},{5,4},{6,5},{7,6},{8,15},{9,8},{10,9... | collective-permute-start | bytes 589832 | tf_op jit(solution)/shard_map/ppermute | solution.py:361

commit v3 on v2

--- a/solution.py
+++ b/solution.py
@@ -16,7 +16,8 @@
 cat = jnp.concatenate
 
 ROWS = 8
-EARLY = 24
+FACES = 24
+EARLY = 16
 SHRINK = 1.0 / 64.0
 
 
@@ -58,18 +59,18 @@
     def step(s, carry):
         outs = []
         for axis in range(2):
-            for r in range(ROWS):
-                j = s * ROWS + r
+            for r in range(FACES):
+                j = s * FACES + r
                 x2 = v2[rows[2 * axis, j]]
                 outs.append((axis, j, two_piece(dot_nn, x2, ch[axis, j], cl[axis, j])))
         for axis, j, out in outs:
             send(rows, flags, v, axis, j, out, sends)
         return carry
 
-    lax.fori_loop(0, rows.shape[1] // ROWS, step, 0)
-
-
-def begin_kernel(rows_in, cols_in, bounds_in, flags_in, block, tiles, stored, *refs):
+    lax.fori_loop(0, rows.shape[1] // FACES, step, 0)
+
+
+def begin_kernel(rows_in, cols_in, bounds_in, block, tiles, stored, *refs):
     (rows, cols, bounds, flags, ch, cl, v, v2, a, b, c, d, early, stage, sems) = refs
     faces = rows.shape[1]
     chunks = faces // ROWS
@@ -84,10 +85,14 @@
         copy.start()
         return copy
 
-    small = [bring(x, y, k) for k, (x, y) in enumerate(((rows_in, rows), (flags_in, flags), (block, v)))]
+    small = [bring(x, y, k) for k, (x, y) in enumerate(((rows_in, rows), (block, v)))]
     for s in range(chunks):
         for axis in range(2):
             fetch(s, axis).start()
+    nx, ny = lax.axis_size("gx"), lax.axis_size("gy")
+    ix, iy = lax.axis_index("gx"), lax.axis_index("gy")
+    for k, flag in enumerate((ix < nx - 1, ix > 0, iy < ny - 1, iy > 0, ix % 2 == 1, iy % 2 == 1)):
+        flags[k] = flag.astype(jnp.int32)
     late = [bring(cols_in, cols, 3), bring(bounds_in, bounds, 4)]
     late.append(bring(stored.at[pl.ds(0, EARLY)], early, 5))
     for copy in small:
@@ -194,8 +199,8 @@
         outs = []
         for axis in range(2):
             odd = flags[4 + axis] > 0
-            for r in range(ROWS):
-                j = s * ROWS + r
+            for r in range(FACES):
+                j = s * FACES + r
                 even, other = received[2 * axis][j], received[2 * axis + 1][j]
                 u2 = stacked(jnp.where(flags[2 * axis] > 0, jnp.where(odd, other, even), 0.0))
                 gain = two_piece(dot_nt, u2, ch[axis, j], cl[axis, j])
@@ -205,7 +210,7 @@
             place_rows(acc, rows, 2 * axis + 1, low, j)
         return carry
 
-    lax.fori_loop(0, faces // ROWS, step, 0)
+    lax.fori_loop(0, faces // FACES, step, 0)
 
 
 def next_kernel(order, rows, flags, bounds, *refs):
@@ -270,22 +275,32 @@
     lax.fori_loop(0, out.shape[0], step, 0)
 
 
-def project_kernel(cols, v, v2, diag, th, out, y2):
+def project_kernel(cols, v, v2, diag, th, out, wb):
+    group = 8
+
+    def begin(s, carry):
+        part = pl.ds(s * group, group)
+        wb[part] = 0.5 * (diag[part][:, None, :] * v[part])
+        return carry
+
+    lax.fori_loop(0, v.shape[0] // group, begin, 0)
+
     def step(c, carry):
         outs = []
         for r in range(ROWS):
             i = c * ROWS + r
-            g2 = cat([v2[cols[k, i]] for k in range(4)], axis=1)
-            outs.append((i, fold(dot_nt(g2, cat([th[i, k] for k in range(4)], axis=1)))))
-        for i, forward in outs:
-            y2[i] = stacked((forward + 0.5 * (diag[pl.ds(i, 1)] * v[i])) * SHRINK)
+            outs.append((i, fold(dot_nn(v2[i], cat([th[i, k] for k in range(4)], axis=1)))))
+        for i, backward in outs:
+            for k in range(4):
+                at = cols[k, i]
+                wb[at] = wb[at] + backward[:, k * 128 : (k + 1) * 128]
         return carry
 
     lax.fori_loop(0, v.shape[0] // ROWS, step, 0)
     total = jnp.zeros((32, 32), F32)
     for s in range(0, v.shape[0], 16):
         a2 = cat([v2[s + r] for r in range(16)], axis=1)
-        b2 = cat([y2[s + r] for r in range(16)], axis=1)
+        b2 = cat([stacked(wb[s + r] * SHRINK) for r in range(16)], axis=1)
         total = total + dot_nt(a2, b2)
     out[...] = quarter(total)
 
@@ -388,11 +403,6 @@
     nx, ny = lax.axis_size("gx"), lax.axis_size("gy")
     peers = nx * ny
     nodes = float(count * tile * peers)
-    ix, iy = lax.axis_index("gx"), lax.axis_index("gy")
-    flags = jnp.stack(
-        [ix < nx - 1, ix > 0, iy < ny - 1, iy > 0, ix % 2 == 1, iy % 2 == 1]
-    ).astype(jnp.int32)
-
     vec = in_vmem((count, width, tile), F32)
     vec2 = in_vmem((count, 2 * width, tile), BF16)
     face = jax.ShapeDtypeStruct((faces, width, tile), F32)
@@ -403,16 +413,16 @@
     local_flops = 16 * stored.size * width
 
     rows, cols, filter_bounds, flags, ch, cl, block, x2, *sends, early = call(
-        begin_kernel, "begin", [HBM] * 7,
+        begin_kernel, "begin", [HBM] * 6,
         [
             pltpu.SMEM(rows.shape, jnp.int32), pltpu.SMEM(cols.shape, jnp.int32),
-            pltpu.SMEM((2,), F32), pltpu.SMEM(flags.shape, jnp.int32),
+            pltpu.SMEM((2,), F32), pltpu.SMEM((6,), jnp.int32),
             face2, face2, vec, vec2, face, face, face, face,
             in_vmem((EARLY,) + stored.shape[1:], F32),
         ],
         [pltpu.VMEM(coupling.shape, F32), pltpu.SemaphoreType.DMA((2 * (faces // ROWS) + 6,))],
         limit=6, flops=local_flops // 2, nbytes=4 * stored.size // 2, smem=4,
-    )(*(in_hbm(x) for x in (rows, cols, filter_bounds, flags, block, coupling, stored)))
+    )(*(in_hbm(x) for x in (rows, cols, filter_bounds, block, coupling, stored)))
 
     def exchange(sends):
         return tuple(pairs(x, k // 2, k % 2) for k, x in enumerate(sends))
@@ -424,7 +434,7 @@
             pltpu.VMEM((count - EARLY,) + stored.shape[1:], F32),
             pltpu.SemaphoreType.DMA(((count - EARLY) // ROWS,)),
         ],
-        limit=14, flops=local_flops, nbytes=4 * stored.size,
+        limit=18, flops=local_flops, nbytes=4 * stored.size,
     )(cols, x2, early, in_hbm(stored))
 
     x, older = block, None
@@ -448,7 +458,7 @@
     ux, uy = ring(mx, "gx", -1), ring(my, "gy", -1)
     (part,) = call(
         project_kernel, "project", [SM] + [VM] * 4, [square],
-        [pltpu.VMEM((count, 2 * width, tile), BF16)],
+        [pltpu.VMEM((count, width, tile), F32)],
         flops=local_flops // 4, nbytes=2 * stored.size,
     )(cols, x, x2, diag, th)
     (sums,) = call(project_faces_kernel, "project_faces", [SM, SM] + [VM] * 6, [small])(

time: 76.1 us -> 73.8 us (0.970)
  Pallas kernels: 45.9 us -> 42.9 us
  blocking collectives: 12.9 us -> 13.9 us
    pallas_call x1, Pallas kernels: 4.14 us -> 2.84 us  [shards(): call(project_kernel, 'project', [SM] + [VM] * 4, [square], [pltpu.VMEM((c...]
    pallas_call x3, Pallas kernels: 9.81 us -> 8.64 us  [shards(): call(functools.partial(next_kernel, order), 'finish%d' % order, [SM, SM,...]
    all_to_all x1, blocking collectives: 12.9 us -> 13.9 us  [shards(): sums = lax.all_to_all(sums, ('gx', 'gy'), 0, 0)]
  transfers between devices with their start and end apart: 14 -> 14, of which waited for: 0 -> 2; matrix products, arithmetic and copies ran while one was open for 0% -> 0% of each run, Pallas kernels for 36% -> 35%
where the time goes in v3:
time: 73.8 us; the launch traced here: 73.6 us
  Pallas kernels  42.9 us (58%)
  starting transfers between devices  15.6 us (21%)
  blocking collectives  13.9 us (19%)
  between operations  0.78 us (1%)
    pallas_call x2, Pallas kernels, shards(): call(local_kernel, 'local%d' % (order + 1), [SM] + [VM] * 3, [vec, vec],...  15.2 us
    all_to_all x1, blocking collectives, shards(): sums = lax.all_to_all(sums, ('gx', 'gy'), 0, 0)  13.9 us
    ppermute x12, starting transfers between devices, pairs(): return lax.ppermute(x, ('gx', 'gy'), moves)  12.5 us
    pallas_call x3, Pallas kernels, shards(): call(functools.partial(next_kernel, order), 'finish%d' % order, [SM, SM,...  8.64 us
    pallas_call x1, Pallas kernels, shards(): call(first_kernel, 'local_first', [SM, VM, VM, HBM], [vec, vec, tile2, ti...  7.77 us
    pallas_call x1, Pallas kernels, shards(): call(begin_kernel, 'begin', [HBM] * 6, [pltpu.SMEM(rows.shape, jnp.int32)...  3.44 us
    ppermute x2, starting transfers between devices, ring(): return lax.ppermute(x, axis, [(i, (i + by) % peers) for i in range(peers)])  3.18 us
    pallas_call x1, Pallas kernels, shards(): call(functools.partial(end_kernel, nodes), 'end', [VM, VM], [jax.ShapeDty...  3.11 us
  transfers between devices with their start and end apart: 14, of which 2 were waited for; matrix products, arithmetic and copies ran while one was open for 0% of the time, Pallas kernels for 35%

profile of v3, /device:TPU:0, one launch (start us, length us, event | category | flops | bytes accessed | tf_op | source)
XLA Modules:
  0.0 73.6 jit_solution(9843006225085743491)
XLA Ops:
  0.6 3.4 %begin.1 = (s32[4,24]{1,0:T(4,128)S(4)}, s32[4,64]{1,0:T(4,128)S(4)}, f32[2]{0:T(128)S(4)}, s32[6]{0:T(128)S(4)}, bf16[2,24,128,128]{3,2,1,0:T(8,128)(2,1)S(1)},...) custom-call(s32[4,24]{1,0:T(4,128)} %bitcast.17, ...), custom_call_target="tpu_custom_call" | custom-call | flops 536870912 | bytes 8388608 | tf_op jit(solution)/shard_map/begin/pallas_call | solution.py:415
  4.1 3.1 %collective-permute-start = (f32[24,16,128]{2,1,0:T(8,128)S(1)}, f32[24,16,128]{2,1,0:T(8,128)S(1)}, u32[]{:S(2)}, u32[]{:S(2)}) collective-permute-start(f32[24,16,128]{2,1,0:T(8,128)S(1)} %get-tuple-element.51), channel_id=1, source_target_pairs={{0,8},{1,9},{2,10},{3,11},{4,12},{5,13},{6,14},{7,15},{8,0},{9,1},... | collective-permute-start | bytes 589832 | tf_op jit(solution)/shard_map/ppermute | solution.py:391
  7.2 0.5 collective-permute-start.2
  7.7 2.6 %collective-permute-start.3 = (f32[24,16,128]{2,1,0:T(8,128)S(1)}, f32[24,16,128]{2,1,0:T(8,128)S(1)}, u32[]{:S(2)}, u32[]{:S(2)}) collective-permute-start(f32[24,16,128]{2,1,0:T(8,128)S(1)} %get-tuple-element.54), channel_id=1, source_target_pairs={{0,8},{1,2},{2,1},{3,4},{4,3},{5,6},{6,5},{7,15},{8,0},{9,10},{10,... | collective-permute-start | bytes 589832 | tf_op jit(solution)/shard_map/ppermute | solution.py:391
  10.3 7.8 %local_first.1 = (f32[64,16,128]{2,1,0:T(8,128)S(1)}, f32[64,16,128]{2,1,0:T(8,128)S(1)}, bf16[64,4,128,128]{3,2,1,0:T(8,128)(2,1)S(1)}, bf16[64,4,128,128]{3,2,1,0:T(8,128)(2,1)S(1)}) custom-call(s32[4,64]{1,0:T(4,128)S(4)} %get-tuple-element.46.cols, bf16[64,32,128]{2,1,0:T(8,128)(2,1)S(1)} %get-tuple-element.47.v2, ...), custom_call_target="tpu_custom_call" | custom-call | flops 1073741824 | bytes 16777216 | tf_op jit(solution)/shard_map/local_first/pallas_call | solution.py:431
  18.2 2.9 %finish1.1 = (f32[64,16,128]{2,1,0:T(8,128)S(1)}, bf16[64,32,128]{2,1,0:T(8,128)(2,1)S(1)}, f32[24,16,128]{2,1,0:T(8,128)S(1)}, f32[24,16,128]{2,1,0:T(8,128)S(1...) custom-call(s32[4,24]{1,0:T(4,128)S(4)} %get-tuple-element.42.rows, s32[6]{0:T(128)S(4)} %get-tuple-element.43.flags, ...), custom_call_target="tpu_custom_call" | custom-call | tf_op jit(solution)/shard_map/finish1/pallas_call | solution.py:445
  21.1 0.1 collective-permute-start.4
  21.2 1.3 %collective-permute-start.5 = (f32[24,16,128]{2,1,0:T(8,128)S(1)}, f32[24,16,128]{2,1,0:T(8,128)S(1)}, u32[]{:S(2)}, u32[]{:S(2)}) collective-permute-start(f32[24,16,128]{2,1,0:T(8,128)S(1)} %get-tuple-element.64), channel_id=1, source_target_pairs={{0,1},{1,0},{2,3},{3,2},{4,5},{5,4},{6,7},{7,6},{8,16},{9,17},{10,... | collective-permute-start | bytes 589832 | tf_op jit(solution)/shard_map/ppermute | solution.py:391
  22.5 0.7 collective-permute-start.7
  23.2 7.6 %local2.1 = (f32[64,16,128]{2,1,0:T(8,128)S(1)}, f32[64,16,128]{2,1,0:T(8,128)S(1)}) custom-call(s32[4,64]{1,0:T(4,128)S(4)} %get-tuple-element.46.cols, bf16[64,32,128]{2,1,0:T(8,128)(2,1)S(1)} %get-tuple-element.58.v2, bf16[64,4,128,128]{3,2,1,0:T(8,128)(2,1)S(1)} %get-tuple-element.59.th, bf16[64,4,128,128]{3,2,1,0:T(8,128)(2,1)S(1)} %get-tuple-element.60.tl), custom_call_target="tpu_custom_call" | custom-call | flops 1073741824 | bytes 16777216 | tf_op jit(solution)/shard_map/local2/pallas_call | solution.py:453
  30.9 2.9 %finish2.1 = (f32[64,16,128]{2,1,0:T(8,128)S(1)}, bf16[64,32,128]{2,1,0:T(8,128)(2,1)S(1)}, f32[24,16,128]{2,1,0:T(8,128)S(1)}, f32[24,16,128]{2,1,0:T(8,128)S(1...) custom-call(s32[4,24]{1,0:T(4,128)S(4)} %get-tuple-element.42.rows, s32[6]{0:T(128)S(4)} %get-tuple-element.43.flags, ...), custom_call_target="tpu_custom_call" | custom-call | tf_op jit(solution)/shard_map/finish2/pallas_call | solution.py:445
  33.8 1.4 %collective-permute-start.8 = (f32[24,16,128]{2,1,0:T(8,128)S(1)}, f32[24,16,128]{2,1,0:T(8,128)S(1)}, u32[]{:S(2)}, u32[]{:S(2)}) collective-permute-start(f32[24,16,128]{2,1,0:T(8,128)S(1)} %get-tuple-element.71), channel_id=1, source_target_pairs={{0,8},{1,9},{2,10},{3,11},{4,12},{5,13},{6,14},{7,15},{8,0},{9,1},... | collective-permute-start | bytes 589832 | tf_op jit(solution)/shard_map/ppermute | solution.py:391
  35.2 0.5 collective-permute-start.10
  35.7 2.2 %collective-permute-start.11 = (f32[24,16,128]{2,1,0:T(8,128)S(1)}, f32[24,16,128]{2,1,0:T(8,128)S(1)}, u32[]{:S(2)}, u32[]{:S(2)}) collective-permute-start(f32[24,16,128]{2,1,0:T(8,128)S(1)} %get-tuple-element.74), channel_id=1, source_target_pairs={{0,8},{1,2},{2,1},{3,4},{4,3},{5,6},{6,5},{7,15},{8,0},{9,10},{10,... | collective-permute-start | bytes 589832 | tf_op jit(solution)/shard_map/ppermute | solution.py:391
  37.9 7.6 %local3.1 = (f32[64,16,128]{2,1,0:T(8,128)S(1)}, f32[64,16,128]{2,1,0:T(8,128)S(1)}) custom-call(s32[4,64]{1,0:T(4,128)S(4)} %get-tuple-element.46.cols, bf16[64,32,128]{2,1,0:T(8,128)(2,1)S(1)} %get-tuple-element.68.v2, bf16[64,4,128,128]{3,2,1,0:T(8,128)(2,1)S(1)} %get-tuple-element.59.th, bf16[64,4,128,128]{3,2,1,0:T(8,128)(2,1)S(1)} %get-tuple-element.60.tl), custom_call_target="tpu_custom_call" | custom-call | flops 1073741824 | bytes 16777216 | tf_op jit(solution)/shard_map/local3/pallas_call | solution.py:453
  45.6 2.8 %finish3.1 = (f32[64,16,128]{2,1,0:T(8,128)S(1)}, bf16[64,32,128]{2,1,0:T(8,128)(2,1)S(1)}, f32[24,16,128]{2,1,0:T(8,128)S(1)}, f32[24,16,128]{2,1,0:T(8,128)S(1)}, f32[16,16]{1,0:T(8,128)S(1)}) custom-call(s32[4,24]{1,0:T(4,128)S(4)} %get-tuple-element.42.rows, s32[6]{0:T(128)S(4)} %get-tuple-element.43.flags, f32[2]{0:T(128)S(4)} %get-tuple-element.44.bounds, ...), custom_call_target="tpu_custom_call" | custom-call | tf_op jit(solution)/shard_map/finish3/pallas_call | solution.py:445
  48.3 1.4 %collective-permute-start.12 = (f32[24,16,128]{2,1,0:T(8,128)S(1)}, f32[24,16,128]{2,1,0:T(8,128)S(1)}, u32[]{:S(2)}, u32[]{:S(2)}) collective-permute-start(f32[24,16,128]{2,1,0:T(8,128)S(1)} %get-tuple-element.76), channel_id=1, source_target_pairs={{0,24},{8,0},{16,8},{24,16},{1,25},{9,1},{17,9},{25,17},{2,26},{10... | collective-permute-start | bytes 589832 | tf_op jit(solution)/shard_map/ppermute | solution.py:376
  49.7 1.8 %collective-permute-start.13 = (f32[24,16,128]{2,1,0:T(8,128)S(1)}, f32[24,16,128]{2,1,0:T(8,128)S(1)}, u32[]{:S(2)}, u32[]{:S(2)}) collective-permute-start(f32[24,16,128]{2,1,0:T(8,128)S(1)} %get-tuple-element.77), channel_id=1, source_target_pairs={{0,7},{1,0},{2,1},{3,2},{4,3},{5,4},{6,5},{7,6},{8,15},{9,8},{10,9... | collective-permute-start | bytes 589832 | tf_op jit(solution)/shard_map/ppermute | solution.py:376
  51.5 2.8 %project.1.part = f32[16,16]{1,0:T(8,128)S(1)} custom-call(s32[4,64]{1,0:T(4,128)S(4)} %get-tuple-element.46.cols, f32[64,16,128]{2,1,0:T(8,128)S(1)} %get-tuple-element.78.v, bf16[64,32,128]{2,1,0:T(8,128)(2,1)S(1)} %get-tuple-element.75.v2, f32[64,128]{1,0:T(8,128)S(1)} %bitcast.12, bf16[64,4,128,128]{3,2,1,0:T(8,128)(2,1)S(1)} %get-tuple-element.59.th), custom_call_target="tpu_custom_call" | custom-call | flops 268435456 | bytes 8388608 | tf_op jit(solution)/shard_map/project/pallas_call | solution.py:459
  54.4 0.2 collective-permute-done.12.ux
  54.6 0.1 collective-permute-done.13.uy
  54.7 1.9 %project_faces.1 = f32[32,8,128]{2,1,0:T(8,128)S(1)} custom-call(s32[4,24]{1,0:T(4,128)S(4)} %get-tuple-element.42.rows, s32[6]{0:T(128)S(4)} %get-tuple-element.43.flags, bf16[64,32,128]{2,1,0:T(8,128)(2,1)S(1)} %get-tuple-element.75.v2, f32[24,16,128]{2,1,0:T(8,128)S(1)} %collective-permute-done.12.ux, f32[24,16,128]{2,1,0:T(8,128)S(1)} %collective-permute-done.13.uy, ...), custom_call_target="tpu_custom_call" | custom-call | tf_op jit(solution)/shard_map/project_faces/pallas_call | solution.py:464
  56.6 13.9 %all_to_all.5.sums = f32[32,8,128]{2,1,0:T(8,128)S(1)} all-to-all(f32[32,8,128]{2,1,0:T(8,128)S(1)} %project_faces.1), channel_id=1, replica_groups=mesh['gx'=4,'gy'=8] {'gx','gy'}, dimensions={0} | all-to-all | bytes 262144 | tf_op jit(solution)/shard_map/all_to_all | solution.py:467
  70.5 3.1 %end.1 = (f32[64,16,128]{2,1,0:T(8,128)}, f32[16,16]{1,0:T(8,128)}) custom-call(f32[32,8,128]{2,1,0:T(8,128)S(1)} %all_to_all.5.sums, bf16[64,32,128]{2,1,0:T(8,128)(2,1)S(1)} %get-tuple-element.75.v2), custom_call_target="tpu_custom_call" | custom-call | tf_op jit(solution)/shard_map/end/pallas_call | solution.py:468
  (17 shorter events, 0.0 us)
Async XLA Ops:
  4.1 14.0 %collective-permute-start = (f32[24,16,128]{2,1,0:T(8,128)S(1)}, f32[24,16,128]{2,1,0:T(8,128)S(1)}, u32[]{:S(2)}, u32[]{:S(2)}) collective-permute-start(f32[24,16,128]{2,1,0:T(8,128)S(1)} %get-tuple-element.51), channel_id=1, source_target_pairs={{0,8},{1,9},{2,10},{3,11},{4,12},{5,13},{6,14},{7,15},{8,0},{9,1},... | collective-permute-start | bytes 589832 | tf_op jit(solution)/shard_map/ppermute | solution.py:391
  7.2 11.0 %collective-permute-start.1 = (f32[24,16,128]{2,1,0:T(8,128)S(1)}, f32[24,16,128]{2,1,0:T(8,128)S(1)}, u32[]{:S(2)}, u32[]{:S(2)}) collective-permute-start(f32[24,16,128]{2,1,0:T(8,128)S(1)} %get-tuple-element.52), channel_id=1, source_target_pairs={{0,1},{1,0},{2,3},{3,2},{4,5},{5,4},{6,7},{7,6},{8,16},{9,17},{10,... | collective-permute-start | bytes 589832 | tf_op jit(solution)/shard_map/ppermute | solution.py:391
  7.2 11.0 %collective-permute-start.2 = (f32[24,16,128]{2,1,0:T(8,128)S(1)}, f32[24,16,128]{2,1,0:T(8,128)S(1)}, u32[]{:S(2)}, u32[]{:S(2)}) collective-permute-start(f32[24,16,128]{2,1,0:T(8,128)S(1)} %get-tuple-element.53), channel_id=1, source_target_pairs={{0,1},{1,0},{2,3},{3,2},{4,5},{5,4},{6,7},{7,6},{8,9},{9,8},{10,11... | collective-permute-start | bytes 589832 | tf_op jit(solution)/shard_map/ppermute | solution.py:391
  7.7 10.5 %collective-permute-start.3 = (f32[24,16,128]{2,1,0:T(8,128)S(1)}, f32[24,16,128]{2,1,0:T(8,128)S(1)}, u32[]{:S(2)}, u32[]{:S(2)}) collective-permute-start(f32[24,16,128]{2,1,0:T(8,128)S(1)} %get-tuple-element.54), channel_id=1, source_target_pairs={{0,8},{1,2},{2,1},{3,4},{4,3},{5,6},{6,5},{7,15},{8,0},{9,10},{10,... | collective-permute-start | bytes 589832 | tf_op jit(solution)/shard_map/ppermute | solution.py:391
  10.3 7.8 %copy-start = (f32[1,1,64,128]{3,2,1,0:T(8,128)S(1)}, f32[1,1,64,128]{3,2,1,0:T(8,128)}, u32[]{:S(2)}) copy-start(f32[1,1,64,128]{3,2,1,0:T(8,128)} %param.10) | copy-start | bytes 98308
  21.1 9.7 %collective-permute-start.4 = (f32[24,16,128]{2,1,0:T(8,128)S(1)}, f32[24,16,128]{2,1,0:T(8,128)S(1)}, u32[]{:S(2)}, u32[]{:S(2)}) collective-permute-start(f32[24,16,128]{2,1,0:T(8,128)S(1)} %get-tuple-element.63), channel_id=1, source_target_pairs={{0,8},{1,9},{2,10},{3,11},{4,12},{5,13},{6,14},{7,15},{8,0},{9,1},... | collective-permute-start | bytes 589832 | tf_op jit(solution)/shard_map/ppermute | solution.py:391
  21.2 9.7 %collective-permute-start.5 = (f32[24,16,128]{2,1,0:T(8,128)S(1)}, f32[24,16,128]{2,1,0:T(8,128)S(1)}, u32[]{:S(2)}, u32[]{:S(2)}) collective-permute-start(f32[24,16,128]{2,1,0:T(8,128)S(1)} %get-tuple-element.64), channel_id=1, source_target_pairs={{0,1},{1,0},{2,3},{3,2},{4,5},{5,4},{6,7},{7,6},{8,16},{9,17},{10,... | collective-permute-start | bytes 589832 | tf_op jit(solution)/shard_map/ppermute | solution.py:391
  22.5 8.3 %collective-permute-start.6 = (f32[24,16,128]{2,1,0:T(8,128)S(1)}, f32[24,16,128]{2,1,0:T(8,128)S(1)}, u32[]{:S(2)}, u32[]{:S(2)}) collective-permute-start(f32[24,16,128]{2,1,0:T(8,128)S(1)} %get-tuple-element.65), channel_id=1, source_target_pairs={{0,1},{1,0},{2,3},{3,2},{4,5},{5,4},{6,7},{7,6},{8,9},{9,8},{10,11... | collective-permute-start | bytes 589832 | tf_op jit(solution)/shard_map/ppermute | solution.py:391
  22.5 8.4 %collective-permute-start.7 = (f32[24,16,128]{2,1,0:T(8,128)S(1)}, f32[24,16,128]{2,1,0:T(8,128)S(1)}, u32[]{:S(2)}, u32[]{:S(2)}) collective-permute-start(f32[24,16,128]{2,1,0:T(8,128)S(1)} %get-tuple-element.66), channel_id=1, source_target_pairs={{0,8},{1,2},{2,1},{3,4},{4,3},{5,6},{6,5},{7,15},{8,0},{9,10},{10,... | collective-permute-start | bytes 589832 | tf_op jit(solution)/shard_map/ppermute | solution.py:391
  33.8 11.7 %collective-permute-start.8 = (f32[24,16,128]{2,1,0:T(8,128)S(1)}, f32[24,16,128]{2,1,0:T(8,128)S(1)}, u32[]{:S(2)}, u32[]{:S(2)}) collective-permute-start(f32[24,16,128]{2,1,0:T(8,128)S(1)} %get-tuple-element.71), channel_id=1, source_target_pairs={{0,8},{1,9},{2,10},{3,11},{4,12},{5,13},{6,14},{7,15},{8,0},{9,1},... | collective-permute-start | bytes 589832 | tf_op jit(solution)/shard_map/ppermute | solution.py:391
  35.2 10.4 %collective-permute-start.9 = (f32[24,16,128]{2,1,0:T(8,128)S(1)}, f32[24,16,128]{2,1,0:T(8,128)S(1)}, u32[]{:S(2)}, u32[]{:S(2)}) collective-permute-start(f32[24,16,128]{2,1,0:T(8,128)S(1)} %get-tuple-element.72), channel_id=1, source_target_pairs={{0,1},{1,0},{2,3},{3,2},{4,5},{5,4},{6,7},{7,6},{8,16},{9,17},{10,... | collective-permute-start | bytes 589832 | tf_op jit(solution)/shard_map/ppermute | solution.py:391
  35.2 10.4 %collective-permute-start.10 = (f32[24,16,128]{2,1,0:T(8,128)S(1)}, f32[24,16,128]{2,1,0:T(8,128)S(1)}, u32[]{:S(2)}, u32[]{:S(2)}) collective-permute-start(f32[24,16,128]{2,1,0:T(8,128)S(1)} %get-tuple-element.73), channel_id=1, source_target_pairs={{0,1},{1,0},{2,3},{3,2},{4,5},{5,4},{6,7},{7,6},{8,9},{9,8},{10,11... | collective-permute-start | bytes 589832 | tf_op jit(solution)/shard_map/ppermute | solution.py:391
  35.7 9.9 %collective-permute-start.11 = (f32[24,16,128]{2,1,0:T(8,128)S(1)}, f32[24,16,128]{2,1,0:T(8,128)S(1)}, u32[]{:S(2)}, u32[]{:S(2)}) collective-permute-start(f32[24,16,128]{2,1,0:T(8,128)S(1)} %get-tuple-element.74), channel_id=1, source_target_pairs={{0,8},{1,2},{2,1},{3,4},{4,3},{5,6},{6,5},{7,15},{8,0},{9,10},{10,... | collective-permute-start | bytes 589832 | tf_op jit(solution)/shard_map/ppermute | solution.py:391
  48.3 6.3 %collective-permute-start.12 = (f32[24,16,128]{2,1,0:T(8,128)S(1)}, f32[24,16,128]{2,1,0:T(8,128)S(1)}, u32[]{:S(2)}, u32[]{:S(2)}) collective-permute-start(f32[24,16,128]{2,1,0:T(8,128)S(1)} %get-tuple-element.76), channel_id=1, source_target_pairs={{0,24},{8,0},{16,8},{24,16},{1,25},{9,1},{17,9},{25,17},{2,26},{10... | collective-permute-start | bytes 589832 | tf_op jit(solution)/shard_map/ppermute | solution.py:376
  49.7 5.0 %collective-permute-start.13 = (f32[24,16,128]{2,1,0:T(8,128)S(1)}, f32[24,16,128]{2,1,0:T(8,128)S(1)}, u32[]{:S(2)}, u32[]{:S(2)}) collective-permute-start(f32[24,16,128]{2,1,0:T(8,128)S(1)} %get-tuple-element.77), channel_id=1, source_target_pairs={{0,7},{1,0},{2,1},{3,2},{4,3},{5,4},{6,5},{7,6},{8,15},{9,8},{10,9... | collective-permute-start | bytes 589832 | tf_op jit(solution)/shard_map/ppermute | solution.py:376

commit v4 on v3

--- a/solution.py
+++ b/solution.py
@@ -9,6 +9,7 @@
 
 F32 = jnp.float32
 BF16 = jnp.bfloat16
+F8 = jnp.float8_e4m3fn
 MIB = 1 << 20
 VM = pl.BlockSpec(memory_space=pltpu.VMEM)
 SM = pl.BlockSpec(memory_space=pltpu.SMEM)
@@ -17,7 +18,11 @@
 
 ROWS = 8
 FACES = 24
+WIDE = 32
+CHUNK = 8
 EARLY = 16
+TILE_SCALE = 2.0**19
+VEC_SCALE = 256.0
 SHRINK = 1.0 / 64.0
 
 
@@ -25,6 +30,35 @@
     high = x.astype(BF16)
     low = (x - high.astype(F32)).astype(BF16)
     return high, low
+
+
+def low_tile(t, high):
+    return ((t - high.astype(F32)) * TILE_SCALE).astype(F8)
+
+
+def stacked8(x):
+    high = x.astype(F8)
+    low = (x - high.astype(F32)).astype(F8)
+    return cat([high, low], axis=-2)
+
+
+def vector_scales(peak):
+    top = jnp.maximum(jnp.max(peak, axis=1, keepdims=True), 1e-30)
+    top = jnp.broadcast_to(top, peak.shape)
+    return VEC_SCALE / top, top * (1.0 / (VEC_SCALE * TILE_SCALE))
+
+
+def shrunk(v, v8, peak, undo):
+    up, down = vector_scales(peak)
+    undo[...] = down
+    group = 8
+
+    def step(s, carry):
+        part = pl.ds(s * group, group)
+        v8[part] = stacked8(v[part] * up)
+        return carry
+
+    lax.fori_loop(0, v.shape[0] // group, step, 0)
 
 
 def stacked(x):
@@ -71,12 +105,12 @@
 
 
 def begin_kernel(rows_in, cols_in, bounds_in, block, tiles, stored, *refs):
-    (rows, cols, bounds, flags, ch, cl, v, v2, a, b, c, d, early, stage, sems) = refs
+    (rows, cols, bounds, flags, ch, cl, v, v2, v8, undo, a, b, c, d, early, stage, sems) = refs
     faces = rows.shape[1]
-    chunks = faces // ROWS
+    chunks = faces // CHUNK
 
     def fetch(s, axis):
-        part = pl.ds(s * ROWS, ROWS)
+        part = pl.ds(s * CHUNK, CHUNK)
         at = sems.at[2 * s + axis]
         return pltpu.make_async_copy(tiles.at[axis, part], stage.at[axis, part], at)
 
@@ -98,13 +132,14 @@
     for copy in small:
         copy.wait()
     v2[...] = stacked(v[...])
+    shrunk(v, v8, jnp.max(jnp.abs(v[...]), axis=0), undo)
 
     def step(s, carry):
         outs = []
         for axis in range(2):
             fetch(s, axis).wait()
-            for r in range(ROWS):
-                j = s * ROWS + r
+            for r in range(CHUNK):
+                j = s * CHUNK + r
                 high, low = split(stage[axis, j])
                 ch[axis, j] = high
                 cl[axis, j] = low
@@ -125,14 +160,18 @@
     sends[2 * axis + 1][j] = jnp.where(odd, product, minus)
 
 
-def local_rows(rows, cols, v2, highs, lows, wf, wb):
+def local_rows(rows, cols, v2, v8, undo, highs, lows, wf, wb):
+    down = undo[...]
+    wide = cat([down] * 4, axis=1)
     outs = []
     for i, high, low in zip(rows, highs, lows):
-        x2 = v2[i]
-        g2 = cat([v2[cols[k, i]] for k in range(4)], axis=1)
+        at = [cols[k, i] for k in range(4)]
         high = cat(high, axis=1)
         low = cat(low, axis=1)
-        outs.append((two_piece(dot_nt, g2, high, low), two_piece(dot_nn, x2, high, low)))
+        forward = fold(dot_nt(cat([v2[c] for c in at], axis=1), high))
+        forward = forward + down * fold(dot_nt(cat([v8[c] for c in at], axis=1), low))
+        backward = fold(dot_nn(v2[i], high)) + wide * fold(dot_nn(v8[i], low))
+        outs.append((forward, backward))
     for i, (forward, backward) in zip(rows, outs):
         wf[i] = forward
         for k in range(4):
@@ -140,7 +179,7 @@
             wb[at] = wb[at] + backward[:, k * 128 : (k + 1) * 128]
 
 
-def first_kernel(cols, v2, early, tiles, wf, wb, th, tl, stage, sems):
+def first_kernel(cols, v2, v8, undo, early, tiles, wf, wb, th, tl, stage, sems):
     copies = stage.shape[0] // ROWS
 
     def fetch(c):
@@ -157,14 +196,18 @@
         rows, highs, lows = [], [], []
         for r in range(ROWS):
             i = start + c * ROWS + r
-            pieces = [split(source[c * ROWS + r, k]) for k in range(4)]
+            pieces = []
+            for k in range(4):
+                t = source[c * ROWS + r, k]
+                high = t.astype(BF16)
+                pieces.append((high, low_tile(t, high)))
             for k in range(4):
                 th[i, k] = pieces[k][0]
                 tl[i, k] = pieces[k][1]
             rows.append(i)
             highs.append([p[0] for p in pieces])
             lows.append([p[1] for p in pieces])
-        local_rows(rows, cols, v2, highs, lows, wf, wb)
+        local_rows(rows, cols, v2, v8, undo, highs, lows, wf, wb)
 
     def step_early(c, carry):
         work(early, 0, c)
@@ -179,17 +222,17 @@
     lax.fori_loop(0, copies, step, 0)
 
 
-def local_kernel(cols, v2, th, tl, wf, wb):
+def local_kernel(cols, v2, v8, undo, th, tl, wf, wb):
     wb[...] = jnp.zeros_like(wb)
 
     def step(c, carry):
-        rows = [c * ROWS + r for r in range(ROWS)]
+        rows = [c * WIDE + r for r in range(WIDE)]
         highs = [[th[i, k] for k in range(4)] for i in rows]
         lows = [[tl[i, k] for k in range(4)] for i in rows]
-        local_rows(rows, cols, v2, highs, lows, wf, wb)
-        return carry
-
-    lax.fori_loop(0, v2.shape[0] // ROWS, step, 0)
+        local_rows(rows, cols, v2, v8, undo, highs, lows, wf, wb)
+        return carry
+
+    lax.fori_loop(0, v2.shape[0] // WIDE, step, 0)
 
 
 def arrive(rows, flags, received, ch, cl, acc):
@@ -219,7 +262,10 @@
         older = None
     else:
         (v, older, wf, wb, diag, ux, lx, uy, ly, ch, cl, *outs, acc) = refs
-    new, new2, *sends = outs
+    if order < 3:
+        new, new2, new8, undo, *sends = outs
+    else:
+        new, new2, *sends = outs
     acc[...] = jnp.zeros_like(acc)
     arrive(rows, flags, (ux, lx, uy, ly), ch, cl, acc)
     lower = jnp.full((16, 128), bounds[0], F32)
@@ -238,10 +284,11 @@
             y = y - older[part]
         new[part] = y
         new2[part] = stacked(y)
-        return carry
-
-    lax.fori_loop(0, v.shape[0] // group, step, 0)
+        return jnp.maximum(carry, jnp.max(jnp.abs(y), axis=0))
+
+    peak = lax.fori_loop(0, v.shape[0] // group, step, jnp.zeros((16, 128), F32))
     if order < 3:
+        shrunk(new, new8, peak, undo)
         leave(new, new2, rows, flags, ch, cl, sends)
         return
     mx, my, gram = sends
@@ -287,8 +334,8 @@
 
     def step(c, carry):
         outs = []
-        for r in range(ROWS):
-            i = c * ROWS + r
+        for r in range(WIDE):
+            i = c * WIDE + r
             outs.append((i, fold(dot_nn(v2[i], cat([th[i, k] for k in range(4)], axis=1)))))
         for i, backward in outs:
             for k in range(4):
@@ -296,7 +343,7 @@
                 wb[at] = wb[at] + backward[:, k * 128 : (k + 1) * 128]
         return carry
 
-    lax.fori_loop(0, v.shape[0] // ROWS, step, 0)
+    lax.fori_loop(0, v.shape[0] // WIDE, step, 0)
     total = jnp.zeros((32, 32), F32)
     for s in range(0, v.shape[0], 16):
         a2 = cat([v2[s + r] for r in range(16)], axis=1)
@@ -308,9 +355,9 @@
 def project_faces_kernel(rows, flags, v2, ux, uy, ch, part, gram, out):
     total = jnp.zeros((32, 32), F32)
     for axis, upper in ((0, ux), (1, uy)):
-        for s in range(0, rows.shape[1], ROWS):
+        for s in range(0, rows.shape[1], CHUNK):
             lefts, rights = [], []
-            for r in range(ROWS):
+            for r in range(CHUNK):
                 j = s + r
                 u2 = stacked(jnp.where(flags[2 * axis] > 0, upper[j], 0.0))
                 rights.append(stacked(fold(dot_nt(u2, ch[axis, j])) * SHRINK))
@@ -358,7 +405,7 @@
     return pltpu.VMEM(shape, dtype)
 
 
-def call(kernel, name, specs, outs, scratch=(), limit=6, flops=0, nbytes=0, smem=0):
+def call(kernel, name, specs, outs, scratch=(), limit=12, flops=0, nbytes=0, smem=0):
     return pl.pallas_call(
         kernel,
         name=name,
@@ -405,23 +452,25 @@
     nodes = float(count * tile * peers)
     vec = in_vmem((count, width, tile), F32)
     vec2 = in_vmem((count, 2 * width, tile), BF16)
+    vec8 = in_vmem((count, 2 * width, tile), F8)
+    scale = in_vmem((width, tile), F32)
     face = jax.ShapeDtypeStruct((faces, width, tile), F32)
-    tile2 = in_vmem(stored.shape, BF16)
+    high, low = in_vmem(stored.shape, BF16), in_vmem(stored.shape, F8)
     face2 = in_vmem(coupling.shape, BF16)
     square = in_vmem((width, width), F32)
     small = jax.ShapeDtypeStruct((peers, 8, 128), F32)
     local_flops = 16 * stored.size * width
 
-    rows, cols, filter_bounds, flags, ch, cl, block, x2, *sends, early = call(
+    rows, cols, filter_bounds, flags, ch, cl, block, x2, x8, undo, *sends, early = call(
         begin_kernel, "begin", [HBM] * 6,
         [
             pltpu.SMEM(rows.shape, jnp.int32), pltpu.SMEM(cols.shape, jnp.int32),
             pltpu.SMEM((2,), F32), pltpu.SMEM((6,), jnp.int32),
-            face2, face2, vec, vec2, face, face, face, face,
+            face2, face2, vec, vec2, vec8, scale, face, face, face, face,
             in_vmem((EARLY,) + stored.shape[1:], F32),
         ],
-        [pltpu.VMEM(coupling.shape, F32), pltpu.SemaphoreType.DMA((2 * (faces // ROWS) + 6,))],
-        limit=6, flops=local_flops // 2, nbytes=4 * stored.size // 2, smem=4,
+        [pltpu.VMEM(coupling.shape, F32), pltpu.SemaphoreType.DMA((2 * (faces // CHUNK) + 6,))],
+        limit=8, flops=local_flops // 2, nbytes=4 * stored.size // 2, smem=4,
     )(*(in_hbm(x) for x in (rows, cols, filter_bounds, block, coupling, stored)))
 
     def exchange(sends):
@@ -429,19 +478,19 @@
 
     received = exchange(sends)
     wf, wb, th, tl = call(
-        first_kernel, "local_first", [SM, VM, VM, HBM], [vec, vec, tile2, tile2],
+        first_kernel, "local_first", [SM] + [VM] * 4 + [HBM], [vec, vec, high, low],
         [
             pltpu.VMEM((count - EARLY,) + stored.shape[1:], F32),
             pltpu.SemaphoreType.DMA(((count - EARLY) // ROWS,)),
         ],
-        limit=18, flops=local_flops, nbytes=4 * stored.size,
-    )(cols, x2, early, in_hbm(stored))
+        limit=24, flops=local_flops, nbytes=4 * stored.size,
+    )(cols, x2, x8, undo, early, in_hbm(stored))
 
     x, older = block, None
     for order in (1, 2, 3):
         carried = (x,) if older is None else (x, older)
         last = order == 3
-        outs = [vec, vec2] + ([face, face, square] if last else [face] * 4)
+        outs = [vec, vec2] + ([face, face, square] if last else [vec8, scale] + [face] * 4)
         new, new2, *sends = call(
             functools.partial(next_kernel, order), "finish%d" % order,
             [SM, SM, SM] + [VM] * (9 + len(carried)), outs,
@@ -449,11 +498,12 @@
         )(rows, flags, filter_bounds, *carried, wf, wb, diag, *received, ch, cl)
         x, x2, older = new, new2, x
         if not last:
+            x8, undo, *sends = sends
             received = exchange(sends)
             wf, wb = call(
-                local_kernel, "local%d" % (order + 1), [SM] + [VM] * 3, [vec, vec],
+                local_kernel, "local%d" % (order + 1), [SM] + [VM] * 5, [vec, vec],
                 flops=local_flops, nbytes=4 * stored.size,
-            )(cols, x2, th, tl)
+            )(cols, x2, x8, undo, th, tl)
     mx, my, gram = sends
     ux, uy = ring(mx, "gx", -1), ring(my, "gy", -1)
     (part,) = call(

time: 73.8 us -> 70.6 us (0.957)
  Pallas kernels: 42.9 us -> 38.9 us
  waiting for transfers between devices: 0.38 us -> 2.08 us
    pallas_call x3, Pallas kernels: 23 us -> 19.1 us  [the longest x2 12.1 us: shards(): call(local_kernel, 'local%d' % (order + 1), [SM] + [VM] * 5, [vec, vec],...]
    ppermute x2, waiting for transfers between devices: 0.35 us -> 1.29 us  [ring(): return lax.ppermute(x, axis, [(i, (i + by) % peers) for i in range(peers)])]
    ppermute x12, waiting for transfers between devices: 0.03 us -> 0.79 us  [pairs(): return lax.ppermute(x, ('gx', 'gy'), moves)]
    ppermute x12, starting transfers between devices: 12.5 us -> 11.7 us  [pairs(): return lax.ppermute(x, ('gx', 'gy'), moves)]
  transfers between devices with their start and end apart: 14 -> 14, of which waited for: 2 -> 2; matrix products, arithmetic and copies ran while one was open for 0% -> 0% of each run, Pallas kernels for 35% -> 30%
where the time goes in v4:
time: 70.6 us; the launch traced here: 70.4 us
  Pallas kernels  38.9 us (55%)
  starting transfers between devices  14.9 us (21%)
  blocking collectives  13.7 us (19%)
  waiting for transfers between devices  2.08 us (3%)
  between operations  0.79 us (1%)
    all_to_all x1, blocking collectives, shards(): sums = lax.all_to_all(sums, ('gx', 'gy'), 0, 0)  13.7 us
    pallas_call x2, Pallas kernels, shards(): call(local_kernel, 'local%d' % (order + 1), [SM] + [VM] * 5, [vec, vec],...  12.1 us
    ppermute x12, starting transfers between devices, pairs(): return lax.ppermute(x, ('gx', 'gy'), moves)  11.7 us
    pallas_call x3, Pallas kernels, shards(): call(functools.partial(next_kernel, order), 'finish%d' % order, [SM, SM,...  9.3 us
    pallas_call x1, Pallas kernels, shards(): call(first_kernel, 'local_first', [SM] + [VM] * 4 + [HBM], [vec, vec, hig...  7 us
    pallas_call x1, Pallas kernels, shards(): call(begin_kernel, 'begin', [HBM] * 6, [pltpu.SMEM(rows.shape, jnp.int32)...  3.44 us
    ppermute x2, starting transfers between devices, ring(): return lax.ppermute(x, axis, [(i, (i + by) % peers) for i in range(peers)])  3.18 us
    pallas_call x1, Pallas kernels, shards(): call(functools.partial(end_kernel, nodes), 'end', [VM, VM], [jax.ShapeDty...  3.11 us
  transfers between devices with their start and end apart: 14, of which 2 were waited for; matrix products, arithmetic and copies ran while one was open for 0% of the time, Pallas kernels for 30%

profile of v4, /device:TPU:0, one launch (start us, length us, event | category | flops | bytes accessed | tf_op | source)
XLA Modules:
  0.0 70.4 jit_solution(5331070852790888924)
XLA Ops:
  0.6 3.4 %begin.1 = (s32[4,24]{1,0:T(4,128)S(4)}, s32[4,64]{1,0:T(4,128)S(4)}, f32[2]{0:T(128)S(4)}, s32[6]{0:T(128)S(4)}, bf16[2,24,128,128]{3,2,1,0:T(8,128)(2,1)S(1)},...) custom-call(s32[4,24]{1,0:T(4,128)} %bitcast.17, ...), custom_call_target="tpu_custom_call" | custom-call | flops 536870912 | bytes 8388608 | tf_op jit(solution)/shard_map/begin/pallas_call | solution.py:464
  4.1 3.1 %collective-permute-start = (f32[24,16,128]{2,1,0:T(8,128)S(1)}, f32[24,16,128]{2,1,0:T(8,128)S(1)}, u32[]{:S(2)}, u32[]{:S(2)}) collective-permute-start(f32[24,16,128]{2,1,0:T(8,128)S(1)} %get-tuple-element.59), channel_id=1, source_target_pairs={{0,8},{1,9},{2,10},{3,11},{4,12},{5,13},{6,14},{7,15},{8,0},{9,1},... | collective-permute-start | bytes 589832 | tf_op jit(solution)/shard_map/ppermute | solution.py:438
  7.2 0.5 collective-permute-start.2
  7.7 2.6 %collective-permute-start.3 = (f32[24,16,128]{2,1,0:T(8,128)S(1)}, f32[24,16,128]{2,1,0:T(8,128)S(1)}, u32[]{:S(2)}, u32[]{:S(2)}) collective-permute-start(f32[24,16,128]{2,1,0:T(8,128)S(1)} %get-tuple-element.62), channel_id=1, source_target_pairs={{0,8},{1,2},{2,1},{3,4},{4,3},{5,6},{6,5},{7,15},{8,0},{9,10},{10,... | collective-permute-start | bytes 589832 | tf_op jit(solution)/shard_map/ppermute | solution.py:438
  10.3 7.0 %local_first.1 = (f32[64,16,128]{2,1,0:T(8,128)S(1)}, f32[64,16,128]{2,1,0:T(8,128)S(1)}, bf16[64,4,128,128]{3,2,1,0:T(8,128)(2,1)S(1)}, f8e4m3fn[64,4,128,128]{3,2,1,0:T(32,128)(4,1)S(1)}) custom-call(s32[4,64]{1,0:T(4,128)S(4)} %get-tuple-element.52.cols, bf16[64,32,128]{2,1,0:T(8,128)(2,1)S(1)} %get-tuple-element.53.v2, ...), custom_call_target="tpu_custom_call" | custom-call | flops 1073741824 | bytes 16777216 | tf_op jit(solution)/shard_map/local_first/pallas_call | solution.py:480
  17.4 3.2 %finish1.1 = (f32[64,16,128]{2,1,0:T(8,128)S(1)}, bf16[64,32,128]{2,1,0:T(8,128)(2,1)S(1)}, f8e4m3fn[64,32,128]{2,1,0:T(32,128)(4,1)S(1)}, f32[16,128]{1,0:T(8,1...) custom-call(s32[4,24]{1,0:T(4,128)S(4)} %get-tuple-element.48.rows, ...), custom_call_target="tpu_custom_call" | custom-call | tf_op jit(solution)/shard_map/finish1/pallas_call | solution.py:494
  20.6 0.1 collective-permute-start.4
  20.7 1.3 %collective-permute-start.5 = (f32[24,16,128]{2,1,0:T(8,128)S(1)}, f32[24,16,128]{2,1,0:T(8,128)S(1)}, u32[]{:S(2)}, u32[]{:S(2)}) collective-permute-start(f32[24,16,128]{2,1,0:T(8,128)S(1)} %get-tuple-element.74), channel_id=1, source_target_pairs={{0,1},{1,0},{2,3},{3,2},{4,5},{5,4},{6,7},{7,6},{8,16},{9,17},{10,... | collective-permute-start | bytes 589832 | tf_op jit(solution)/shard_map/ppermute | solution.py:438
  22.0 0.7 collective-permute-start.7
  22.7 5.9 %local2.1 = (f32[64,16,128]{2,1,0:T(8,128)S(1)}, f32[64,16,128]{2,1,0:T(8,128)S(1)}) custom-call(s32[4,64]{1,0:T(4,128)S(4)} %get-tuple-element.52.cols, bf16[64,32,128]{2,1,0:T(8,128)(2,1)S(1)} %get-tuple-element.66.v2, f8e4m3fn[64,32,128]{2,1,0:T(32,128)(4,1)S(1)} %get-tuple-element.67.v8, f32[16,128]{1,0:T(8,128)S(1)} %get-tuple-element.68.undo, ...), custom_call_target="tpu_custom_call" | custom-call | flops 1073741824 | bytes 16777216 | tf_op jit(solution)/shard_map/local2/pallas_call | solution.py:503
  28.7 0.8 %collective-permute-done.7.refs_8_ = f32[24,16,128]{2,1,0:T(8,128)S(1)} collective-permute-done((f32[24,16,128]{2,1,0:T(8,128)S(1)}, f32[24,16,128]{2,1,0:T(8,128)S(1)}, u32[]{:S(2)}, u32[]{:S(2)}) %collective-permute-start.7) | collective-permute-done | bytes 196640 | tf_op jit(solution)/shard_map/ppermute | solution.py:438
  29.5 3.3 %finish2.1 = (f32[64,16,128]{2,1,0:T(8,128)S(1)}, bf16[64,32,128]{2,1,0:T(8,128)(2,1)S(1)}, f8e4m3fn[64,32,128]{2,1,0:T(32,128)(4,1)S(1)}, f32[16,128]{1,0:T(8,1...) custom-call(s32[4,24]{1,0:T(4,128)S(4)} %get-tuple-element.48.rows, ...), custom_call_target="tpu_custom_call" | custom-call | tf_op jit(solution)/shard_map/finish2/pallas_call | solution.py:494
  32.7 1.2 %collective-permute-start.8 = (f32[24,16,128]{2,1,0:T(8,128)S(1)}, f32[24,16,128]{2,1,0:T(8,128)S(1)}, u32[]{:S(2)}, u32[]{:S(2)}) collective-permute-start(f32[24,16,128]{2,1,0:T(8,128)S(1)} %get-tuple-element.83), channel_id=1, source_target_pairs={{0,8},{1,9},{2,10},{3,11},{4,12},{5,13},{6,14},{7,15},{8,0},{9,1},... | collective-permute-start | bytes 589832 | tf_op jit(solution)/shard_map/ppermute | solution.py:438
  33.9 0.5 collective-permute-start.10
  34.4 1.7 %collective-permute-start.11 = (f32[24,16,128]{2,1,0:T(8,128)S(1)}, f32[24,16,128]{2,1,0:T(8,128)S(1)}, u32[]{:S(2)}, u32[]{:S(2)}) collective-permute-start(f32[24,16,128]{2,1,0:T(8,128)S(1)} %get-tuple-element.86), channel_id=1, source_target_pairs={{0,8},{1,2},{2,1},{3,4},{4,3},{5,6},{6,5},{7,15},{8,0},{9,10},{10,... | collective-permute-start | bytes 589832 | tf_op jit(solution)/shard_map/ppermute | solution.py:438
  36.1 6.1 %local3.1 = (f32[64,16,128]{2,1,0:T(8,128)S(1)}, f32[64,16,128]{2,1,0:T(8,128)S(1)}) custom-call(s32[4,64]{1,0:T(4,128)S(4)} %get-tuple-element.52.cols, bf16[64,32,128]{2,1,0:T(8,128)(2,1)S(1)} %get-tuple-element.78.v2, f8e4m3fn[64,32,128]{2,1,0:T(32,128)(4,1)S(1)} %get-tuple-element.79.v8, f32[16,128]{1,0:T(8,128)S(1)} %get-tuple-element.80.undo, ...), custom_call_target="tpu_custom_call" | custom-call | flops 1073741824 | bytes 16777216 | tf_op jit(solution)/shard_map/local3/pallas_call | solution.py:503
  42.3 2.8 %finish3.1 = (f32[64,16,128]{2,1,0:T(8,128)S(1)}, bf16[64,32,128]{2,1,0:T(8,128)(2,1)S(1)}, f32[24,16,128]{2,1,0:T(8,128)S(1)}, f32[24,16,128]{2,1,0:T(8,128)S(1)}, f32[16,16]{1,0:T(8,128)S(1)}) custom-call(s32[4,24]{1,0:T(4,128)S(4)} %get-tuple-element.48.rows, s32[6]{0:T(128)S(4)} %get-tuple-element.49.flags, f32[2]{0:T(128)S(4)} %get-tuple-element.50.bounds, ...), custom_call_target="tpu_custom_call" | custom-call | tf_op jit(solution)/shard_map/finish3/pallas_call | solution.py:494
  45.1 1.8 %collective-permute-start.12 = (f32[24,16,128]{2,1,0:T(8,128)S(1)}, f32[24,16,128]{2,1,0:T(8,128)S(1)}, u32[]{:S(2)}, u32[]{:S(2)}) collective-permute-start(f32[24,16,128]{2,1,0:T(8,128)S(1)} %get-tuple-element.88), channel_id=1, source_target_pairs={{0,24},{8,0},{16,8},{24,16},{1,25},{9,1},{17,9},{25,17},{2,26},{10... | collective-permute-start | bytes 589832 | tf_op jit(solution)/shard_map/ppermute | solution.py:423
  46.9 1.4 %collective-permute-start.13 = (f32[24,16,128]{2,1,0:T(8,128)S(1)}, f32[24,16,128]{2,1,0:T(8,128)S(1)}, u32[]{:S(2)}, u32[]{:S(2)}) collective-permute-start(f32[24,16,128]{2,1,0:T(8,128)S(1)} %get-tuple-element.89), channel_id=1, source_target_pairs={{0,7},{1,0},{2,1},{3,2},{4,3},{5,4},{6,5},{7,6},{8,15},{9,8},{10,9... | collective-permute-start | bytes 589832 | tf_op jit(solution)/shard_map/ppermute | solution.py:423
  48.3 2.1 %project.1.part = f32[16,16]{1,0:T(8,128)S(1)} custom-call(s32[4,64]{1,0:T(4,128)S(4)} %get-tuple-element.52.cols, f32[64,16,128]{2,1,0:T(8,128)S(1)} %get-tuple-element.90.v, bf16[64,32,128]{2,1,0:T(8,128)(2,1)S(1)} %get-tuple-element.87.v2, f32[64,128]{1,0:T(8,128)S(1)} %bitcast.12, bf16[64,4,128,128]{3,2,1,0:T(8,128)(2,1)S(1)} %get-tuple-element.69.th), custom_call_target="tpu_custom_call" | custom-call | flops 268435456 | bytes 8388608 | tf_op jit(solution)/shard_map/project/pallas_call | solution.py:509
  50.4 1.3 %collective-permute-done.12.ux = f32[24,16,128]{2,1,0:T(8,128)S(1)} collective-permute-done((f32[24,16,128]{2,1,0:T(8,128)S(1)}, f32[24,16,128]{2,1,0:T(8,128)S(1)}, u32[]{:S(2)}, u32[]{:S(2)}) %collective-permute-start.12) | collective-permute-done | bytes 196640 | tf_op jit(solution)/shard_map/ppermute | solution.py:423
  51.7 1.9 %project_faces.1 = f32[32,8,128]{2,1,0:T(8,128)S(1)} custom-call(s32[4,24]{1,0:T(4,128)S(4)} %get-tuple-element.48.rows, s32[6]{0:T(128)S(4)} %get-tuple-element.49.flags, bf16[64,32,128]{2,1,0:T(8,128)(2,1)S(1)} %get-tuple-element.87.v2, f32[24,16,128]{2,1,0:T(8,128)S(1)} %collective-permute-done.12.ux, f32[24,16,128]{2,1,0:T(8,128)S(1)} %collective-permute-done.13.uy, ...), custom_call_target="tpu_custom_call" | custom-call | tf_op jit(solution)/shard_map/project_faces/pallas_call | solution.py:514
  53.6 13.7 %all_to_all.5.sums = f32[32,8,128]{2,1,0:T(8,128)S(1)} all-to-all(f32[32,8,128]{2,1,0:T(8,128)S(1)} %project_faces.1), channel_id=1, replica_groups=mesh['gx'=4,'gy'=8] {'gx','gy'}, dimensions={0} | all-to-all | bytes 262144 | tf_op jit(solution)/shard_map/all_to_all | solution.py:517
  67.3 3.1 %end.1 = (f32[64,16,128]{2,1,0:T(8,128)}, f32[16,16]{1,0:T(8,128)}) custom-call(f32[32,8,128]{2,1,0:T(8,128)S(1)} %all_to_all.5.sums, bf16[64,32,128]{2,1,0:T(8,128)(2,1)S(1)} %get-tuple-element.87.v2), custom_call_target="tpu_custom_call" | custom-call | tf_op jit(solution)/shard_map/end/pallas_call | solution.py:518
  (17 shorter events, 0.0 us)
Async XLA Ops:
  4.1 13.3 %collective-permute-start = (f32[24,16,128]{2,1,0:T(8,128)S(1)}, f32[24,16,128]{2,1,0:T(8,128)S(1)}, u32[]{:S(2)}, u32[]{:S(2)}) collective-permute-start(f32[24,16,128]{2,1,0:T(8,128)S(1)} %get-tuple-element.59), channel_id=1, source_target_pairs={{0,8},{1,9},{2,10},{3,11},{4,12},{5,13},{6,14},{7,15},{8,0},{9,1},... | collective-permute-start | bytes 589832 | tf_op jit(solution)/shard_map/ppermute | solution.py:438
  7.2 10.2 %collective-permute-start.1 = (f32[24,16,128]{2,1,0:T(8,128)S(1)}, f32[24,16,128]{2,1,0:T(8,128)S(1)}, u32[]{:S(2)}, u32[]{:S(2)}) collective-permute-start(f32[24,16,128]{2,1,0:T(8,128)S(1)} %get-tuple-element.60), channel_id=1, source_target_pairs={{0,1},{1,0},{2,3},{3,2},{4,5},{5,4},{6,7},{7,6},{8,16},{9,17},{10,... | collective-permute-start | bytes 589832 | tf_op jit(solution)/shard_map/ppermute | solution.py:438
  7.2 10.2 %collective-permute-start.2 = (f32[24,16,128]{2,1,0:T(8,128)S(1)}, f32[24,16,128]{2,1,0:T(8,128)S(1)}, u32[]{:S(2)}, u32[]{:S(2)}) collective-permute-start(f32[24,16,128]{2,1,0:T(8,128)S(1)} %get-tuple-element.61), channel_id=1, source_target_pairs={{0,1},{1,0},{2,3},{3,2},{4,5},{5,4},{6,7},{7,6},{8,9},{9,8},{10,11... | collective-permute-start | bytes 589832 | tf_op jit(solution)/shard_map/ppermute | solution.py:438
  7.7 9.7 %collective-permute-start.3 = (f32[24,16,128]{2,1,0:T(8,128)S(1)}, f32[24,16,128]{2,1,0:T(8,128)S(1)}, u32[]{:S(2)}, u32[]{:S(2)}) collective-permute-start(f32[24,16,128]{2,1,0:T(8,128)S(1)} %get-tuple-element.62), channel_id=1, source_target_pairs={{0,8},{1,2},{2,1},{3,4},{4,3},{5,6},{6,5},{7,15},{8,0},{9,10},{10,... | collective-permute-start | bytes 589832 | tf_op jit(solution)/shard_map/ppermute | solution.py:438
  10.3 7.1 %copy-start = (f32[1,1,64,128]{3,2,1,0:T(8,128)S(1)}, f32[1,1,64,128]{3,2,1,0:T(8,128)}, u32[]{:S(2)}) copy-start(f32[1,1,64,128]{3,2,1,0:T(8,128)} %param.10) | copy-start | bytes 98308
  20.6 8.1 %collective-permute-start.4 = (f32[24,16,128]{2,1,0:T(8,128)S(1)}, f32[24,16,128]{2,1,0:T(8,128)S(1)}, u32[]{:S(2)}, u32[]{:S(2)}) collective-permute-start(f32[24,16,128]{2,1,0:T(8,128)S(1)} %get-tuple-element.73), channel_id=1, source_target_pairs={{0,8},{1,9},{2,10},{3,11},{4,12},{5,13},{6,14},{7,15},{8,0},{9,1},... | collective-permute-start | bytes 589832 | tf_op jit(solution)/shard_map/ppermute | solution.py:438
  20.7 8.0 %collective-permute-start.5 = (f32[24,16,128]{2,1,0:T(8,128)S(1)}, f32[24,16,128]{2,1,0:T(8,128)S(1)}, u32[]{:S(2)}, u32[]{:S(2)}) collective-permute-start(f32[24,16,128]{2,1,0:T(8,128)S(1)} %get-tuple-element.74), channel_id=1, source_target_pairs={{0,1},{1,0},{2,3},{3,2},{4,5},{5,4},{6,7},{7,6},{8,16},{9,17},{10,... | collective-permute-start | bytes 589832 | tf_op jit(solution)/shard_map/ppermute | solution.py:438
  22.0 6.7 %collective-permute-start.6 = (f32[24,16,128]{2,1,0:T(8,128)S(1)}, f32[24,16,128]{2,1,0:T(8,128)S(1)}, u32[]{:S(2)}, u32[]{:S(2)}) collective-permute-start(f32[24,16,128]{2,1,0:T(8,128)S(1)} %get-tuple-element.75), channel_id=1, source_target_pairs={{0,1},{1,0},{2,3},{3,2},{4,5},{5,4},{6,7},{7,6},{8,9},{9,8},{10,11... | collective-permute-start | bytes 589832 | tf_op jit(solution)/shard_map/ppermute | solution.py:438
  22.0 7.4 %collective-permute-start.7 = (f32[24,16,128]{2,1,0:T(8,128)S(1)}, f32[24,16,128]{2,1,0:T(8,128)S(1)}, u32[]{:S(2)}, u32[]{:S(2)}) collective-permute-start(f32[24,16,128]{2,1,0:T(8,128)S(1)} %get-tuple-element.76), channel_id=1, source_target_pairs={{0,8},{1,2},{2,1},{3,4},{4,3},{5,6},{6,5},{7,15},{8,0},{9,10},{10,... | collective-permute-start | bytes 589832 | tf_op jit(solution)/shard_map/ppermute | solution.py:438
  32.7 9.5 %collective-permute-start.8 = (f32[24,16,128]{2,1,0:T(8,128)S(1)}, f32[24,16,128]{2,1,0:T(8,128)S(1)}, u32[]{:S(2)}, u32[]{:S(2)}) collective-permute-start(f32[24,16,128]{2,1,0:T(8,128)S(1)} %get-tuple-element.83), channel_id=1, source_target_pairs={{0,8},{1,9},{2,10},{3,11},{4,12},{5,13},{6,14},{7,15},{8,0},{9,1},... | collective-permute-start | bytes 589832 | tf_op jit(solution)/shard_map/ppermute | solution.py:438
  33.9 8.3 %collective-permute-start.9 = (f32[24,16,128]{2,1,0:T(8,128)S(1)}, f32[24,16,128]{2,1,0:T(8,128)S(1)}, u32[]{:S(2)}, u32[]{:S(2)}) collective-permute-start(f32[24,16,128]{2,1,0:T(8,128)S(1)} %get-tuple-element.84), channel_id=1, source_target_pairs={{0,1},{1,0},{2,3},{3,2},{4,5},{5,4},{6,7},{7,6},{8,16},{9,17},{10,... | collective-permute-start | bytes 589832 | tf_op jit(solution)/shard_map/ppermute | solution.py:438
  33.9 8.3 %collective-permute-start.10 = (f32[24,16,128]{2,1,0:T(8,128)S(1)}, f32[24,16,128]{2,1,0:T(8,128)S(1)}, u32[]{:S(2)}, u32[]{:S(2)}) collective-permute-start(f32[24,16,128]{2,1,0:T(8,128)S(1)} %get-tuple-element.85), channel_id=1, source_target_pairs={{0,1},{1,0},{2,3},{3,2},{4,5},{5,4},{6,7},{7,6},{8,9},{9,8},{10,11... | collective-permute-start | bytes 589832 | tf_op jit(solution)/shard_map/ppermute | solution.py:438
  34.4 7.8 %collective-permute-start.11 = (f32[24,16,128]{2,1,0:T(8,128)S(1)}, f32[24,16,128]{2,1,0:T(8,128)S(1)}, u32[]{:S(2)}, u32[]{:S(2)}) collective-permute-start(f32[24,16,128]{2,1,0:T(8,128)S(1)} %get-tuple-element.86), channel_id=1, source_target_pairs={{0,8},{1,2},{2,1},{3,4},{4,3},{5,6},{6,5},{7,15},{8,0},{9,10},{10,... | collective-permute-start | bytes 589832 | tf_op jit(solution)/shard_map/ppermute | solution.py:438
  45.1 6.6 %collective-permute-start.12 = (f32[24,16,128]{2,1,0:T(8,128)S(1)}, f32[24,16,128]{2,1,0:T(8,128)S(1)}, u32[]{:S(2)}, u32[]{:S(2)}) collective-permute-start(f32[24,16,128]{2,1,0:T(8,128)S(1)} %get-tuple-element.88), channel_id=1, source_target_pairs={{0,24},{8,0},{16,8},{24,16},{1,25},{9,1},{17,9},{25,17},{2,26},{10... | collective-permute-start | bytes 589832 | tf_op jit(solution)/shard_map/ppermute | solution.py:423
  46.9 4.8 %collective-permute-start.13 = (f32[24,16,128]{2,1,0:T(8,128)S(1)}, f32[24,16,128]{2,1,0:T(8,128)S(1)}, u32[]{:S(2)}, u32[]{:S(2)}) collective-permute-start(f32[24,16,128]{2,1,0:T(8,128)S(1)} %get-tuple-element.89), channel_id=1, source_target_pairs={{0,7},{1,0},{2,1},{3,2},{4,3},{5,4},{6,5},{7,6},{8,15},{9,8},{10,9... | collective-permute-start | bytes 589832 | tf_op jit(solution)/shard_map/ppermute | solution.py:423

commit v5 on v4

--- a/solution.py
+++ b/solution.py
@@ -105,7 +105,7 @@
 
 
 def begin_kernel(rows_in, cols_in, bounds_in, block, tiles, stored, *refs):
-    (rows, cols, bounds, flags, ch, cl, v, v2, v8, undo, a, b, c, d, early, stage, sems) = refs
+    (rows, cols, bounds, flags, ch, cl, dh, dl, v, v2, v8, undo, a, b, c, d, early, stage, sems) = refs
     faces = rows.shape[1]
     chunks = faces // CHUNK
 
@@ -143,6 +143,8 @@
                 high, low = split(stage[axis, j])
                 ch[axis, j] = high
                 cl[axis, j] = low
+                dh[axis, j] = high.T
+                dl[axis, j] = low.T
                 outs.append((axis, j, two_piece(dot_nn, v2[rows[2 * axis, j]], high, low)))
         for axis, j, out in outs:
             send(rows, flags, v, axis, j, out, (a, b, c, d))
@@ -235,7 +237,7 @@
     lax.fori_loop(0, v2.shape[0] // WIDE, step, 0)
 
 
-def arrive(rows, flags, received, ch, cl, acc):
+def arrive(rows, flags, received, dh, dl, acc):
     faces = rows.shape[1]
 
     def step(s, carry):
@@ -246,7 +248,7 @@
                 j = s * FACES + r
                 even, other = received[2 * axis][j], received[2 * axis + 1][j]
                 u2 = stacked(jnp.where(flags[2 * axis] > 0, jnp.where(odd, other, even), 0.0))
-                gain = two_piece(dot_nt, u2, ch[axis, j], cl[axis, j])
+                gain = two_piece(dot_nn, u2, dh[axis, j], dl[axis, j])
                 outs.append((axis, j, gain, jnp.where(flags[2 * axis + 1] > 0, jnp.where(odd, even, other), 0.0)))
         for axis, j, gain, low in outs:
             place_rows(acc, rows, 2 * axis, gain, j)
@@ -258,16 +260,16 @@
 
 def next_kernel(order, rows, flags, bounds, *refs):
     if order == 1:
-        (v, wf, wb, diag, ux, lx, uy, ly, ch, cl, *outs, acc) = refs
+        (v, wf, wb, diag, ux, lx, uy, ly, dh, dl, ch, cl, *outs, acc) = refs
         older = None
     else:
-        (v, older, wf, wb, diag, ux, lx, uy, ly, ch, cl, *outs, acc) = refs
+        (v, older, wf, wb, diag, ux, lx, uy, ly, dh, dl, ch, cl, *outs, acc) = refs
     if order < 3:
         new, new2, new8, undo, *sends = outs
     else:
         new, new2, *sends = outs
     acc[...] = jnp.zeros_like(acc)
-    arrive(rows, flags, (ux, lx, uy, ly), ch, cl, acc)
+    arrive(rows, flags, (ux, lx, uy, ly), dh, dl, acc)
     lower = jnp.full((16, 128), bounds[0], F32)
     upper = jnp.full((16, 128), bounds[1], F32)
     half = (upper - lower) / 2.0
@@ -291,7 +293,7 @@
         shrunk(new, new8, peak, undo)
         leave(new, new2, rows, flags, ch, cl, sends)
         return
-    mx, my, gram = sends
+    mx, my = sends
 
     def copy(j, carry):
         mx[j] = new[rows[1, j]]
@@ -299,11 +301,6 @@
         return carry
 
     lax.fori_loop(0, rows.shape[1], copy, 0, unroll=8)
-    total = jnp.zeros((32, 32), F32)
-    for s in range(0, v.shape[0], 16):
-        x2 = cat([new2[s + r] for r in range(16)], axis=1)
-        total = total + dot_nt(x2, x2)
-    gram[...] = quarter(total)
 
 
 def quarter(total):
@@ -312,8 +309,8 @@
 
 
 def spread(out, gram, half):
-    value = cat([gram[:8], gram[8:], half[:8], half[8:]], axis=1)
-    value = cat([value, jnp.zeros((8, 128 - value.shape[1]), F32)], axis=1)
+    n = gram.shape[0]
+    value = cat([cat([x[k : k + 2] for k in range(0, n, 2)], axis=1) for x in (gram, half)], axis=0)
 
     def step(d, carry):
         out[d] = value
@@ -322,7 +319,7 @@
     lax.fori_loop(0, out.shape[0], step, 0)
 
 
-def project_kernel(cols, v, v2, diag, th, out, wb):
+def project_kernel(rows, cols, v, v2, diag, th, ch, out, over, gram, wb):
     group = 8
 
     def begin(s, carry):
@@ -344,57 +341,76 @@
         return carry
 
     lax.fori_loop(0, v.shape[0] // WIDE, step, 0)
-    total = jnp.zeros((32, 32), F32)
+
+    def face(s, carry):
+        for axis in range(2):
+            for r in range(CHUNK):
+                j = s * CHUNK + r
+                out = fold(dot_nn(v2[rows[2 * axis, j]], ch[axis, j]))
+                over[axis, j] = stacked(out * SHRINK)
+        return carry
+
+    lax.fori_loop(0, rows.shape[1] // CHUNK, face, 0, unroll=True)
+    total = other = jnp.zeros((32, 32), F32)
     for s in range(0, v.shape[0], 16):
         a2 = cat([v2[s + r] for r in range(16)], axis=1)
         b2 = cat([stacked(wb[s + r] * SHRINK) for r in range(16)], axis=1)
         total = total + dot_nt(a2, b2)
+        other = other + dot_nt(a2, a2)
     out[...] = quarter(total)
-
-
-def project_faces_kernel(rows, flags, v2, ux, uy, ch, part, gram, out):
+    gram[...] = quarter(other)
+
+
+def project_faces_kernel(flags, over, ux, uy, part, gram, out):
     total = jnp.zeros((32, 32), F32)
     for axis, upper in ((0, ux), (1, uy)):
-        for s in range(0, rows.shape[1], CHUNK):
+        for s in range(0, upper.shape[0], CHUNK):
             lefts, rights = [], []
             for r in range(CHUNK):
                 j = s + r
-                u2 = stacked(jnp.where(flags[2 * axis] > 0, upper[j], 0.0))
-                rights.append(stacked(fold(dot_nt(u2, ch[axis, j])) * SHRINK))
-                lefts.append(v2[rows[2 * axis, j]])
+                rights.append(stacked(jnp.where(flags[2 * axis] > 0, upper[j], 0.0)))
+                lefts.append(over[axis, j])
             total = total + dot_nt(cat(lefts, axis=1), cat(rights, axis=1))
     spread(out, gram[...], part[...] + quarter(total))
 
 
-def end_kernel(nodes, sums, v2, basis, projected):
+def end_kernel(nodes, sums, v2, out, projected, basis, sems):
     total = sums[0]
     for d in range(1, sums.shape[0]):
         total = total + sums[d]
     n = v2.shape[1] // 2
-    g = cat([total[:, :n], total[:, n : 2 * n]], axis=0) / nodes
-    half = cat([total[:, 2 * n : 3 * n], total[:, 3 * n : 4 * n]], axis=0)
+    g, half = (
+        cat([total[k : k + 2, j : j + n] for j in range(0, n * n // 2, n)], axis=0) for k in (0, 2)
+    )
+    g = g / nodes
     row = lax.broadcasted_iota(jnp.int32, (n, n), 0)
     col = lax.broadcasted_iota(jnp.int32, (n, n), 1)
-    e = jnp.where(row == col, 1.0, 0.0).astype(F32)
-    pivots = jnp.zeros((n, n), F32)
+    m = cat([g, jnp.where(row == col, 1.0, 0.0).astype(F32)], axis=1)
+    row = lax.broadcasted_iota(jnp.int32, m.shape, 0)
+    pivots = jnp.zeros(m.shape, F32)
     for k in range(n):
-        pivot = jnp.broadcast_to(g[k : k + 1, k : k + 1], (n, n))
-        pivots = jnp.where(row == k, pivot, pivots)
-        factor = jnp.broadcast_to(g[:, k : k + 1], (n, n)) / pivot
-        factor = jnp.where(row > k, factor, 0.0)
-        g = g - factor * g[k : k + 1, :]
-        e = e - factor * e[k : k + 1, :]
-    inv = e / jnp.sqrt(pivots)
+        column = jnp.broadcast_to(m[:, k : k + 1], m.shape)
+        pivots = jnp.where(row == k, column, pivots)
+        factor = jnp.where(row > k, column * (1.0 / column[k : k + 1]), 0.0)
+        m = m - factor * m[k : k + 1]
+    inv = m[:, n:] / jnp.sqrt(pivots[:, n:])
     high, low = split(inv)
     left = cat([cat([high, high], axis=1), cat([low, jnp.zeros_like(low)], axis=1)], axis=0)
-    for s in range(0, v2.shape[0], 8):
-        out = fold(dot_nn(left, cat([v2[s + r] for r in range(8)], axis=1)))
-        for r in range(8):
-            basis[s + r] = out[:, r * 128 : (r + 1) * 128]
+    group = 16
+    copies = []
+    for s in range(0, v2.shape[0], group):
+        part = fold(dot_nn(left, cat([v2[s + r] for r in range(group)], axis=1)))
+        for r in range(group):
+            basis[s + r] = part[:, r * 128 : (r + 1) * 128]
+        at = pl.ds(s, group)
+        copies.append(pltpu.make_async_copy(basis.at[at], out.at[at], sems.at[s // group]))
+        copies[-1].start()
     exact = dict(precision=lax.Precision.HIGHEST, preferred_element_type=F32)
     raw = lax.dot_general(inv, half, (((1,), (0,)), ((), ())), **exact)
     raw = lax.dot_general(raw, inv, (((1,), (1,)), ((), ())), **exact)
     projected[...] = (raw + raw.T) * (1.0 / (SHRINK * nodes))
+    for copy in copies:
+        copy.wait()
 
 
 def in_hbm(x):
@@ -405,12 +421,12 @@
     return pltpu.VMEM(shape, dtype)
 
 
-def call(kernel, name, specs, outs, scratch=(), limit=12, flops=0, nbytes=0, smem=0):
+def call(kernel, name, specs, outs, scratch=(), limit=12, flops=0, nbytes=0, smem=0, out_specs=None):
     return pl.pallas_call(
         kernel,
         name=name,
         in_specs=specs,
-        out_specs=[SM] * smem + [VM] * (len(outs) - smem),
+        out_specs=out_specs or [SM] * smem + [VM] * (len(outs) - smem),
         out_shape=outs,
         scratch_shapes=list(scratch),
         cost_estimate=pl.CostEstimate(flops=flops, bytes_accessed=nbytes, transcendentals=0),
@@ -458,15 +474,15 @@
     high, low = in_vmem(stored.shape, BF16), in_vmem(stored.shape, F8)
     face2 = in_vmem(coupling.shape, BF16)
     square = in_vmem((width, width), F32)
-    small = jax.ShapeDtypeStruct((peers, 8, 128), F32)
+    small = jax.ShapeDtypeStruct((peers, 4, 128), F32)
     local_flops = 16 * stored.size * width
 
-    rows, cols, filter_bounds, flags, ch, cl, block, x2, x8, undo, *sends, early = call(
+    rows, cols, filter_bounds, flags, ch, cl, dh, dl, block, x2, x8, undo, *sends, early = call(
         begin_kernel, "begin", [HBM] * 6,
         [
             pltpu.SMEM(rows.shape, jnp.int32), pltpu.SMEM(cols.shape, jnp.int32),
             pltpu.SMEM((2,), F32), pltpu.SMEM((6,), jnp.int32),
-            face2, face2, vec, vec2, vec8, scale, face, face, face, face,
+            face2, face2, face2, face2, vec, vec2, vec8, scale, face, face, face, face,
             in_vmem((EARLY,) + stored.shape[1:], F32),
         ],
         [pltpu.VMEM(coupling.shape, F32), pltpu.SemaphoreType.DMA((2 * (faces // CHUNK) + 6,))],
@@ -490,12 +506,12 @@
     for order in (1, 2, 3):
         carried = (x,) if older is None else (x, older)
         last = order == 3
-        outs = [vec, vec2] + ([face, face, square] if last else [vec8, scale] + [face] * 4)
+        outs = [vec, vec2] + ([face, face] if last else [vec8, scale] + [face] * 4)
         new, new2, *sends = call(
             functools.partial(next_kernel, order), "finish%d" % order,
-            [SM, SM, SM] + [VM] * (9 + len(carried)), outs,
+            [SM, SM, SM] + [VM] * (11 + len(carried)), outs,
             [pltpu.VMEM((count, width, tile), F32)],
-        )(rows, flags, filter_bounds, *carried, wf, wb, diag, *received, ch, cl)
+        )(rows, flags, filter_bounds, *carried, wf, wb, diag, *received, dh, dl, ch, cl)
         x, x2, older = new, new2, x
         if not last:
             x8, undo, *sends = sends
@@ -504,20 +520,23 @@
                 local_kernel, "local%d" % (order + 1), [SM] + [VM] * 5, [vec, vec],
                 flops=local_flops, nbytes=4 * stored.size,
             )(cols, x2, x8, undo, th, tl)
-    mx, my, gram = sends
+    mx, my = sends
     ux, uy = ring(mx, "gx", -1), ring(my, "gy", -1)
-    (part,) = call(
-        project_kernel, "project", [SM] + [VM] * 4, [square],
+    part, over, gram = call(
+        project_kernel, "project", [SM, SM] + [VM] * 5,
+        [square, in_vmem((2, faces, 2 * width, tile), BF16), square],
         [pltpu.VMEM((count, width, tile), F32)],
         flops=local_flops // 4, nbytes=2 * stored.size,
-    )(cols, x, x2, diag, th)
-    (sums,) = call(project_faces_kernel, "project_faces", [SM, SM] + [VM] * 6, [small])(
-        rows, flags, x2, ux, uy, ch, part, gram
+    )(rows, cols, x, x2, diag, th, ch)
+    (sums,) = call(project_faces_kernel, "project_faces", [SM] + [VM] * 5, [small])(
+        flags, over, ux, uy, part, gram
     )
     sums = lax.all_to_all(sums, ("gx", "gy"), 0, 0)
     basis, projected = call(
         functools.partial(end_kernel, nodes), "end", [VM, VM],
         [jax.ShapeDtypeStruct((count, width, tile), F32), jax.ShapeDtypeStruct((width, width), F32)],
+        [pltpu.VMEM((count, width, tile), F32), pltpu.SemaphoreType.DMA((count // 16,))],
+        out_specs=[HBM, VM],
     )(sums, x2)
     return (basis[None, None], projected)
 

time: 70.6 us -> 65.6 us (0.929)
  Pallas kernels: 38.9 us -> 35.2 us
  blocking collectives: 13.7 us -> 12.9 us
    pallas_call x3, Pallas kernels: 9.3 us -> 6.31 us  [shards(): call(functools.partial(next_kernel, order), 'finish%d' % order, [SM, SM,...]
    all_to_all x1, blocking collectives: 13.7 us -> 12.9 us  [shards(): sums = lax.all_to_all(sums, ('gx', 'gy'), 0, 0)]
  transfers between devices with their start and end apart: 14 -> 14, of which waited for: 2 -> 2; matrix products, arithmetic and copies ran while one was open for 0% -> 0% of each run, Pallas kernels for 30% -> 33%
where the time goes in v5:
time: 65.6 us; the launch traced here: 65.4 us
  Pallas kernels  35.2 us (54%)
  starting transfers between devices  14.8 us (23%)
  blocking collectives  12.9 us (20%)
  waiting for transfers between devices  1.52 us (2%)
  between operations  0.96 us (1%)
    all_to_all x1, blocking collectives, shards(): sums = lax.all_to_all(sums, ('gx', 'gy'), 0, 0)  12.9 us
    pallas_call x2, Pallas kernels, shards(): call(local_kernel, 'local%d' % (order + 1), [SM] + [VM] * 5, [vec, vec],...  12.1 us
    ppermute x12, starting transfers between devices, pairs(): return lax.ppermute(x, ('gx', 'gy'), moves)  11.7 us
    pallas_call x1, Pallas kernels, shards(): call(first_kernel, 'local_first', [SM] + [VM] * 4 + [HBM], [vec, vec, hig...  7.01 us
    pallas_call x3, Pallas kernels, shards(): call(functools.partial(next_kernel, order), 'finish%d' % order, [SM, SM,...  6.31 us
    pallas_call x1, Pallas kernels, shards(): call(begin_kernel, 'begin', [HBM] * 6, [pltpu.SMEM(rows.shape, jnp.int32)...  3.44 us
    ppermute x2, starting transfers between devices, ring(): return lax.ppermute(x, axis, [(i, (i + by) % peers) for i in range(peers)])  3.13 us
    pallas_call x1, Pallas kernels, shards(): call(functools.partial(end_kernel, nodes), 'end', [VM, VM], [jax.ShapeDty...  3.03 us
  transfers between devices with their start and end apart: 14, of which 2 were waited for; matrix products, arithmetic and copies ran while one was open for 0% of the time, Pallas kernels for 33%

profile of v5, /device:TPU:0, one launch (start us, length us, event | category | flops | bytes accessed | tf_op | source)
XLA Modules:
  0.0 65.4 jit_solution(1487181386725173593)
XLA Ops:
  0.6 3.4 %begin.1 = (s32[4,24]{1,0:T(4,128)S(4)}, s32[4,64]{1,0:T(4,128)S(4)}, f32[2]{0:T(128)S(4)}, s32[6]{0:T(128)S(4)}, bf16[2,24,128,128]{3,2,1,0:T(8,128)(2,1)S(1)},...) custom-call(s32[4,24]{1,0:T(4,128)} %bitcast.17, ...), custom_call_target="tpu_custom_call" | custom-call | flops 536870912 | bytes 8388608 | tf_op jit(solution)/shard_map/begin/pallas_call | solution.py:480
  4.1 3.1 %collective-permute-start = (f32[24,16,128]{2,1,0:T(8,128)S(1)}, f32[24,16,128]{2,1,0:T(8,128)S(1)}, u32[]{:S(2)}, u32[]{:S(2)}) collective-permute-start(f32[24,16,128]{2,1,0:T(8,128)S(1)} %get-tuple-element.63), channel_id=1, source_target_pairs={{0,8},{1,9},{2,10},{3,11},{4,12},{5,13},{6,14},{7,15},{8,0},{9,1},... | collective-permute-start | bytes 589832 | tf_op jit(solution)/shard_map/ppermute | solution.py:454
  7.2 0.5 collective-permute-start.2
  7.7 2.6 %collective-permute-start.3 = (f32[24,16,128]{2,1,0:T(8,128)S(1)}, f32[24,16,128]{2,1,0:T(8,128)S(1)}, u32[]{:S(2)}, u32[]{:S(2)}) collective-permute-start(f32[24,16,128]{2,1,0:T(8,128)S(1)} %get-tuple-element.66), channel_id=1, source_target_pairs={{0,8},{1,2},{2,1},{3,4},{4,3},{5,6},{6,5},{7,15},{8,0},{9,10},{10,... | collective-permute-start | bytes 589832 | tf_op jit(solution)/shard_map/ppermute | solution.py:454
  10.3 7.0 %local_first.1 = (f32[64,16,128]{2,1,0:T(8,128)S(1)}, f32[64,16,128]{2,1,0:T(8,128)S(1)}, bf16[64,4,128,128]{3,2,1,0:T(8,128)(2,1)S(1)}, f8e4m3fn[64,4,128,128]{3,2,1,0:T(32,128)(4,1)S(1)}) custom-call(s32[4,64]{1,0:T(4,128)S(4)} %get-tuple-element.54.cols, bf16[64,32,128]{2,1,0:T(8,128)(2,1)S(1)} %get-tuple-element.57.v2, ...), custom_call_target="tpu_custom_call" | custom-call | flops 1073741824 | bytes 16777216 | tf_op jit(solution)/shard_map/local_first/pallas_call | solution.py:496
  17.4 2.4 %finish1.1 = (f32[64,16,128]{2,1,0:T(8,128)S(1)}, bf16[64,32,128]{2,1,0:T(8,128)(2,1)S(1)}, f8e4m3fn[64,32,128]{2,1,0:T(32,128)(4,1)S(1)}, f32[16,128]{1,0:T(8,1...) custom-call(s32[4,24]{1,0:T(4,128)S(4)} %get-tuple-element.53.rows, ...), custom_call_target="tpu_custom_call" | custom-call | tf_op jit(solution)/shard_map/finish1/pallas_call | solution.py:510
  19.8 0.1 collective-permute-start.4
  19.9 1.3 %collective-permute-start.5 = (f32[24,16,128]{2,1,0:T(8,128)S(1)}, f32[24,16,128]{2,1,0:T(8,128)S(1)}, u32[]{:S(2)}, u32[]{:S(2)}) collective-permute-start(f32[24,16,128]{2,1,0:T(8,128)S(1)} %get-tuple-element.80), channel_id=1, source_target_pairs={{0,1},{1,0},{2,3},{3,2},{4,5},{5,4},{6,7},{7,6},{8,16},{9,17},{10,... | collective-permute-start | bytes 589832 | tf_op jit(solution)/shard_map/ppermute | solution.py:454
  21.2 0.7 %collective-permute-start.7 = (f32[24,16,128]{2,1,0:T(8,128)S(1)}, f32[24,16,128]{2,1,0:T(8,128)S(1)}, u32[]{:S(2)}, u32[]{:S(2)}) collective-permute-start(f32[24,16,128]{2,1,0:T(8,128)S(1)} %get-tuple-element.82), channel_id=1, source_target_pairs={{0,8},{1,2},{2,1},{3,4},{4,3},{5,6},{6,5},{7,15},{8,0},{9,10},{10,... | collective-permute-start | bytes 589832 | tf_op jit(solution)/shard_map/ppermute | solution.py:454
  21.9 5.9 %local2.1 = (f32[64,16,128]{2,1,0:T(8,128)S(1)}, f32[64,16,128]{2,1,0:T(8,128)S(1)}) custom-call(s32[4,64]{1,0:T(4,128)S(4)} %get-tuple-element.54.cols, bf16[64,32,128]{2,1,0:T(8,128)(2,1)S(1)} %get-tuple-element.72.v2, f8e4m3fn[64,32,128]{2,1,0:T(32,128)(4,1)S(1)} %get-tuple-element.73.v8, f32[16,128]{1,0:T(8,128)S(1)} %get-tuple-element.74.undo, ...), custom_call_target="tpu_custom_call" | custom-call | flops 1073741824 | bytes 16777216 | tf_op jit(solution)/shard_map/local2/pallas_call | solution.py:519
  27.9 0.8 %collective-permute-done.7.refs_8_ = f32[24,16,128]{2,1,0:T(8,128)S(1)} collective-permute-done((f32[24,16,128]{2,1,0:T(8,128)S(1)}, f32[24,16,128]{2,1,0:T(8,128)S(1)}, u32[]{:S(2)}, u32[]{:S(2)}) %collective-permute-start.7) | collective-permute-done | bytes 196640 | tf_op jit(solution)/shard_map/ppermute | solution.py:454
  28.7 2.5 %finish2.1 = (f32[64,16,128]{2,1,0:T(8,128)S(1)}, bf16[64,32,128]{2,1,0:T(8,128)(2,1)S(1)}, f8e4m3fn[64,32,128]{2,1,0:T(32,128)(4,1)S(1)}, f32[16,128]{1,0:T(8,1...) custom-call(s32[4,24]{1,0:T(4,128)S(4)} %get-tuple-element.53.rows, ...), custom_call_target="tpu_custom_call" | custom-call | tf_op jit(solution)/shard_map/finish2/pallas_call | solution.py:510
  31.2 1.2 %collective-permute-start.8 = (f32[24,16,128]{2,1,0:T(8,128)S(1)}, f32[24,16,128]{2,1,0:T(8,128)S(1)}, u32[]{:S(2)}, u32[]{:S(2)}) collective-permute-start(f32[24,16,128]{2,1,0:T(8,128)S(1)} %get-tuple-element.89), channel_id=1, source_target_pairs={{0,8},{1,9},{2,10},{3,11},{4,12},{5,13},{6,14},{7,15},{8,0},{9,1},... | collective-permute-start | bytes 589832 | tf_op jit(solution)/shard_map/ppermute | solution.py:454
  32.4 0.5 collective-permute-start.10
  32.9 1.7 %collective-permute-start.11 = (f32[24,16,128]{2,1,0:T(8,128)S(1)}, f32[24,16,128]{2,1,0:T(8,128)S(1)}, u32[]{:S(2)}, u32[]{:S(2)}) collective-permute-start(f32[24,16,128]{2,1,0:T(8,128)S(1)} %get-tuple-element.92), channel_id=1, source_target_pairs={{0,8},{1,2},{2,1},{3,4},{4,3},{5,6},{6,5},{7,15},{8,0},{9,10},{10,... | collective-permute-start | bytes 589832 | tf_op jit(solution)/shard_map/ppermute | solution.py:454
  34.5 6.1 %local3.1 = (f32[64,16,128]{2,1,0:T(8,128)S(1)}, f32[64,16,128]{2,1,0:T(8,128)S(1)}) custom-call(s32[4,64]{1,0:T(4,128)S(4)} %get-tuple-element.54.cols, bf16[64,32,128]{2,1,0:T(8,128)(2,1)S(1)} %get-tuple-element.84.v2, f8e4m3fn[64,32,128]{2,1,0:T(32,128)(4,1)S(1)} %get-tuple-element.85.v8, f32[16,128]{1,0:T(8,128)S(1)} %get-tuple-element.86.undo, ...), custom_call_target="tpu_custom_call" | custom-call | flops 1073741824 | bytes 16777216 | tf_op jit(solution)/shard_map/local3/pallas_call | solution.py:519
  40.7 1.4 %finish3.1 = (f32[64,16,128]{2,1,0:T(8,128)S(1)}, bf16[64,32,128]{2,1,0:T(8,128)(2,1)S(1)}, f32[24,16,128]{2,1,0:T(8,128)S(1)}, f32[24,16,128]{2,1,0:T(8,128)S(1)}) custom-call(s32[4,24]{1,0:T(4,128)S(4)} %get-tuple-element.53.rows, s32[6]{0:T(128)S(4)} %get-tuple-element.52.flags, f32[2]{0:T(128)S(4)} %get-tuple-element.55.bounds, ...), custom_call_target="tpu_custom_call" | custom-call | tf_op jit(solution)/shard_map/finish3/pallas_call | solution.py:510
  42.1 1.7 %collective-permute-start.12 = (f32[24,16,128]{2,1,0:T(8,128)S(1)}, f32[24,16,128]{2,1,0:T(8,128)S(1)}, u32[]{:S(2)}, u32[]{:S(2)}) collective-permute-start(f32[24,16,128]{2,1,0:T(8,128)S(1)} %get-tuple-element.96), channel_id=1, source_target_pairs={{0,24},{8,0},{16,8},{24,16},{1,25},{9,1},{17,9},{25,17},{2,26},{10... | collective-permute-start | bytes 589832 | tf_op jit(solution)/shard_map/ppermute | solution.py:439
  43.8 1.4 %collective-permute-start.13 = (f32[24,16,128]{2,1,0:T(8,128)S(1)}, f32[24,16,128]{2,1,0:T(8,128)S(1)}, u32[]{:S(2)}, u32[]{:S(2)}) collective-permute-start(f32[24,16,128]{2,1,0:T(8,128)S(1)} %get-tuple-element.97), channel_id=1, source_target_pairs={{0,7},{1,0},{2,1},{3,2},{4,3},{5,4},{6,5},{7,6},{8,15},{9,8},{10,9... | collective-permute-start | bytes 589832 | tf_op jit(solution)/shard_map/ppermute | solution.py:439
  45.3 2.7 %project.1 = (f32[16,16]{1,0:T(8,128)S(1)}, bf16[2,24,32,128]{3,2,1,0:T(8,128)(2,1)S(1)}, f32[16,16]{1,0:T(8,128)S(1)}) custom-call(s32[4,24]{1,0:T(4,128)S(4)} %get-tuple-element.53.rows, s32[4,64]{1,0:T(4,128)S(4)} %get-tuple-element.54.cols, f32[64,16,128]{2,1,0:T(8,128)S(1)} %get-tuple-element.93.v, bf16[64,32,128]{2,1,0:T(8,128)(2,1)S(1)} %get-tuple-element.94.v2, ...), custom_call_target="tpu_custom_call" | custom-call | flops 268435456 | bytes 8388608 | tf_op jit(solution)/shard_map/project/pallas_call | solution.py:525
  47.9 0.7 %collective-permute-done.12.ux = f32[24,16,128]{2,1,0:T(8,128)S(1)} collective-permute-done((f32[24,16,128]{2,1,0:T(8,128)S(1)}, f32[24,16,128]{2,1,0:T(8,128)S(1)}, u32[]{:S(2)}, u32[]{:S(2)}) %collective-permute-start.12) | collective-permute-done | bytes 196640 | tf_op jit(solution)/shard_map/ppermute | solution.py:439
  48.7 0.6 project_faces.1
  49.3 12.9 %all_to_all.5.sums = f32[32,4,128]{2,1,0:T(4,128)S(1)} all-to-all(f32[32,4,128]{2,1,0:T(4,128)S(1)} %project_faces.1), channel_id=1, replica_groups=mesh['gx'=4,'gy'=8] {'gx','gy'}, dimensions={0} | all-to-all | bytes 131072 | tf_op jit(solution)/shard_map/all_to_all | solution.py:534
  62.2 3.0 %end.1 = (f32[64,16,128]{2,1,0:T(8,128)}, f32[16,16]{1,0:T(8,128)}) custom-call(f32[32,4,128]{2,1,0:T(4,128)S(1)} %all_to_all.5.sums, bf16[64,32,128]{2,1,0:T(8,128)(2,1)S(1)} %get-tuple-element.94.v2), custom_call_target="tpu_custom_call" | custom-call | tf_op jit(solution)/shard_map/end/pallas_call | solution.py:535
  (17 shorter events, 0.0 us)
Async XLA Ops:
  4.1 13.3 %collective-permute-start = (f32[24,16,128]{2,1,0:T(8,128)S(1)}, f32[24,16,128]{2,1,0:T(8,128)S(1)}, u32[]{:S(2)}, u32[]{:S(2)}) collective-permute-start(f32[24,16,128]{2,1,0:T(8,128)S(1)} %get-tuple-element.63), channel_id=1, source_target_pairs={{0,8},{1,9},{2,10},{3,11},{4,12},{5,13},{6,14},{7,15},{8,0},{9,1},... | collective-permute-start | bytes 589832 | tf_op jit(solution)/shard_map/ppermute | solution.py:454
  7.2 10.2 %collective-permute-start.1 = (f32[24,16,128]{2,1,0:T(8,128)S(1)}, f32[24,16,128]{2,1,0:T(8,128)S(1)}, u32[]{:S(2)}, u32[]{:S(2)}) collective-permute-start(f32[24,16,128]{2,1,0:T(8,128)S(1)} %get-tuple-element.64), channel_id=1, source_target_pairs={{0,1},{1,0},{2,3},{3,2},{4,5},{5,4},{6,7},{7,6},{8,16},{9,17},{10,... | collective-permute-start | bytes 589832 | tf_op jit(solution)/shard_map/ppermute | solution.py:454
  7.2 10.2 %collective-permute-start.2 = (f32[24,16,128]{2,1,0:T(8,128)S(1)}, f32[24,16,128]{2,1,0:T(8,128)S(1)}, u32[]{:S(2)}, u32[]{:S(2)}) collective-permute-start(f32[24,16,128]{2,1,0:T(8,128)S(1)} %get-tuple-element.65), channel_id=1, source_target_pairs={{0,1},{1,0},{2,3},{3,2},{4,5},{5,4},{6,7},{7,6},{8,9},{9,8},{10,11... | collective-permute-start | bytes 589832 | tf_op jit(solution)/shard_map/ppermute | solution.py:454
  7.7 9.7 %collective-permute-start.3 = (f32[24,16,128]{2,1,0:T(8,128)S(1)}, f32[24,16,128]{2,1,0:T(8,128)S(1)}, u32[]{:S(2)}, u32[]{:S(2)}) collective-permute-start(f32[24,16,128]{2,1,0:T(8,128)S(1)} %get-tuple-element.66), channel_id=1, source_target_pairs={{0,8},{1,2},{2,1},{3,4},{4,3},{5,6},{6,5},{7,15},{8,0},{9,10},{10,... | collective-permute-start | bytes 589832 | tf_op jit(solution)/shard_map/ppermute | solution.py:454
  10.3 7.1 %copy-start = (f32[1,1,64,128]{3,2,1,0:T(8,128)S(1)}, f32[1,1,64,128]{3,2,1,0:T(8,128)}, u32[]{:S(2)}) copy-start(f32[1,1,64,128]{3,2,1,0:T(8,128)} %param.10) | copy-start | bytes 98308
  19.8 8.0 %collective-permute-start.4 = (f32[24,16,128]{2,1,0:T(8,128)S(1)}, f32[24,16,128]{2,1,0:T(8,128)S(1)}, u32[]{:S(2)}, u32[]{:S(2)}) collective-permute-start(f32[24,16,128]{2,1,0:T(8,128)S(1)} %get-tuple-element.79), channel_id=1, source_target_pairs={{0,8},{1,9},{2,10},{3,11},{4,12},{5,13},{6,14},{7,15},{8,0},{9,1},... | collective-permute-start | bytes 589832 | tf_op jit(solution)/shard_map/ppermute | solution.py:454
  19.9 8.0 %collective-permute-start.5 = (f32[24,16,128]{2,1,0:T(8,128)S(1)}, f32[24,16,128]{2,1,0:T(8,128)S(1)}, u32[]{:S(2)}, u32[]{:S(2)}) collective-permute-start(f32[24,16,128]{2,1,0:T(8,128)S(1)} %get-tuple-element.80), channel_id=1, source_target_pairs={{0,1},{1,0},{2,3},{3,2},{4,5},{5,4},{6,7},{7,6},{8,16},{9,17},{10,... | collective-permute-start | bytes 589832 | tf_op jit(solution)/shard_map/ppermute | solution.py:454
  21.2 6.7 %collective-permute-start.6 = (f32[24,16,128]{2,1,0:T(8,128)S(1)}, f32[24,16,128]{2,1,0:T(8,128)S(1)}, u32[]{:S(2)}, u32[]{:S(2)}) collective-permute-start(f32[24,16,128]{2,1,0:T(8,128)S(1)} %get-tuple-element.81), channel_id=1, source_target_pairs={{0,1},{1,0},{2,3},{3,2},{4,5},{5,4},{6,7},{7,6},{8,9},{9,8},{10,11... | collective-permute-start | bytes 589832 | tf_op jit(solution)/shard_map/ppermute | solution.py:454
  21.2 7.4 %collective-permute-start.7 = (f32[24,16,128]{2,1,0:T(8,128)S(1)}, f32[24,16,128]{2,1,0:T(8,128)S(1)}, u32[]{:S(2)}, u32[]{:S(2)}) collective-permute-start(f32[24,16,128]{2,1,0:T(8,128)S(1)} %get-tuple-element.82), channel_id=1, source_target_pairs={{0,8},{1,2},{2,1},{3,4},{4,3},{5,6},{6,5},{7,15},{8,0},{9,10},{10,... | collective-permute-start | bytes 589832 | tf_op jit(solution)/shard_map/ppermute | solution.py:454
  31.2 9.5 %collective-permute-start.8 = (f32[24,16,128]{2,1,0:T(8,128)S(1)}, f32[24,16,128]{2,1,0:T(8,128)S(1)}, u32[]{:S(2)}, u32[]{:S(2)}) collective-permute-start(f32[24,16,128]{2,1,0:T(8,128)S(1)} %get-tuple-element.89), channel_id=1, source_target_pairs={{0,8},{1,9},{2,10},{3,11},{4,12},{5,13},{6,14},{7,15},{8,0},{9,1},... | collective-permute-start | bytes 589832 | tf_op jit(solution)/shard_map/ppermute | solution.py:454
  32.4 8.3 %collective-permute-start.9 = (f32[24,16,128]{2,1,0:T(8,128)S(1)}, f32[24,16,128]{2,1,0:T(8,128)S(1)}, u32[]{:S(2)}, u32[]{:S(2)}) collective-permute-start(f32[24,16,128]{2,1,0:T(8,128)S(1)} %get-tuple-element.90), channel_id=1, source_target_pairs={{0,1},{1,0},{2,3},{3,2},{4,5},{5,4},{6,7},{7,6},{8,16},{9,17},{10,... | collective-permute-start | bytes 589832 | tf_op jit(solution)/shard_map/ppermute | solution.py:454
  32.4 8.3 %collective-permute-start.10 = (f32[24,16,128]{2,1,0:T(8,128)S(1)}, f32[24,16,128]{2,1,0:T(8,128)S(1)}, u32[]{:S(2)}, u32[]{:S(2)}) collective-permute-start(f32[24,16,128]{2,1,0:T(8,128)S(1)} %get-tuple-element.91), channel_id=1, source_target_pairs={{0,1},{1,0},{2,3},{3,2},{4,5},{5,4},{6,7},{7,6},{8,9},{9,8},{10,11... | collective-permute-start | bytes 589832 | tf_op jit(solution)/shard_map/ppermute | solution.py:454
  32.9 7.8 %collective-permute-start.11 = (f32[24,16,128]{2,1,0:T(8,128)S(1)}, f32[24,16,128]{2,1,0:T(8,128)S(1)}, u32[]{:S(2)}, u32[]{:S(2)}) collective-permute-start(f32[24,16,128]{2,1,0:T(8,128)S(1)} %get-tuple-element.92), channel_id=1, source_target_pairs={{0,8},{1,2},{2,1},{3,4},{4,3},{5,6},{6,5},{7,15},{8,0},{9,10},{10,... | collective-permute-start | bytes 589832 | tf_op jit(solution)/shard_map/ppermute | solution.py:454
  42.1 6.5 %collective-permute-start.12 = (f32[24,16,128]{2,1,0:T(8,128)S(1)}, f32[24,16,128]{2,1,0:T(8,128)S(1)}, u32[]{:S(2)}, u32[]{:S(2)}) collective-permute-start(f32[24,16,128]{2,1,0:T(8,128)S(1)} %get-tuple-element.96), channel_id=1, source_target_pairs={{0,24},{8,0},{16,8},{24,16},{1,25},{9,1},{17,9},{25,17},{2,26},{10... | collective-permute-start | bytes 589832 | tf_op jit(solution)/shard_map/ppermute | solution.py:439
  43.8 4.8 %collective-permute-start.13 = (f32[24,16,128]{2,1,0:T(8,128)S(1)}, f32[24,16,128]{2,1,0:T(8,128)S(1)}, u32[]{:S(2)}, u32[]{:S(2)}) collective-permute-start(f32[24,16,128]{2,1,0:T(8,128)S(1)} %get-tuple-element.97), channel_id=1, source_target_pairs={{0,7},{1,0},{2,1},{3,2},{4,3},{5,4},{6,5},{7,6},{8,15},{9,8},{10,9... | collective-permute-start | bytes 589832 | tf_op jit(solution)/shard_map/ppermute | solution.py:439

commit v6 on v5

--- a/solution.py
+++ b/solution.py
@@ -162,16 +162,17 @@
     sends[2 * axis + 1][j] = jnp.where(odd, product, minus)
 
 
-def local_rows(rows, cols, v2, v8, undo, highs, lows, wf, wb):
+def local_rows(rows, cols, v2, v8, undo, pieces, wf, wb):
     down = undo[...]
     wide = cat([down] * 4, axis=1)
     outs = []
-    for i, high, low in zip(rows, highs, lows):
+    for r, i in enumerate(rows):
+        high, low, high_t, low_t = pieces(r, i)
         at = [cols[k, i] for k in range(4)]
         high = cat(high, axis=1)
         low = cat(low, axis=1)
-        forward = fold(dot_nt(cat([v2[c] for c in at], axis=1), high))
-        forward = forward + down * fold(dot_nt(cat([v8[c] for c in at], axis=1), low))
+        forward = fold(dot_nn(cat([v2[c] for c in at], axis=1), cat(high_t, axis=0)))
+        forward = forward + down * fold(dot_nn(cat([v8[c] for c in at], axis=1), cat(low_t, axis=0)))
         backward = fold(dot_nn(v2[i], high)) + wide * fold(dot_nn(v8[i], low))
         outs.append((forward, backward))
     for i, (forward, backward) in zip(rows, outs):
@@ -181,57 +182,62 @@
             wb[at] = wb[at] + backward[:, k * 128 : (k + 1) * 128]
 
 
-def first_kernel(cols, v2, v8, undo, early, tiles, wf, wb, th, tl, stage, sems):
-    copies = stage.shape[0] // ROWS
+def first_kernel(cols, v2, v8, undo, early, tiles, wf, wb, th, tl, thT, tlT, stage, sems):
+    copies = tiles.shape[0] // ROWS - EARLY // ROWS
+    slots = stage.shape[0]
+    ahead = slots - 1
 
     def fetch(c):
-        part = pl.ds(c * ROWS, ROWS)
-        return pltpu.make_async_copy(
-            tiles.at[pl.ds(EARLY + c * ROWS, ROWS)], stage.at[part], sems.at[c]
-        )
-
-    for c in range(copies):
-        fetch(c).start()
+        slot = lax.rem(c, slots)
+        part = pl.ds(EARLY + c * ROWS, ROWS)
+        return pltpu.make_async_copy(tiles.at[part], stage.at[slot], sems.at[slot])
+
+    for c in range(ahead):
+        fetch(jnp.int32(c)).start()
     wb[...] = jnp.zeros_like(wb)
 
-    def work(source, start, c):
-        rows, highs, lows = [], [], []
-        for r in range(ROWS):
-            i = start + c * ROWS + r
-            pieces = []
+    def work(source, start):
+        def pieces(r, i):
+            made = [[], [], [], []]
             for k in range(4):
-                t = source[c * ROWS + r, k]
+                t = source[r, k]
                 high = t.astype(BF16)
-                pieces.append((high, low_tile(t, high)))
-            for k in range(4):
-                th[i, k] = pieces[k][0]
-                tl[i, k] = pieces[k][1]
-            rows.append(i)
-            highs.append([p[0] for p in pieces])
-            lows.append([p[1] for p in pieces])
-        local_rows(rows, cols, v2, v8, undo, highs, lows, wf, wb)
+                low = low_tile(t, high)
+                for out, ref, x in zip(made, (th, tl, thT, tlT), (high, low, high.T, low.T)):
+                    ref[i, k] = x
+                    out.append(x)
+            return made
+
+        local_rows([start + r for r in range(ROWS)], cols, v2, v8, undo, pieces, wf, wb)
 
     def step_early(c, carry):
-        work(early, 0, c)
+        work(early.at[pl.ds(c * ROWS, ROWS)], c * ROWS)
         return carry
 
     def step(c, carry):
         fetch(c).wait()
-        work(stage, EARLY, c)
+
+        @pl.when(c + ahead < copies)
+        def _():
+            fetch(c + ahead).start()
+
+        work(stage.at[lax.rem(c, slots)], EARLY + c * ROWS)
         return carry
 
     lax.fori_loop(0, EARLY // ROWS, step_early, 0)
     lax.fori_loop(0, copies, step, 0)
 
 
-def local_kernel(cols, v2, v8, undo, th, tl, wf, wb):
+def local_kernel(cols, v2, v8, undo, th, tl, thT, tlT, wf, wb):
     wb[...] = jnp.zeros_like(wb)
 
     def step(c, carry):
         rows = [c * WIDE + r for r in range(WIDE)]
-        highs = [[th[i, k] for k in range(4)] for i in rows]
-        lows = [[tl[i, k] for k in range(4)] for i in rows]
-        local_rows(rows, cols, v2, v8, undo, highs, lows, wf, wb)
+
+        def pieces(r, i):
+            return [[ref[i, k] for k in range(4)] for ref in (th, tl, thT, tlT)]
+
+        local_rows(rows, cols, v2, v8, undo, pieces, wf, wb)
         return carry
 
     lax.fori_loop(0, v2.shape[0] // WIDE, step, 0)
@@ -293,14 +299,20 @@
         shrunk(new, new8, peak, undo)
         leave(new, new2, rows, flags, ch, cl, sends)
         return
-    mx, my = sends
-
-    def copy(j, carry):
-        mx[j] = new[rows[1, j]]
-        my[j] = new[rows[3, j]]
-        return carry
-
-    lax.fori_loop(0, rows.shape[1], copy, 0, unroll=8)
+    last_sends(new, new2, rows, flags, ch, sends)
+
+
+def last_sends(v, v2, rows, flags, ch, sends):
+    part = rows.shape[1] // 2
+    outs = []
+    for axis in range(2):
+        for j in range(part):
+            outs.append((axis, j, fold(dot_nn(v2[rows[2 * axis, j]], ch[axis, j]))))
+    for axis, j, out in outs:
+        minus = v[rows[2 * axis + 1, part + j]]
+        odd = flags[4 + axis] > 0
+        sends[2 * axis][j] = jnp.where(odd, minus, out)
+        sends[2 * axis + 1][j] = jnp.where(odd, out, minus)
 
 
 def quarter(total):
@@ -342,15 +354,11 @@
 
     lax.fori_loop(0, v.shape[0] // WIDE, step, 0)
 
-    def face(s, carry):
-        for axis in range(2):
-            for r in range(CHUNK):
-                j = s * CHUNK + r
-                out = fold(dot_nn(v2[rows[2 * axis, j]], ch[axis, j]))
-                over[axis, j] = stacked(out * SHRINK)
-        return carry
-
-    lax.fori_loop(0, rows.shape[1] // CHUNK, face, 0, unroll=True)
+    part = over.shape[1]
+    for axis in range(2):
+        for j in range(part):
+            product = fold(dot_nn(v2[rows[2 * axis, part + j]], ch[axis, part + j]))
+            over[axis, j] = stacked(product * SHRINK)
     total = other = jnp.zeros((32, 32), F32)
     for s in range(0, v.shape[0], 16):
         a2 = cat([v2[s + r] for r in range(16)], axis=1)
@@ -361,16 +369,19 @@
     gram[...] = quarter(other)
 
 
-def project_faces_kernel(flags, over, ux, uy, part, gram, out):
+def project_faces_kernel(rows, flags, v2, over, xe, xo, ye, yo, part, gram, out):
     total = jnp.zeros((32, 32), F32)
-    for axis, upper in ((0, ux), (1, uy)):
-        for s in range(0, upper.shape[0], CHUNK):
-            lefts, rights = [], []
-            for r in range(CHUNK):
-                j = s + r
-                rights.append(stacked(jnp.where(flags[2 * axis] > 0, upper[j], 0.0)))
-                lefts.append(over[axis, j])
-            total = total + dot_nt(cat(lefts, axis=1), cat(rights, axis=1))
+    count = xe.shape[0]
+    for axis, (even, odd) in enumerate(((xe, xo), (ye, yo))):
+        swapped = flags[4 + axis] > 0
+        lefts, rights = [], []
+        for j in range(count):
+            e, o = even[j], odd[j]
+            above = jnp.where(flags[2 * axis] > 0, jnp.where(swapped, o, e), 0.0)
+            below = jnp.where(flags[2 * axis + 1] > 0, jnp.where(swapped, e, o), 0.0)
+            lefts += [over[axis, j], stacked(below * SHRINK)]
+            rights += [stacked(above), v2[rows[2 * axis + 1, j]]]
+        total = total + dot_nt(cat(lefts, axis=1), cat(rights, axis=1))
     spread(out, gram[...], part[...] + quarter(total))
 
 
@@ -388,11 +399,19 @@
     m = cat([g, jnp.where(row == col, 1.0, 0.0).astype(F32)], axis=1)
     row = lax.broadcasted_iota(jnp.int32, m.shape, 0)
     pivots = jnp.zeros(m.shape, F32)
-    for k in range(n):
-        column = jnp.broadcast_to(m[:, k : k + 1], m.shape)
-        pivots = jnp.where(row == k, column, pivots)
-        factor = jnp.where(row > k, column * (1.0 / column[k : k + 1]), 0.0)
-        m = m - factor * m[k : k + 1]
+    for k in range(0, n, 2):
+        first = jnp.broadcast_to(m[:, k : k + 1], m.shape)
+        second = jnp.broadcast_to(m[:, k + 1 : k + 2], m.shape)
+        pivots = jnp.where(row == k, first, pivots)
+        ratio = 1.0 / first[k : k + 1]
+        step = first[k + 1 : k + 2] * ratio
+        second = second - first * (second[k : k + 1] * ratio)
+        pivots = jnp.where(row == k + 1, second, pivots)
+        top = m[k : k + 1]
+        below = m[k + 1 : k + 2] - step * top
+        factor = jnp.where(row > k, first * ratio, 0.0)
+        other = jnp.where(row > k + 1, second * (1.0 / second[k + 1 : k + 2]), 0.0)
+        m = m - factor * top - other * below
     inv = m[:, n:] / jnp.sqrt(pivots[:, n:])
     high, low = split(inv)
     left = cat([cat([high, high], axis=1), cat([low, jnp.zeros_like(low)], axis=1)], axis=0)
@@ -434,11 +453,6 @@
     )
 
 
-def ring(x, axis, by):
-    peers = lax.axis_size(axis)
-    return lax.ppermute(x, axis, [(i, (i + by) % peers) for i in range(peers)])
-
-
 def pairs(x, axis, odd):
     nx, ny = lax.axis_size("gx"), lax.axis_size("gy")
     moves = []
@@ -470,6 +484,7 @@
     vec2 = in_vmem((count, 2 * width, tile), BF16)
     vec8 = in_vmem((count, 2 * width, tile), F8)
     scale = in_vmem((width, tile), F32)
+    half_face = jax.ShapeDtypeStruct((faces // 2, width, tile), F32)
     face = jax.ShapeDtypeStruct((faces, width, tile), F32)
     high, low = in_vmem(stored.shape, BF16), in_vmem(stored.shape, F8)
     face2 = in_vmem(coupling.shape, BF16)
@@ -493,20 +508,20 @@
         return tuple(pairs(x, k // 2, k % 2) for k, x in enumerate(sends))
 
     received = exchange(sends)
-    wf, wb, th, tl = call(
-        first_kernel, "local_first", [SM] + [VM] * 4 + [HBM], [vec, vec, high, low],
+    wf, wb, th, tl, thT, tlT = call(
+        first_kernel, "local_first", [SM] + [VM] * 4 + [HBM], [vec, vec, high, low, high, low],
         [
-            pltpu.VMEM((count - EARLY,) + stored.shape[1:], F32),
-            pltpu.SemaphoreType.DMA(((count - EARLY) // ROWS,)),
+            pltpu.VMEM((4, ROWS) + stored.shape[1:], F32),
+            pltpu.SemaphoreType.DMA((4,)),
         ],
-        limit=24, flops=local_flops, nbytes=4 * stored.size,
+        limit=16, flops=local_flops, nbytes=4 * stored.size,
     )(cols, x2, x8, undo, early, in_hbm(stored))
 
     x, older = block, None
     for order in (1, 2, 3):
         carried = (x,) if older is None else (x, older)
         last = order == 3
-        outs = [vec, vec2] + ([face, face] if last else [vec8, scale] + [face] * 4)
+        outs = [vec, vec2] + ([half_face] * 4 if last else [vec8, scale] + [face] * 4)
         new, new2, *sends = call(
             functools.partial(next_kernel, order), "finish%d" % order,
             [SM, SM, SM] + [VM] * (11 + len(carried)), outs,
@@ -517,19 +532,18 @@
             x8, undo, *sends = sends
             received = exchange(sends)
             wf, wb = call(
-                local_kernel, "local%d" % (order + 1), [SM] + [VM] * 5, [vec, vec],
+                local_kernel, "local%d" % (order + 1), [SM] + [VM] * 7, [vec, vec],
                 flops=local_flops, nbytes=4 * stored.size,
-            )(cols, x2, x8, undo, th, tl)
-    mx, my = sends
-    ux, uy = ring(mx, "gx", -1), ring(my, "gy", -1)
+            )(cols, x2, x8, undo, th, tl, thT, tlT)
+    received = exchange(sends)
     part, over, gram = call(
         project_kernel, "project", [SM, SM] + [VM] * 5,
-        [square, in_vmem((2, faces, 2 * width, tile), BF16), square],
+        [square, in_vmem((2, faces // 2, 2 * width, tile), BF16), square],
         [pltpu.VMEM((count, width, tile), F32)],
         flops=local_flops // 4, nbytes=2 * stored.size,
     )(rows, cols, x, x2, diag, th, ch)
-    (sums,) = call(project_faces_kernel, "project_faces", [SM] + [VM] * 5, [small])(
-        flags, over, ux, uy, part, gram
+    (sums,) = call(project_faces_kernel, "project_faces", [SM, SM] + [VM] * 8, [small])(
+        rows, flags, x2, over, *received, part, gram
     )
     sums = lax.all_to_all(sums, ("gx", "gy"), 0, 0)
     basis, projected = call(

time: 65.6 us -> 63.5 us (0.968)
  blocking collectives: 12.9 us -> 11.7 us
  Pallas kernels: 35.2 us -> 34.2 us
    ppermute x2 -> x0, starting transfers between devices: 3.13 us -> none  [ring(): return lax.ppermute(x, axis, [(i, (i + by) % peers) for i in range(peers)])]
    ppermute x12 -> x16, starting transfers between devices: 11.7 us -> 14.8 us  [pairs(): return lax.ppermute(x, ('gx', 'gy'), moves)]
    all_to_all x1, blocking collectives: 12.9 us -> 11.7 us  [shards(): sums = lax.all_to_all(sums, ('gx', 'gy'), 0, 0)]
    ppermute x12 -> x16, waiting for transfers between devices: 0.8 us -> 1.65 us  [pairs(): return lax.ppermute(x, ('gx', 'gy'), moves)]
    pallas_call x3, Pallas kernels: 12.7 us -> 11.9 us  [the longest x2 11.3 us: shards(): call(local_kernel, 'local%d' % (order + 1), [SM] + [VM] * 7, [vec, vec],...]
    ppermute x2 -> x0, waiting for transfers between devices: 0.73 us -> none  [ring(): return lax.ppermute(x, axis, [(i, (i + by) % peers) for i in range(peers)])]
  transfers between devices with their start and end apart: 14 -> 16, of which waited for: 2 -> 3; matrix products, arithmetic and copies ran while one was open for 0% -> 0% of each run, Pallas kernels for 33% -> 33%
where the time goes in v6:
time: 63.5 us; the launch traced here: 63.3 us
  Pallas kernels  34.2 us (54%)
  starting transfers between devices  14.8 us (23%)
  blocking collectives  11.7 us (18%)
  waiting for transfers between devices  1.65 us (3%)
  between operations  0.96 us (2%)
    ppermute x16, starting transfers between devices, pairs(): return lax.ppermute(x, ('gx', 'gy'), moves)  14.8 us
    all_to_all x1, blocking collectives, shards(): sums = lax.all_to_all(sums, ('gx', 'gy'), 0, 0)  11.7 us
    pallas_call x2, Pallas kernels, shards(): call(local_kernel, 'local%d' % (order + 1), [SM] + [VM] * 7, [vec, vec],...  11.3 us
    pallas_call x1, Pallas kernels, shards(): call(first_kernel, 'local_first', [SM] + [VM] * 4 + [HBM], [vec, vec, hig...  7.04 us
    pallas_call x3, Pallas kernels, shards(): call(functools.partial(next_kernel, order), 'finish%d' % order, [SM, SM,...  6.81 us
    pallas_call x1, Pallas kernels, shards(): call(begin_kernel, 'begin', [HBM] * 6, [pltpu.SMEM(rows.shape, jnp.int32)...  3.44 us
    pallas_call x1, Pallas kernels, shards(): call(functools.partial(end_kernel, nodes), 'end', [VM, VM], [jax.ShapeDty...  2.5 us
    pallas_call x1, Pallas kernels, shards(): call(project_kernel, 'project', [SM, SM] + [VM] * 5, [square, in_vmem((2,...  2.48 us
  transfers between devices with their start and end apart: 16, of which 3 were waited for; matrix products, arithmetic and copies ran while one was open for 0% of the time, Pallas kernels for 33%

profile of v6, /device:TPU:0, one launch (start us, length us, event | category | flops | bytes accessed | tf_op | source)
XLA Modules:
  0.0 63.3 jit_solution(8202226174831784920)
XLA Ops:
  0.6 3.4 %begin.1 = (s32[4,24]{1,0:T(4,128)S(4)}, s32[4,64]{1,0:T(4,128)S(4)}, f32[2]{0:T(128)S(4)}, s32[6]{0:T(128)S(4)}, bf16[2,24,128,128]{3,2,1,0:T(8,128)(2,1)S(1)},...) custom-call(s32[4,24]{1,0:T(4,128)} %bitcast.17, ...), custom_call_target="tpu_custom_call" | custom-call | flops 536870912 | bytes 8388608 | tf_op jit(solution)/shard_map/begin/pallas_call | solution.py:495
  4.1 3.1 %collective-permute-start = (f32[24,16,128]{2,1,0:T(8,128)S(1)}, f32[24,16,128]{2,1,0:T(8,128)S(1)}, u32[]{:S(2)}, u32[]{:S(2)}) collective-permute-start(f32[24,16,128]{2,1,0:T(8,128)S(1)} %get-tuple-element.67), channel_id=1, source_target_pairs={{0,8},{1,9},{2,10},{3,11},{4,12},{5,13},{6,14},{7,15},{8,0},{9,1},... | collective-permute-start | bytes 589832 | tf_op jit(solution)/shard_map/ppermute | solution.py:468
  7.2 0.5 collective-permute-start.2
  7.7 2.6 %collective-permute-start.3 = (f32[24,16,128]{2,1,0:T(8,128)S(1)}, f32[24,16,128]{2,1,0:T(8,128)S(1)}, u32[]{:S(2)}, u32[]{:S(2)}) collective-permute-start(f32[24,16,128]{2,1,0:T(8,128)S(1)} %get-tuple-element.70), channel_id=1, source_target_pairs={{0,8},{1,2},{2,1},{3,4},{4,3},{5,6},{6,5},{7,15},{8,0},{9,10},{10,... | collective-permute-start | bytes 589832 | tf_op jit(solution)/shard_map/ppermute | solution.py:468
  10.3 7.0 %local_first.1 = (f32[64,16,128]{2,1,0:T(8,128)S(1)}, f32[64,16,128]{2,1,0:T(8,128)S(1)}, bf16[64,4,128,128]{3,2,1,0:T(8,128)(2,1)S(1)}, f8e4m3fn[64,4,128,128]{...) custom-call(s32[4,64]{1,0:T(4,128)S(4)} %get-tuple-element.60.cols, ...), custom_call_target="tpu_custom_call" | custom-call | flops 1073741824 | bytes 16777216 | tf_op jit(solution)/shard_map/local_first/pallas_call | solution.py:511
  17.4 2.5 %finish1.1 = (f32[64,16,128]{2,1,0:T(8,128)S(1)}, bf16[64,32,128]{2,1,0:T(8,128)(2,1)S(1)}, f8e4m3fn[64,32,128]{2,1,0:T(32,128)(4,1)S(1)}, f32[16,128]{1,0:T(8,1...) custom-call(s32[4,24]{1,0:T(4,128)S(4)} %get-tuple-element.56.rows, ...), custom_call_target="tpu_custom_call" | custom-call | tf_op jit(solution)/shard_map/finish1/pallas_call | solution.py:525
  20.0 1.3 %collective-permute-start.5 = (f32[24,16,128]{2,1,0:T(8,128)S(1)}, f32[24,16,128]{2,1,0:T(8,128)S(1)}, u32[]{:S(2)}, u32[]{:S(2)}) collective-permute-start(f32[24,16,128]{2,1,0:T(8,128)S(1)} %get-tuple-element.86), channel_id=1, source_target_pairs={{0,1},{1,0},{2,3},{3,2},{4,5},{5,4},{6,7},{7,6},{8,16},{9,17},{10,... | collective-permute-start | bytes 589832 | tf_op jit(solution)/shard_map/ppermute | solution.py:468
  21.3 0.7 %collective-permute-start.7 = (f32[24,16,128]{2,1,0:T(8,128)S(1)}, f32[24,16,128]{2,1,0:T(8,128)S(1)}, u32[]{:S(2)}, u32[]{:S(2)}) collective-permute-start(f32[24,16,128]{2,1,0:T(8,128)S(1)} %get-tuple-element.88), channel_id=1, source_target_pairs={{0,8},{1,2},{2,1},{3,4},{4,3},{5,6},{6,5},{7,15},{8,0},{9,10},{10,... | collective-permute-start | bytes 589832 | tf_op jit(solution)/shard_map/ppermute | solution.py:468
  22.0 5.6 %local2.1 = (f32[64,16,128]{2,1,0:T(8,128)S(1)}, f32[64,16,128]{2,1,0:T(8,128)S(1)}) custom-call(s32[4,64]{1,0:T(4,128)S(4)} %get-tuple-element.60.cols, bf16[64,32,128]{2,1,0:T(8,128)(2,1)S(1)} %get-tuple-element.76.v2, f8e4m3fn[64,32,128]{2,1,0:T(32,128)(4,1)S(1)} %get-tuple-element.77.v8, f32[16,128]{1,0:T(8,128)S(1)} %get-tuple-element.78.undo, ...), custom_call_target="tpu_custom_call" | custom-call | flops 1073741824 | bytes 16777216 | tf_op jit(solution)/shard_map/local2/pallas_call | solution.py:534
  27.7 1.1 %collective-permute-done.7.refs_8_ = f32[24,16,128]{2,1,0:T(8,128)S(1)} collective-permute-done((f32[24,16,128]{2,1,0:T(8,128)S(1)}, f32[24,16,128]{2,1,0:T(8,128)S(1)}, u32[]{:S(2)}, u32[]{:S(2)}) %collective-permute-start.7) | collective-permute-done | bytes 196640 | tf_op jit(solution)/shard_map/ppermute | solution.py:468
  28.8 2.5 %finish2.1 = (f32[64,16,128]{2,1,0:T(8,128)S(1)}, bf16[64,32,128]{2,1,0:T(8,128)(2,1)S(1)}, f8e4m3fn[64,32,128]{2,1,0:T(32,128)(4,1)S(1)}, f32[16,128]{1,0:T(8,1...) custom-call(s32[4,24]{1,0:T(4,128)S(4)} %get-tuple-element.56.rows, ...), custom_call_target="tpu_custom_call" | custom-call | tf_op jit(solution)/shard_map/finish2/pallas_call | solution.py:525
  31.3 1.2 %collective-permute-start.8 = (f32[24,16,128]{2,1,0:T(8,128)S(1)}, f32[24,16,128]{2,1,0:T(8,128)S(1)}, u32[]{:S(2)}, u32[]{:S(2)}) collective-permute-start(f32[24,16,128]{2,1,0:T(8,128)S(1)} %get-tuple-element.95), channel_id=1, source_target_pairs={{0,8},{1,9},{2,10},{3,11},{4,12},{5,13},{6,14},{7,15},{8,0},{9,1},... | collective-permute-start | bytes 589832 | tf_op jit(solution)/shard_map/ppermute | solution.py:468
  32.5 0.5 collective-permute-start.10
  33.0 1.4 %collective-permute-start.11 = (f32[24,16,128]{2,1,0:T(8,128)S(1)}, f32[24,16,128]{2,1,0:T(8,128)S(1)}, u32[]{:S(2)}, u32[]{:S(2)}) collective-permute-start(f32[24,16,128]{2,1,0:T(8,128)S(1)} %get-tuple-element.98), channel_id=1, source_target_pairs={{0,8},{1,2},{2,1},{3,4},{4,3},{5,6},{6,5},{7,15},{8,0},{9,10},{10,... | collective-permute-start | bytes 589832 | tf_op jit(solution)/shard_map/ppermute | solution.py:468
  34.4 5.6 %local3.1 = (f32[64,16,128]{2,1,0:T(8,128)S(1)}, f32[64,16,128]{2,1,0:T(8,128)S(1)}) custom-call(s32[4,64]{1,0:T(4,128)S(4)} %get-tuple-element.60.cols, bf16[64,32,128]{2,1,0:T(8,128)(2,1)S(1)} %get-tuple-element.90.v2, f8e4m3fn[64,32,128]{2,1,0:T(32,128)(4,1)S(1)} %get-tuple-element.91.v8, f32[16,128]{1,0:T(8,128)S(1)} %get-tuple-element.92.undo, ...), custom_call_target="tpu_custom_call" | custom-call | flops 1073741824 | bytes 16777216 | tf_op jit(solution)/shard_map/local3/pallas_call | solution.py:534
  40.1 1.8 %finish3.1 = (f32[64,16,128]{2,1,0:T(8,128)S(1)}, bf16[64,32,128]{2,1,0:T(8,128)(2,1)S(1)}, f32[12,16,128]{2,1,0:T(8,128)S(1)}, f32[12,16,128]{2,1,0:T(8,128)S(1...) custom-call(s32[4,24]{1,0:T(4,128)S(4)} %get-tuple-element.56.rows, s32[6]{0:T(128)S(4)} %get-tuple-element.57.flags, ...), custom_call_target="tpu_custom_call" | custom-call | tf_op jit(solution)/shard_map/finish3/pallas_call | solution.py:525
  41.9 1.2 %collective-permute-start.12 = (f32[12,16,128]{2,1,0:T(8,128)S(1)}, f32[12,16,128]{2,1,0:T(8,128)S(1)}, u32[]{:S(2)}, u32[]{:S(2)}) collective-permute-start(f32[12,16,128]{2,1,0:T(8,128)S(1)} %get-tuple-element.102), channel_id=1, source_target_pairs={{0,8},{1,9},{2,10},{3,11},{4,12},{5,13},{6,14},{7,15},{8,0},{9,1},... | collective-permute-start | bytes 294920 | tf_op jit(solution)/shard_map/ppermute | solution.py:468
  43.1 0.3 collective-permute-start.13
  43.7 1.6 %collective-permute-start.15 = (f32[12,16,128]{2,1,0:T(8,128)S(1)}, f32[12,16,128]{2,1,0:T(8,128)S(1)}, u32[]{:S(2)}, u32[]{:S(2)}) collective-permute-start(f32[12,16,128]{2,1,0:T(8,128)S(1)} %get-tuple-element.105), channel_id=1, source_target_pairs={{0,8},{1,2},{2,1},{3,4},{4,3},{5,6},{6,5},{7,15},{8,0},{9,10},{10,... | collective-permute-start | bytes 294920 | tf_op jit(solution)/shard_map/ppermute | solution.py:468
  45.3 2.5 %project.1 = (f32[16,16]{1,0:T(8,128)S(1)}, bf16[2,12,32,128]{3,2,1,0:T(8,128)(2,1)S(1)}, f32[16,16]{1,0:T(8,128)S(1)}) custom-call(s32[4,24]{1,0:T(4,128)S(4)} %get-tuple-element.56.rows, s32[4,64]{1,0:T(4,128)S(4)} %get-tuple-element.60.cols, f32[64,16,128]{2,1,0:T(8,128)S(1)} %get-tuple-element.100.v, bf16[64,32,128]{2,1,0:T(8,128)(2,1)S(1)} %get-tuple-element.99.v2, ...), custom_call_target="tpu_custom_call" | custom-call | flops 268435456 | bytes 8388608 | tf_op jit(solution)/shard_map/project/pallas_call | solution.py:539
  47.8 0.5 collective-permute-done.15.yo
  48.3 0.6 %project_faces.1 = f32[32,4,128]{2,1,0:T(4,128)S(1)} custom-call(s32[4,24]{1,0:T(4,128)S(4)} %get-tuple-element.56.rows, s32[6]{0:T(128)S(4)} %get-tuple-element.57.flags, bf16[64,32,128]{2,1,0:T(8,128)(2,1)S(1)} %get-tuple-element.99.v2, bf16[2,12,32,128]{3,2,1,0:T(8,128)(2,1)S(1)} %get-tuple-element.101.over, ...), custom_call_target="tpu_custom_call" | custom-call | tf_op jit(solution)/shard_map/project_faces/pallas_call | solution.py:545
  48.9 11.7 %all_to_all.5.sums = f32[32,4,128]{2,1,0:T(4,128)S(1)} all-to-all(f32[32,4,128]{2,1,0:T(4,128)S(1)} %project_faces.1), channel_id=1, replica_groups=mesh['gx'=4,'gy'=8] {'gx','gy'}, dimensions={0} | all-to-all | bytes 131072 | tf_op jit(solution)/shard_map/all_to_all | solution.py:548
  60.7 2.5 %end.1 = (f32[64,16,128]{2,1,0:T(8,128)}, f32[16,16]{1,0:T(8,128)}) custom-call(f32[32,4,128]{2,1,0:T(4,128)S(1)} %all_to_all.5.sums, bf16[64,32,128]{2,1,0:T(8,128)(2,1)S(1)} %get-tuple-element.99.v2), custom_call_target="tpu_custom_call" | custom-call | tf_op jit(solution)/shard_map/end/pallas_call | solution.py:549
  (21 shorter events, 0.4 us)
Async XLA Ops:
  4.1 13.3 %collective-permute-start = (f32[24,16,128]{2,1,0:T(8,128)S(1)}, f32[24,16,128]{2,1,0:T(8,128)S(1)}, u32[]{:S(2)}, u32[]{:S(2)}) collective-permute-start(f32[24,16,128]{2,1,0:T(8,128)S(1)} %get-tuple-element.67), channel_id=1, source_target_pairs={{0,8},{1,9},{2,10},{3,11},{4,12},{5,13},{6,14},{7,15},{8,0},{9,1},... | collective-permute-start | bytes 589832 | tf_op jit(solution)/shard_map/ppermute | solution.py:468
  7.2 10.2 %collective-permute-start.1 = (f32[24,16,128]{2,1,0:T(8,128)S(1)}, f32[24,16,128]{2,1,0:T(8,128)S(1)}, u32[]{:S(2)}, u32[]{:S(2)}) collective-permute-start(f32[24,16,128]{2,1,0:T(8,128)S(1)} %get-tuple-element.68), channel_id=1, source_target_pairs={{0,1},{1,0},{2,3},{3,2},{4,5},{5,4},{6,7},{7,6},{8,16},{9,17},{10,... | collective-permute-start | bytes 589832 | tf_op jit(solution)/shard_map/ppermute | solution.py:468
  7.2 10.2 %collective-permute-start.2 = (f32[24,16,128]{2,1,0:T(8,128)S(1)}, f32[24,16,128]{2,1,0:T(8,128)S(1)}, u32[]{:S(2)}, u32[]{:S(2)}) collective-permute-start(f32[24,16,128]{2,1,0:T(8,128)S(1)} %get-tuple-element.69), channel_id=1, source_target_pairs={{0,1},{1,0},{2,3},{3,2},{4,5},{5,4},{6,7},{7,6},{8,9},{9,8},{10,11... | collective-permute-start | bytes 589832 | tf_op jit(solution)/shard_map/ppermute | solution.py:468
  7.7 9.7 %collective-permute-start.3 = (f32[24,16,128]{2,1,0:T(8,128)S(1)}, f32[24,16,128]{2,1,0:T(8,128)S(1)}, u32[]{:S(2)}, u32[]{:S(2)}) collective-permute-start(f32[24,16,128]{2,1,0:T(8,128)S(1)} %get-tuple-element.70), channel_id=1, source_target_pairs={{0,8},{1,2},{2,1},{3,4},{4,3},{5,6},{6,5},{7,15},{8,0},{9,10},{10,... | collective-permute-start | bytes 589832 | tf_op jit(solution)/shard_map/ppermute | solution.py:468
  10.3 7.1 %copy-start = (f32[1,1,64,128]{3,2,1,0:T(8,128)S(1)}, f32[1,1,64,128]{3,2,1,0:T(8,128)}, u32[]{:S(2)}) copy-start(f32[1,1,64,128]{3,2,1,0:T(8,128)} %param.10) | copy-start | bytes 98308
  19.9 7.8 %collective-permute-start.4 = (f32[24,16,128]{2,1,0:T(8,128)S(1)}, f32[24,16,128]{2,1,0:T(8,128)S(1)}, u32[]{:S(2)}, u32[]{:S(2)}) collective-permute-start(f32[24,16,128]{2,1,0:T(8,128)S(1)} %get-tuple-element.85), channel_id=1, source_target_pairs={{0,8},{1,9},{2,10},{3,11},{4,12},{5,13},{6,14},{7,15},{8,0},{9,1},... | collective-permute-start | bytes 589832 | tf_op jit(solution)/shard_map/ppermute | solution.py:468
  20.0 7.7 %collective-permute-start.5 = (f32[24,16,128]{2,1,0:T(8,128)S(1)}, f32[24,16,128]{2,1,0:T(8,128)S(1)}, u32[]{:S(2)}, u32[]{:S(2)}) collective-permute-start(f32[24,16,128]{2,1,0:T(8,128)S(1)} %get-tuple-element.86), channel_id=1, source_target_pairs={{0,1},{1,0},{2,3},{3,2},{4,5},{5,4},{6,7},{7,6},{8,16},{9,17},{10,... | collective-permute-start | bytes 589832 | tf_op jit(solution)/shard_map/ppermute | solution.py:468
  21.3 6.4 %collective-permute-start.6 = (f32[24,16,128]{2,1,0:T(8,128)S(1)}, f32[24,16,128]{2,1,0:T(8,128)S(1)}, u32[]{:S(2)}, u32[]{:S(2)}) collective-permute-start(f32[24,16,128]{2,1,0:T(8,128)S(1)} %get-tuple-element.87), channel_id=1, source_target_pairs={{0,1},{1,0},{2,3},{3,2},{4,5},{5,4},{6,7},{7,6},{8,9},{9,8},{10,11... | collective-permute-start | bytes 589832 | tf_op jit(solution)/shard_map/ppermute | solution.py:468
  21.3 7.4 %collective-permute-start.7 = (f32[24,16,128]{2,1,0:T(8,128)S(1)}, f32[24,16,128]{2,1,0:T(8,128)S(1)}, u32[]{:S(2)}, u32[]{:S(2)}) collective-permute-start(f32[24,16,128]{2,1,0:T(8,128)S(1)} %get-tuple-element.88), channel_id=1, source_target_pairs={{0,8},{1,2},{2,1},{3,4},{4,3},{5,6},{6,5},{7,15},{8,0},{9,10},{10,... | collective-permute-start | bytes 589832 | tf_op jit(solution)/shard_map/ppermute | solution.py:468
  31.3 8.7 %collective-permute-start.8 = (f32[24,16,128]{2,1,0:T(8,128)S(1)}, f32[24,16,128]{2,1,0:T(8,128)S(1)}, u32[]{:S(2)}, u32[]{:S(2)}) collective-permute-start(f32[24,16,128]{2,1,0:T(8,128)S(1)} %get-tuple-element.95), channel_id=1, source_target_pairs={{0,8},{1,9},{2,10},{3,11},{4,12},{5,13},{6,14},{7,15},{8,0},{9,1},... | collective-permute-start | bytes 589832 | tf_op jit(solution)/shard_map/ppermute | solution.py:468
  32.5 7.6 %collective-permute-start.9 = (f32[24,16,128]{2,1,0:T(8,128)S(1)}, f32[24,16,128]{2,1,0:T(8,128)S(1)}, u32[]{:S(2)}, u32[]{:S(2)}) collective-permute-start(f32[24,16,128]{2,1,0:T(8,128)S(1)} %get-tuple-element.96), channel_id=1, source_target_pairs={{0,1},{1,0},{2,3},{3,2},{4,5},{5,4},{6,7},{7,6},{8,16},{9,17},{10,... | collective-permute-start | bytes 589832 | tf_op jit(solution)/shard_map/ppermute | solution.py:468
  32.5 7.6 %collective-permute-start.10 = (f32[24,16,128]{2,1,0:T(8,128)S(1)}, f32[24,16,128]{2,1,0:T(8,128)S(1)}, u32[]{:S(2)}, u32[]{:S(2)}) collective-permute-start(f32[24,16,128]{2,1,0:T(8,128)S(1)} %get-tuple-element.97), channel_id=1, source_target_pairs={{0,1},{1,0},{2,3},{3,2},{4,5},{5,4},{6,7},{7,6},{8,9},{9,8},{10,11... | collective-permute-start | bytes 589832 | tf_op jit(solution)/shard_map/ppermute | solution.py:468
  33.0 7.1 %collective-permute-start.11 = (f32[24,16,128]{2,1,0:T(8,128)S(1)}, f32[24,16,128]{2,1,0:T(8,128)S(1)}, u32[]{:S(2)}, u32[]{:S(2)}) collective-permute-start(f32[24,16,128]{2,1,0:T(8,128)S(1)} %get-tuple-element.98), channel_id=1, source_target_pairs={{0,8},{1,2},{2,1},{3,4},{4,3},{5,6},{6,5},{7,15},{8,0},{9,10},{10,... | collective-permute-start | bytes 589832 | tf_op jit(solution)/shard_map/ppermute | solution.py:468
  41.9 5.8 %collective-permute-start.12 = (f32[12,16,128]{2,1,0:T(8,128)S(1)}, f32[12,16,128]{2,1,0:T(8,128)S(1)}, u32[]{:S(2)}, u32[]{:S(2)}) collective-permute-start(f32[12,16,128]{2,1,0:T(8,128)S(1)} %get-tuple-element.102), channel_id=1, source_target_pairs={{0,8},{1,9},{2,10},{3,11},{4,12},{5,13},{6,14},{7,15},{8,0},{9,1},... | collective-permute-start | bytes 294920 | tf_op jit(solution)/shard_map/ppermute | solution.py:468
  43.1 4.6 %collective-permute-start.13 = (f32[12,16,128]{2,1,0:T(8,128)S(1)}, f32[12,16,128]{2,1,0:T(8,128)S(1)}, u32[]{:S(2)}, u32[]{:S(2)}) collective-permute-start(f32[12,16,128]{2,1,0:T(8,128)S(1)} %get-tuple-element.103), channel_id=1, source_target_pairs={{0,1},{1,0},{2,3},{3,2},{4,5},{5,4},{6,7},{7,6},{8,16},{9,17},{10,... | collective-permute-start | bytes 294920 | tf_op jit(solution)/shard_map/ppermute | solution.py:468
  43.5 4.3 %collective-permute-start.14 = (f32[12,16,128]{2,1,0:T(8,128)S(1)}, f32[12,16,128]{2,1,0:T(8,128)S(1)}, u32[]{:S(2)}, u32[]{:S(2)}) collective-permute-start(f32[12,16,128]{2,1,0:T(8,128)S(1)} %get-tuple-element.104), channel_id=1, source_target_pairs={{0,1},{1,0},{2,3},{3,2},{4,5},{5,4},{6,7},{7,6},{8,9},{9,8},{10,11... | collective-permute-start | bytes 294920 | tf_op jit(solution)/shard_map/ppermute | solution.py:468
  43.7 4.6 %collective-permute-start.15 = (f32[12,16,128]{2,1,0:T(8,128)S(1)}, f32[12,16,128]{2,1,0:T(8,128)S(1)}, u32[]{:S(2)}, u32[]{:S(2)}) collective-permute-start(f32[12,16,128]{2,1,0:T(8,128)S(1)} %get-tuple-element.105), channel_id=1, source_target_pairs={{0,8},{1,2},{2,1},{3,4},{4,3},{5,6},{6,5},{7,15},{8,0},{9,10},{10,... | collective-permute-start | bytes 294920 | tf_op jit(solution)/shard_map/ppermute | solution.py:468

commit v7 on v6

--- a/solution.py
+++ b/solution.py
@@ -18,8 +18,8 @@
 
 ROWS = 8
 FACES = 24
-WIDE = 32
-CHUNK = 8
+WIDE = 64
+CHUNK = 12
 EARLY = 16
 TILE_SCALE = 2.0**19
 VEC_SCALE = 256.0
@@ -51,7 +51,7 @@
 def shrunk(v, v8, peak, undo):
     up, down = vector_scales(peak)
     undo[...] = down
-    group = 8
+    group = 16
 
     def step(s, carry):
         part = pl.ds(s * group, group)
@@ -281,7 +281,7 @@
     half = (upper - lower) / 2.0
     centre = (upper + lower) / 2.0
     scale = (1.0 if order == 1 else 2.0) / half
-    group = 8
+    group = 16
 
     def step(s, carry):
         part = pl.ds(s * group, group)

time: 63.5 us -> 63.3 us (level)
  Pallas kernels: 34.2 us -> 33.4 us
  waiting for transfers between devices: 1.65 us -> 2.29 us
    ppermute x16, waiting for transfers between devices: 1.65 us -> 2.29 us  [pairs(): return lax.ppermute(x, ('gx', 'gy'), moves)]
  transfers between devices with their start and end apart: 16 -> 16, of which waited for: 3 -> 4; matrix products, arithmetic and copies ran while one was open for 0% -> 0% of each run, Pallas kernels for 33% -> 32%
where the time goes in v7:
time: 63.3 us; the launch traced here: 63.1 us
  Pallas kernels  33.4 us (53%)
  starting transfers between devices  14.8 us (23%)
  blocking collectives  11.7 us (18%)
  waiting for transfers between devices  2.29 us (4%)
  between operations  0.97 us (2%)
    ppermute x16, starting transfers between devices, pairs(): return lax.ppermute(x, ('gx', 'gy'), moves)  14.8 us
    all_to_all x1, blocking collectives, shards(): sums = lax.all_to_all(sums, ('gx', 'gy'), 0, 0)  11.7 us
    pallas_call x2, Pallas kernels, shards(): call(local_kernel, 'local%d' % (order + 1), [SM] + [VM] * 7, [vec, vec],...  11 us
    pallas_call x1, Pallas kernels, shards(): call(first_kernel, 'local_first', [SM] + [VM] * 4 + [HBM], [vec, vec, hig...  7.05 us
    pallas_call x3, Pallas kernels, shards(): call(functools.partial(next_kernel, order), 'finish%d' % order, [SM, SM,...  6.6 us
    pallas_call x1, Pallas kernels, shards(): call(begin_kernel, 'begin', [HBM] * 6, [pltpu.SMEM(rows.shape, jnp.int32)...  3.42 us
    pallas_call x1, Pallas kernels, shards(): call(functools.partial(end_kernel, nodes), 'end', [VM, VM], [jax.ShapeDty...  2.51 us
    ppermute x16, waiting for transfers between devices, pairs(): return lax.ppermute(x, ('gx', 'gy'), moves)  2.29 us
  transfers between devices with their start and end apart: 16, of which 4 were waited for; matrix products, arithmetic and copies ran while one was open for 0% of the time, Pallas kernels for 32%

profile of v7, /device:TPU:0, one launch (start us, length us, event | category | flops | bytes accessed | tf_op | source)
XLA Modules:
  0.0 63.1 jit_solution(2041712954899123001)
XLA Ops:
  0.6 3.4 %begin.1 = (s32[4,24]{1,0:T(4,128)S(4)}, s32[4,64]{1,0:T(4,128)S(4)}, f32[2]{0:T(128)S(4)}, s32[6]{0:T(128)S(4)}, bf16[2,24,128,128]{3,2,1,0:T(8,128)(2,1)S(1)},...) custom-call(s32[4,24]{1,0:T(4,128)} %bitcast.17, ...), custom_call_target="tpu_custom_call" | custom-call | flops 536870912 | bytes 8388608 | tf_op jit(solution)/shard_map/begin/pallas_call | solution.py:495
  4.1 3.1 %collective-permute-start = (f32[24,16,128]{2,1,0:T(8,128)S(1)}, f32[24,16,128]{2,1,0:T(8,128)S(1)}, u32[]{:S(2)}, u32[]{:S(2)}) collective-permute-start(f32[24,16,128]{2,1,0:T(8,128)S(1)} %get-tuple-element.67), channel_id=1, source_target_pairs={{0,8},{1,9},{2,10},{3,11},{4,12},{5,13},{6,14},{7,15},{8,0},{9,1},... | collective-permute-start | bytes 589832 | tf_op jit(solution)/shard_map/ppermute | solution.py:468
  7.2 0.5 collective-permute-start.2
  7.7 2.6 %collective-permute-start.3 = (f32[24,16,128]{2,1,0:T(8,128)S(1)}, f32[24,16,128]{2,1,0:T(8,128)S(1)}, u32[]{:S(2)}, u32[]{:S(2)}) collective-permute-start(f32[24,16,128]{2,1,0:T(8,128)S(1)} %get-tuple-element.70), channel_id=1, source_target_pairs={{0,8},{1,2},{2,1},{3,4},{4,3},{5,6},{6,5},{7,15},{8,0},{9,10},{10,... | collective-permute-start | bytes 589832 | tf_op jit(solution)/shard_map/ppermute | solution.py:468
  10.3 7.0 %local_first.1 = (f32[64,16,128]{2,1,0:T(8,128)S(1)}, f32[64,16,128]{2,1,0:T(8,128)S(1)}, bf16[64,4,128,128]{3,2,1,0:T(8,128)(2,1)S(1)}, f8e4m3fn[64,4,128,128]{...) custom-call(s32[4,64]{1,0:T(4,128)S(4)} %get-tuple-element.60.cols, ...), custom_call_target="tpu_custom_call" | custom-call | flops 1073741824 | bytes 16777216 | tf_op jit(solution)/shard_map/local_first/pallas_call | solution.py:511
  17.4 2.4 %finish1.1 = (f32[64,16,128]{2,1,0:T(8,128)S(1)}, bf16[64,32,128]{2,1,0:T(8,128)(2,1)S(1)}, f8e4m3fn[64,32,128]{2,1,0:T(32,128)(4,1)S(1)}, f32[16,128]{1,0:T(8,1...) custom-call(s32[4,24]{1,0:T(4,128)S(4)} %get-tuple-element.56.rows, ...), custom_call_target="tpu_custom_call" | custom-call | tf_op jit(solution)/shard_map/finish1/pallas_call | solution.py:525
  19.9 1.3 %collective-permute-start.5 = (f32[24,16,128]{2,1,0:T(8,128)S(1)}, f32[24,16,128]{2,1,0:T(8,128)S(1)}, u32[]{:S(2)}, u32[]{:S(2)}) collective-permute-start(f32[24,16,128]{2,1,0:T(8,128)S(1)} %get-tuple-element.86), channel_id=1, source_target_pairs={{0,1},{1,0},{2,3},{3,2},{4,5},{5,4},{6,7},{7,6},{8,16},{9,17},{10,... | collective-permute-start | bytes 589832 | tf_op jit(solution)/shard_map/ppermute | solution.py:468
  21.2 0.7 %collective-permute-start.7 = (f32[24,16,128]{2,1,0:T(8,128)S(1)}, f32[24,16,128]{2,1,0:T(8,128)S(1)}, u32[]{:S(2)}, u32[]{:S(2)}) collective-permute-start(f32[24,16,128]{2,1,0:T(8,128)S(1)} %get-tuple-element.88), channel_id=1, source_target_pairs={{0,8},{1,2},{2,1},{3,4},{4,3},{5,6},{6,5},{7,15},{8,0},{9,10},{10,... | collective-permute-start | bytes 589832 | tf_op jit(solution)/shard_map/ppermute | solution.py:468
  21.9 5.5 %local2.1 = (f32[64,16,128]{2,1,0:T(8,128)S(1)}, f32[64,16,128]{2,1,0:T(8,128)S(1)}) custom-call(s32[4,64]{1,0:T(4,128)S(4)} %get-tuple-element.60.cols, bf16[64,32,128]{2,1,0:T(8,128)(2,1)S(1)} %get-tuple-element.76.v2, f8e4m3fn[64,32,128]{2,1,0:T(32,128)(4,1)S(1)} %get-tuple-element.77.v8, f32[16,128]{1,0:T(8,128)S(1)} %get-tuple-element.78.undo, ...), custom_call_target="tpu_custom_call" | custom-call | flops 1073741824 | bytes 16777216 | tf_op jit(solution)/shard_map/local2/pallas_call | solution.py:534
  27.4 1.2 %collective-permute-done.7.refs_8_ = f32[24,16,128]{2,1,0:T(8,128)S(1)} collective-permute-done((f32[24,16,128]{2,1,0:T(8,128)S(1)}, f32[24,16,128]{2,1,0:T(8,128)S(1)}, u32[]{:S(2)}, u32[]{:S(2)}) %collective-permute-start.7) | collective-permute-done | bytes 196640 | tf_op jit(solution)/shard_map/ppermute | solution.py:468
  28.7 2.6 %finish2.1 = (f32[64,16,128]{2,1,0:T(8,128)S(1)}, bf16[64,32,128]{2,1,0:T(8,128)(2,1)S(1)}, f8e4m3fn[64,32,128]{2,1,0:T(32,128)(4,1)S(1)}, f32[16,128]{1,0:T(8,1...) custom-call(s32[4,24]{1,0:T(4,128)S(4)} %get-tuple-element.56.rows, ...), custom_call_target="tpu_custom_call" | custom-call | tf_op jit(solution)/shard_map/finish2/pallas_call | solution.py:525
  31.3 1.2 %collective-permute-start.8 = (f32[24,16,128]{2,1,0:T(8,128)S(1)}, f32[24,16,128]{2,1,0:T(8,128)S(1)}, u32[]{:S(2)}, u32[]{:S(2)}) collective-permute-start(f32[24,16,128]{2,1,0:T(8,128)S(1)} %get-tuple-element.95), channel_id=1, source_target_pairs={{0,8},{1,9},{2,10},{3,11},{4,12},{5,13},{6,14},{7,15},{8,0},{9,1},... | collective-permute-start | bytes 589832 | tf_op jit(solution)/shard_map/ppermute | solution.py:468
  32.5 0.5 collective-permute-start.10
  33.0 1.2 %collective-permute-start.11 = (f32[24,16,128]{2,1,0:T(8,128)S(1)}, f32[24,16,128]{2,1,0:T(8,128)S(1)}, u32[]{:S(2)}, u32[]{:S(2)}) collective-permute-start(f32[24,16,128]{2,1,0:T(8,128)S(1)} %get-tuple-element.98), channel_id=1, source_target_pairs={{0,8},{1,2},{2,1},{3,4},{4,3},{5,6},{6,5},{7,15},{8,0},{9,10},{10,... | collective-permute-start | bytes 589832 | tf_op jit(solution)/shard_map/ppermute | solution.py:468
  34.2 5.5 %local3.1 = (f32[64,16,128]{2,1,0:T(8,128)S(1)}, f32[64,16,128]{2,1,0:T(8,128)S(1)}) custom-call(s32[4,64]{1,0:T(4,128)S(4)} %get-tuple-element.60.cols, bf16[64,32,128]{2,1,0:T(8,128)(2,1)S(1)} %get-tuple-element.90.v2, f8e4m3fn[64,32,128]{2,1,0:T(32,128)(4,1)S(1)} %get-tuple-element.91.v8, f32[16,128]{1,0:T(8,128)S(1)} %get-tuple-element.92.undo, ...), custom_call_target="tpu_custom_call" | custom-call | flops 1073741824 | bytes 16777216 | tf_op jit(solution)/shard_map/local3/pallas_call | solution.py:534
  40.0 1.6 %finish3.1 = (f32[64,16,128]{2,1,0:T(8,128)S(1)}, bf16[64,32,128]{2,1,0:T(8,128)(2,1)S(1)}, f32[12,16,128]{2,1,0:T(8,128)S(1)}, f32[12,16,128]{2,1,0:T(8,128)S(1...) custom-call(s32[4,24]{1,0:T(4,128)S(4)} %get-tuple-element.56.rows, s32[6]{0:T(128)S(4)} %get-tuple-element.57.flags, ...), custom_call_target="tpu_custom_call" | custom-call | tf_op jit(solution)/shard_map/finish3/pallas_call | solution.py:525
  41.6 1.4 %collective-permute-start.12 = (f32[12,16,128]{2,1,0:T(8,128)S(1)}, f32[12,16,128]{2,1,0:T(8,128)S(1)}, u32[]{:S(2)}, u32[]{:S(2)}) collective-permute-start(f32[12,16,128]{2,1,0:T(8,128)S(1)} %get-tuple-element.102), channel_id=1, source_target_pairs={{0,8},{1,9},{2,10},{3,11},{4,12},{5,13},{6,14},{7,15},{8,0},{9,1},... | collective-permute-start | bytes 294920 | tf_op jit(solution)/shard_map/ppermute | solution.py:468
  43.0 0.4 collective-permute-start.14
  43.4 1.6 %collective-permute-start.15 = (f32[12,16,128]{2,1,0:T(8,128)S(1)}, f32[12,16,128]{2,1,0:T(8,128)S(1)}, u32[]{:S(2)}, u32[]{:S(2)}) collective-permute-start(f32[12,16,128]{2,1,0:T(8,128)S(1)} %get-tuple-element.105), channel_id=1, source_target_pairs={{0,8},{1,2},{2,1},{3,4},{4,3},{5,6},{6,5},{7,15},{8,0},{9,10},{10,... | collective-permute-start | bytes 294920 | tf_op jit(solution)/shard_map/ppermute | solution.py:468
  45.1 2.2 %project.1 = (f32[16,16]{1,0:T(8,128)S(1)}, bf16[2,12,32,128]{3,2,1,0:T(8,128)(2,1)S(1)}, f32[16,16]{1,0:T(8,128)S(1)}) custom-call(s32[4,24]{1,0:T(4,128)S(4)} %get-tuple-element.56.rows, s32[4,64]{1,0:T(4,128)S(4)} %get-tuple-element.60.cols, f32[64,16,128]{2,1,0:T(8,128)S(1)} %get-tuple-element.100.v, bf16[64,32,128]{2,1,0:T(8,128)(2,1)S(1)} %get-tuple-element.99.v2, ...), custom_call_target="tpu_custom_call" | custom-call | flops 268435456 | bytes 8388608 | tf_op jit(solution)/shard_map/project/pallas_call | solution.py:539
  47.3 0.7 %collective-permute-done.15.yo = f32[12,16,128]{2,1,0:T(8,128)S(1)} collective-permute-done((f32[12,16,128]{2,1,0:T(8,128)S(1)}, f32[12,16,128]{2,1,0:T(8,128)S(1)}, u32[]{:S(2)}, u32[]{:S(2)}) %collective-permute-start.15) | collective-permute-done | bytes 98336 | tf_op jit(solution)/shard_map/ppermute | solution.py:468
  48.1 0.6 %project_faces.1 = f32[32,4,128]{2,1,0:T(4,128)S(1)} custom-call(s32[4,24]{1,0:T(4,128)S(4)} %get-tuple-element.56.rows, s32[6]{0:T(128)S(4)} %get-tuple-element.57.flags, bf16[64,32,128]{2,1,0:T(8,128)(2,1)S(1)} %get-tuple-element.99.v2, bf16[2,12,32,128]{3,2,1,0:T(8,128)(2,1)S(1)} %get-tuple-element.101.over, ...), custom_call_target="tpu_custom_call" | custom-call | tf_op jit(solution)/shard_map/project_faces/pallas_call | solution.py:545
  48.7 11.7 %all_to_all.5.sums = f32[32,4,128]{2,1,0:T(4,128)S(1)} all-to-all(f32[32,4,128]{2,1,0:T(4,128)S(1)} %project_faces.1), channel_id=1, replica_groups=mesh['gx'=4,'gy'=8] {'gx','gy'}, dimensions={0} | all-to-all | bytes 131072 | tf_op jit(solution)/shard_map/all_to_all | solution.py:548
  60.4 2.5 %end.1 = (f32[64,16,128]{2,1,0:T(8,128)}, f32[16,16]{1,0:T(8,128)}) custom-call(f32[32,4,128]{2,1,0:T(4,128)S(1)} %all_to_all.5.sums, bf16[64,32,128]{2,1,0:T(8,128)(2,1)S(1)} %get-tuple-element.99.v2), custom_call_target="tpu_custom_call" | custom-call | tf_op jit(solution)/shard_map/end/pallas_call | solution.py:549
  (21 shorter events, 0.5 us)
Async XLA Ops:
  4.1 13.3 %collective-permute-start = (f32[24,16,128]{2,1,0:T(8,128)S(1)}, f32[24,16,128]{2,1,0:T(8,128)S(1)}, u32[]{:S(2)}, u32[]{:S(2)}) collective-permute-start(f32[24,16,128]{2,1,0:T(8,128)S(1)} %get-tuple-element.67), channel_id=1, source_target_pairs={{0,8},{1,9},{2,10},{3,11},{4,12},{5,13},{6,14},{7,15},{8,0},{9,1},... | collective-permute-start | bytes 589832 | tf_op jit(solution)/shard_map/ppermute | solution.py:468
  7.2 10.2 %collective-permute-start.1 = (f32[24,16,128]{2,1,0:T(8,128)S(1)}, f32[24,16,128]{2,1,0:T(8,128)S(1)}, u32[]{:S(2)}, u32[]{:S(2)}) collective-permute-start(f32[24,16,128]{2,1,0:T(8,128)S(1)} %get-tuple-element.68), channel_id=1, source_target_pairs={{0,1},{1,0},{2,3},{3,2},{4,5},{5,4},{6,7},{7,6},{8,16},{9,17},{10,... | collective-permute-start | bytes 589832 | tf_op jit(solution)/shard_map/ppermute | solution.py:468
  7.2 10.2 %collective-permute-start.2 = (f32[24,16,128]{2,1,0:T(8,128)S(1)}, f32[24,16,128]{2,1,0:T(8,128)S(1)}, u32[]{:S(2)}, u32[]{:S(2)}) collective-permute-start(f32[24,16,128]{2,1,0:T(8,128)S(1)} %get-tuple-element.69), channel_id=1, source_target_pairs={{0,1},{1,0},{2,3},{3,2},{4,5},{5,4},{6,7},{7,6},{8,9},{9,8},{10,11... | collective-permute-start | bytes 589832 | tf_op jit(solution)/shard_map/ppermute | solution.py:468
  7.7 9.7 %collective-permute-start.3 = (f32[24,16,128]{2,1,0:T(8,128)S(1)}, f32[24,16,128]{2,1,0:T(8,128)S(1)}, u32[]{:S(2)}, u32[]{:S(2)}) collective-permute-start(f32[24,16,128]{2,1,0:T(8,128)S(1)} %get-tuple-element.70), channel_id=1, source_target_pairs={{0,8},{1,2},{2,1},{3,4},{4,3},{5,6},{6,5},{7,15},{8,0},{9,10},{10,... | collective-permute-start | bytes 589832 | tf_op jit(solution)/shard_map/ppermute | solution.py:468
  10.3 7.1 %copy-start = (f32[1,1,64,128]{3,2,1,0:T(8,128)S(1)}, f32[1,1,64,128]{3,2,1,0:T(8,128)}, u32[]{:S(2)}) copy-start(f32[1,1,64,128]{3,2,1,0:T(8,128)} %param.10) | copy-start | bytes 98308
  19.8 7.6 %collective-permute-start.4 = (f32[24,16,128]{2,1,0:T(8,128)S(1)}, f32[24,16,128]{2,1,0:T(8,128)S(1)}, u32[]{:S(2)}, u32[]{:S(2)}) collective-permute-start(f32[24,16,128]{2,1,0:T(8,128)S(1)} %get-tuple-element.85), channel_id=1, source_target_pairs={{0,8},{1,9},{2,10},{3,11},{4,12},{5,13},{6,14},{7,15},{8,0},{9,1},... | collective-permute-start | bytes 589832 | tf_op jit(solution)/shard_map/ppermute | solution.py:468
  19.9 7.5 %collective-permute-start.5 = (f32[24,16,128]{2,1,0:T(8,128)S(1)}, f32[24,16,128]{2,1,0:T(8,128)S(1)}, u32[]{:S(2)}, u32[]{:S(2)}) collective-permute-start(f32[24,16,128]{2,1,0:T(8,128)S(1)} %get-tuple-element.86), channel_id=1, source_target_pairs={{0,1},{1,0},{2,3},{3,2},{4,5},{5,4},{6,7},{7,6},{8,16},{9,17},{10,... | collective-permute-start | bytes 589832 | tf_op jit(solution)/shard_map/ppermute | solution.py:468
  21.2 6.2 %collective-permute-start.6 = (f32[24,16,128]{2,1,0:T(8,128)S(1)}, f32[24,16,128]{2,1,0:T(8,128)S(1)}, u32[]{:S(2)}, u32[]{:S(2)}) collective-permute-start(f32[24,16,128]{2,1,0:T(8,128)S(1)} %get-tuple-element.87), channel_id=1, source_target_pairs={{0,1},{1,0},{2,3},{3,2},{4,5},{5,4},{6,7},{7,6},{8,9},{9,8},{10,11... | collective-permute-start | bytes 589832 | tf_op jit(solution)/shard_map/ppermute | solution.py:468
  21.2 7.4 %collective-permute-start.7 = (f32[24,16,128]{2,1,0:T(8,128)S(1)}, f32[24,16,128]{2,1,0:T(8,128)S(1)}, u32[]{:S(2)}, u32[]{:S(2)}) collective-permute-start(f32[24,16,128]{2,1,0:T(8,128)S(1)} %get-tuple-element.88), channel_id=1, source_target_pairs={{0,8},{1,2},{2,1},{3,4},{4,3},{5,6},{6,5},{7,15},{8,0},{9,10},{10,... | collective-permute-start | bytes 589832 | tf_op jit(solution)/shard_map/ppermute | solution.py:468
  31.3 8.4 %collective-permute-start.8 = (f32[24,16,128]{2,1,0:T(8,128)S(1)}, f32[24,16,128]{2,1,0:T(8,128)S(1)}, u32[]{:S(2)}, u32[]{:S(2)}) collective-permute-start(f32[24,16,128]{2,1,0:T(8,128)S(1)} %get-tuple-element.95), channel_id=1, source_target_pairs={{0,8},{1,9},{2,10},{3,11},{4,12},{5,13},{6,14},{7,15},{8,0},{9,1},... | collective-permute-start | bytes 589832 | tf_op jit(solution)/shard_map/ppermute | solution.py:468
  32.5 7.2 %collective-permute-start.9 = (f32[24,16,128]{2,1,0:T(8,128)S(1)}, f32[24,16,128]{2,1,0:T(8,128)S(1)}, u32[]{:S(2)}, u32[]{:S(2)}) collective-permute-start(f32[24,16,128]{2,1,0:T(8,128)S(1)} %get-tuple-element.96), channel_id=1, source_target_pairs={{0,1},{1,0},{2,3},{3,2},{4,5},{5,4},{6,7},{7,6},{8,16},{9,17},{10,... | collective-permute-start | bytes 589832 | tf_op jit(solution)/shard_map/ppermute | solution.py:468
  32.5 7.2 %collective-permute-start.10 = (f32[24,16,128]{2,1,0:T(8,128)S(1)}, f32[24,16,128]{2,1,0:T(8,128)S(1)}, u32[]{:S(2)}, u32[]{:S(2)}) collective-permute-start(f32[24,16,128]{2,1,0:T(8,128)S(1)} %get-tuple-element.97), channel_id=1, source_target_pairs={{0,1},{1,0},{2,3},{3,2},{4,5},{5,4},{6,7},{7,6},{8,9},{9,8},{10,11... | collective-permute-start | bytes 589832 | tf_op jit(solution)/shard_map/ppermute | solution.py:468
  33.0 7.0 %collective-permute-start.11 = (f32[24,16,128]{2,1,0:T(8,128)S(1)}, f32[24,16,128]{2,1,0:T(8,128)S(1)}, u32[]{:S(2)}, u32[]{:S(2)}) collective-permute-start(f32[24,16,128]{2,1,0:T(8,128)S(1)} %get-tuple-element.98), channel_id=1, source_target_pairs={{0,8},{1,2},{2,1},{3,4},{4,3},{5,6},{6,5},{7,15},{8,0},{9,10},{10,... | collective-permute-start | bytes 589832 | tf_op jit(solution)/shard_map/ppermute | solution.py:468
  41.6 5.7 %collective-permute-start.12 = (f32[12,16,128]{2,1,0:T(8,128)S(1)}, f32[12,16,128]{2,1,0:T(8,128)S(1)}, u32[]{:S(2)}, u32[]{:S(2)}) collective-permute-start(f32[12,16,128]{2,1,0:T(8,128)S(1)} %get-tuple-element.102), channel_id=1, source_target_pairs={{0,8},{1,9},{2,10},{3,11},{4,12},{5,13},{6,14},{7,15},{8,0},{9,1},... | collective-permute-start | bytes 294920 | tf_op jit(solution)/shard_map/ppermute | solution.py:468
  42.9 4.4 %collective-permute-start.13 = (f32[12,16,128]{2,1,0:T(8,128)S(1)}, f32[12,16,128]{2,1,0:T(8,128)S(1)}, u32[]{:S(2)}, u32[]{:S(2)}) collective-permute-start(f32[12,16,128]{2,1,0:T(8,128)S(1)} %get-tuple-element.103), channel_id=1, source_target_pairs={{0,1},{1,0},{2,3},{3,2},{4,5},{5,4},{6,7},{7,6},{8,16},{9,17},{10,... | collective-permute-start | bytes 294920 | tf_op jit(solution)/shard_map/ppermute | solution.py:468
  43.0 4.3 %collective-permute-start.14 = (f32[12,16,128]{2,1,0:T(8,128)S(1)}, f32[12,16,128]{2,1,0:T(8,128)S(1)}, u32[]{:S(2)}, u32[]{:S(2)}) collective-permute-start(f32[12,16,128]{2,1,0:T(8,128)S(1)} %get-tuple-element.104), channel_id=1, source_target_pairs={{0,1},{1,0},{2,3},{3,2},{4,5},{5,4},{6,7},{7,6},{8,9},{9,8},{10,11... | collective-permute-start | bytes 294920 | tf_op jit(solution)/shard_map/ppermute | solution.py:468
  43.4 4.6 %collective-permute-start.15 = (f32[12,16,128]{2,1,0:T(8,128)S(1)}, f32[12,16,128]{2,1,0:T(8,128)S(1)}, u32[]{:S(2)}, u32[]{:S(2)}) collective-permute-start(f32[12,16,128]{2,1,0:T(8,128)S(1)} %get-tuple-element.105), channel_id=1, source_target_pairs={{0,8},{1,2},{2,1},{3,4},{4,3},{5,6},{6,5},{7,15},{8,0},{9,10},{10,... | collective-permute-start | bytes 294920 | tf_op jit(solution)/shard_map/ppermute | solution.py:468

commit v8 on v7

--- a/solution.py
+++ b/solution.py
@@ -228,7 +228,8 @@
     lax.fori_loop(0, copies, step, 0)
 
 
-def local_kernel(cols, v2, v8, undo, th, tl, thT, tlT, wf, wb):
+def local_kernel(cols, v, peak, v2, th, tl, thT, tlT, wf, wb, v8, undo):
+    shrunk(v, v8, peak[...], undo)
     wb[...] = jnp.zeros_like(wb)
 
     def step(c, carry):
@@ -271,7 +272,7 @@
     else:
         (v, older, wf, wb, diag, ux, lx, uy, ly, dh, dl, ch, cl, *outs, acc) = refs
     if order < 3:
-        new, new2, new8, undo, *sends = outs
+        new, new2, top, *sends = outs
     else:
         new, new2, *sends = outs
     acc[...] = jnp.zeros_like(acc)
@@ -281,7 +282,7 @@
     half = (upper - lower) / 2.0
     centre = (upper + lower) / 2.0
     scale = (1.0 if order == 1 else 2.0) / half
-    group = 16
+    group = 32
 
     def step(s, carry):
         part = pl.ds(s * group, group)
@@ -296,7 +297,7 @@
 
     peak = lax.fori_loop(0, v.shape[0] // group, step, jnp.zeros((16, 128), F32))
     if order < 3:
-        shrunk(new, new8, peak, undo)
+        top[...] = peak
         leave(new, new2, rows, flags, ch, cl, sends)
         return
     last_sends(new, new2, rows, flags, ch, sends)
@@ -521,7 +522,7 @@
     for order in (1, 2, 3):
         carried = (x,) if older is None else (x, older)
         last = order == 3
-        outs = [vec, vec2] + ([half_face] * 4 if last else [vec8, scale] + [face] * 4)
+        outs = [vec, vec2] + ([half_face] * 4 if last else [scale] + [face] * 4)
         new, new2, *sends = call(
             functools.partial(next_kernel, order), "finish%d" % order,
             [SM, SM, SM] + [VM] * (11 + len(carried)), outs,
@@ -529,12 +530,13 @@
         )(rows, flags, filter_bounds, *carried, wf, wb, diag, *received, dh, dl, ch, cl)
         x, x2, older = new, new2, x
         if not last:
-            x8, undo, *sends = sends
+            peak, *sends = sends
             received = exchange(sends)
             wf, wb = call(
                 local_kernel, "local%d" % (order + 1), [SM] + [VM] * 7, [vec, vec],
+                [pltpu.VMEM((count, 2 * width, tile), F8), pltpu.VMEM((width, tile), F32)],
                 flops=local_flops, nbytes=4 * stored.size,
-            )(cols, x2, x8, undo, th, tl, thT, tlT)
+            )(cols, x, peak, x2, th, tl, thT, tlT)
     received = exchange(sends)
     part, over, gram = call(
         project_kernel, "project", [SM, SM] + [VM] * 5,

time: 63.3 us -> 62.6 us (0.989)
    pallas_call x3, Pallas kernels: 6.6 us -> 5.9 us  [shards(): call(functools.partial(next_kernel, order), 'finish%d' % order, [SM, SM,...]
  transfers between devices with their start and end apart: 16 -> 16, of which waited for: 4 -> 3; matrix products, arithmetic and copies ran while one was open for 0% -> 0% of each run, Pallas kernels for 32% -> 33%
where the time goes in v8:
time: 62.6 us; the launch traced here: 62.4 us
  Pallas kernels  33.2 us (53%)
  starting transfers between devices  14.6 us (23%)
  blocking collectives  11.8 us (19%)
  waiting for transfers between devices  1.82 us (3%)
  between operations  0.98 us (2%)
    ppermute x16, starting transfers between devices, pairs(): return lax.ppermute(x, ('gx', 'gy'), moves)  14.6 us
    all_to_all x1, blocking collectives, shards(): sums = lax.all_to_all(sums, ('gx', 'gy'), 0, 0)  11.8 us
    pallas_call x2, Pallas kernels, shards(): call(local_kernel, 'local%d' % (order + 1), [SM] + [VM] * 7, [vec, vec],...  11.6 us
    pallas_call x1, Pallas kernels, shards(): call(first_kernel, 'local_first', [SM] + [VM] * 4 + [HBM], [vec, vec, hig...  7.04 us
    pallas_call x3, Pallas kernels, shards(): call(functools.partial(next_kernel, order), 'finish%d' % order, [SM, SM,...  5.9 us
    pallas_call x1, Pallas kernels, shards(): call(begin_kernel, 'begin', [HBM] * 6, [pltpu.SMEM(rows.shape, jnp.int32)...  3.42 us
    pallas_call x1, Pallas kernels, shards(): call(functools.partial(end_kernel, nodes), 'end', [VM, VM], [jax.ShapeDty...  2.5 us
    pallas_call x1, Pallas kernels, shards(): call(project_kernel, 'project', [SM, SM] + [VM] * 5, [square, in_vmem((2,...  2.17 us
  transfers between devices with their start and end apart: 16, of which 3 were waited for; matrix products, arithmetic and copies ran while one was open for 0% of the time, Pallas kernels for 33%

profile of v8, /device:TPU:0, one launch (start us, length us, event | category | flops | bytes accessed | tf_op | source)
XLA Modules:
  0.0 62.4 jit_solution(4312208020279094166)
XLA Ops:
  0.6 3.4 %begin.1 = (s32[4,24]{1,0:T(4,128)S(4)}, s32[4,64]{1,0:T(4,128)S(4)}, f32[2]{0:T(128)S(4)}, s32[6]{0:T(128)S(4)}, bf16[2,24,128,128]{3,2,1,0:T(8,128)(2,1)S(1)},...) custom-call(s32[4,24]{1,0:T(4,128)} %bitcast.17, ...), custom_call_target="tpu_custom_call" | custom-call | flops 536870912 | bytes 8388608 | tf_op jit(solution)/shard_map/begin/pallas_call | solution.py:496
  4.1 3.1 %collective-permute-start = (f32[24,16,128]{2,1,0:T(8,128)S(1)}, f32[24,16,128]{2,1,0:T(8,128)S(1)}, u32[]{:S(2)}, u32[]{:S(2)}) collective-permute-start(f32[24,16,128]{2,1,0:T(8,128)S(1)} %get-tuple-element.65), channel_id=1, source_target_pairs={{0,8},{1,9},{2,10},{3,11},{4,12},{5,13},{6,14},{7,15},{8,0},{9,1},... | collective-permute-start | bytes 589832 | tf_op jit(solution)/shard_map/ppermute | solution.py:469
  7.2 0.5 collective-permute-start.2
  7.7 2.6 %collective-permute-start.3 = (f32[24,16,128]{2,1,0:T(8,128)S(1)}, f32[24,16,128]{2,1,0:T(8,128)S(1)}, u32[]{:S(2)}, u32[]{:S(2)}) collective-permute-start(f32[24,16,128]{2,1,0:T(8,128)S(1)} %get-tuple-element.68), channel_id=1, source_target_pairs={{0,8},{1,2},{2,1},{3,4},{4,3},{5,6},{6,5},{7,15},{8,0},{9,10},{10,... | collective-permute-start | bytes 589832 | tf_op jit(solution)/shard_map/ppermute | solution.py:469
  10.3 7.0 %local_first.1 = (f32[64,16,128]{2,1,0:T(8,128)S(1)}, f32[64,16,128]{2,1,0:T(8,128)S(1)}, bf16[64,4,128,128]{3,2,1,0:T(8,128)(2,1)S(1)}, f8e4m3fn[64,4,128,128]{...) custom-call(s32[4,64]{1,0:T(4,128)S(4)} %get-tuple-element.58.cols, ...), custom_call_target="tpu_custom_call" | custom-call | flops 1073741824 | bytes 16777216 | tf_op jit(solution)/shard_map/local_first/pallas_call | solution.py:512
  17.4 2.2 %finish1.1 = (f32[64,16,128]{2,1,0:T(8,128)S(1)}, bf16[64,32,128]{2,1,0:T(8,128)(2,1)S(1)}, f32[16,128]{1,0:T(8,128)S(1)}, f32[24,16,128]{2,1,0:T(8,128)S(1)}, f...) custom-call(s32[4,24]{1,0:T(4,128)S(4)} %get-tuple-element.54.rows, ...), custom_call_target="tpu_custom_call" | custom-call | tf_op jit(solution)/shard_map/finish1/pallas_call | solution.py:526
  19.7 1.3 %collective-permute-start.5 = (f32[24,16,128]{2,1,0:T(8,128)S(1)}, f32[24,16,128]{2,1,0:T(8,128)S(1)}, u32[]{:S(2)}, u32[]{:S(2)}) collective-permute-start(f32[24,16,128]{2,1,0:T(8,128)S(1)} %get-tuple-element.83), channel_id=1, source_target_pairs={{0,1},{1,0},{2,3},{3,2},{4,5},{5,4},{6,7},{7,6},{8,16},{9,17},{10,... | collective-permute-start | bytes 589832 | tf_op jit(solution)/shard_map/ppermute | solution.py:469
  21.0 0.7 %collective-permute-start.7 = (f32[24,16,128]{2,1,0:T(8,128)S(1)}, f32[24,16,128]{2,1,0:T(8,128)S(1)}, u32[]{:S(2)}, u32[]{:S(2)}) collective-permute-start(f32[24,16,128]{2,1,0:T(8,128)S(1)} %get-tuple-element.85), channel_id=1, source_target_pairs={{0,8},{1,2},{2,1},{3,4},{4,3},{5,6},{6,5},{7,15},{8,0},{9,10},{10,... | collective-permute-start | bytes 589832 | tf_op jit(solution)/shard_map/ppermute | solution.py:469
  21.7 5.7 %local2.1 = (f32[64,16,128]{2,1,0:T(8,128)S(1)}, f32[64,16,128]{2,1,0:T(8,128)S(1)}) custom-call(s32[4,64]{1,0:T(4,128)S(4)} %get-tuple-element.58.cols, f32[64,16,128]{2,1,0:T(8,128)S(1)} %get-tuple-element.73.v.refs_0_.refs_1_, f32[16,128]{1,0:T(8,128)S(1)} %get-tuple-element.74.peak, bf16[64,32,128]{2,1,0:T(8,128)(2,1)S(1)} %get-tuple-element.75.v2, ...), custom_call_target="tpu_custom_call" | custom-call | flops 1073741824 | bytes 16777216 | tf_op jit(solution)/shard_map/local2/pallas_call | solution.py:535
  27.4 1.0 %collective-permute-done.7.refs_8_ = f32[24,16,128]{2,1,0:T(8,128)S(1)} collective-permute-done((f32[24,16,128]{2,1,0:T(8,128)S(1)}, f32[24,16,128]{2,1,0:T(8,128)S(1)}, u32[]{:S(2)}, u32[]{:S(2)}) %collective-permute-start.7) | collective-permute-done | bytes 196640 | tf_op jit(solution)/shard_map/ppermute | solution.py:469
  28.4 2.2 %finish2.1 = (f32[64,16,128]{2,1,0:T(8,128)S(1)}, bf16[64,32,128]{2,1,0:T(8,128)(2,1)S(1)}, f32[16,128]{1,0:T(8,128)S(1)}, f32[24,16,128]{2,1,0:T(8,128)S(1)}, f...) custom-call(s32[4,24]{1,0:T(4,128)S(4)} %get-tuple-element.54.rows, ...), custom_call_target="tpu_custom_call" | custom-call | tf_op jit(solution)/shard_map/finish2/pallas_call | solution.py:526
  30.6 1.2 %collective-permute-start.8 = (f32[24,16,128]{2,1,0:T(8,128)S(1)}, f32[24,16,128]{2,1,0:T(8,128)S(1)}, u32[]{:S(2)}, u32[]{:S(2)}) collective-permute-start(f32[24,16,128]{2,1,0:T(8,128)S(1)} %get-tuple-element.91), channel_id=1, source_target_pairs={{0,8},{1,9},{2,10},{3,11},{4,12},{5,13},{6,14},{7,15},{8,0},{9,1},... | collective-permute-start | bytes 589832 | tf_op jit(solution)/shard_map/ppermute | solution.py:469
  31.8 0.5 collective-permute-start.10
  32.3 1.4 %collective-permute-start.11 = (f32[24,16,128]{2,1,0:T(8,128)S(1)}, f32[24,16,128]{2,1,0:T(8,128)S(1)}, u32[]{:S(2)}, u32[]{:S(2)}) collective-permute-start(f32[24,16,128]{2,1,0:T(8,128)S(1)} %get-tuple-element.94), channel_id=1, source_target_pairs={{0,8},{1,2},{2,1},{3,4},{4,3},{5,6},{6,5},{7,15},{8,0},{9,10},{10,... | collective-permute-start | bytes 589832 | tf_op jit(solution)/shard_map/ppermute | solution.py:469
  33.7 5.9 %local3.1 = (f32[64,16,128]{2,1,0:T(8,128)S(1)}, f32[64,16,128]{2,1,0:T(8,128)S(1)}) custom-call(s32[4,64]{1,0:T(4,128)S(4)} %get-tuple-element.58.cols, f32[64,16,128]{2,1,0:T(8,128)S(1)} %get-tuple-element.86.v.refs_0_, f32[16,128]{1,0:T(8,128)S(1)} %get-tuple-element.87.peak, bf16[64,32,128]{2,1,0:T(8,128)(2,1)S(1)} %get-tuple-element.88.v2, ...), custom_call_target="tpu_custom_call" | custom-call | flops 1073741824 | bytes 16777216 | tf_op jit(solution)/shard_map/local3/pallas_call | solution.py:535
  39.7 1.6 %finish3.1 = (f32[64,16,128]{2,1,0:T(8,128)S(1)}, bf16[64,32,128]{2,1,0:T(8,128)(2,1)S(1)}, f32[12,16,128]{2,1,0:T(8,128)S(1)}, f32[12,16,128]{2,1,0:T(8,128)S(1...) custom-call(s32[4,24]{1,0:T(4,128)S(4)} %get-tuple-element.54.rows, s32[6]{0:T(128)S(4)} %get-tuple-element.55.flags, ...), custom_call_target="tpu_custom_call" | custom-call | tf_op jit(solution)/shard_map/finish3/pallas_call | solution.py:526
  41.2 1.0 %collective-permute-start.12 = (f32[12,16,128]{2,1,0:T(8,128)S(1)}, f32[12,16,128]{2,1,0:T(8,128)S(1)}, u32[]{:S(2)}, u32[]{:S(2)}) collective-permute-start(f32[12,16,128]{2,1,0:T(8,128)S(1)} %get-tuple-element.98), channel_id=1, source_target_pairs={{0,8},{1,9},{2,10},{3,11},{4,12},{5,13},{6,14},{7,15},{8,0},{9,1},... | collective-permute-start | bytes 294920 | tf_op jit(solution)/shard_map/ppermute | solution.py:469
  42.2 0.4 collective-permute-start.13
  42.7 1.6 %collective-permute-start.15 = (f32[12,16,128]{2,1,0:T(8,128)S(1)}, f32[12,16,128]{2,1,0:T(8,128)S(1)}, u32[]{:S(2)}, u32[]{:S(2)}) collective-permute-start(f32[12,16,128]{2,1,0:T(8,128)S(1)} %get-tuple-element.101), channel_id=1, source_target_pairs={{0,8},{1,2},{2,1},{3,4},{4,3},{5,6},{6,5},{7,15},{8,0},{9,10},{10,... | collective-permute-start | bytes 294920 | tf_op jit(solution)/shard_map/ppermute | solution.py:469
  44.4 2.2 %project.1 = (f32[16,16]{1,0:T(8,128)S(1)}, bf16[2,12,32,128]{3,2,1,0:T(8,128)(2,1)S(1)}, f32[16,16]{1,0:T(8,128)S(1)}) custom-call(s32[4,24]{1,0:T(4,128)S(4)} %get-tuple-element.54.rows, s32[4,64]{1,0:T(4,128)S(4)} %get-tuple-element.58.cols, f32[64,16,128]{2,1,0:T(8,128)S(1)} %get-tuple-element.96.v, bf16[64,32,128]{2,1,0:T(8,128)(2,1)S(1)} %get-tuple-element.95.v2, ...), custom_call_target="tpu_custom_call" | custom-call | flops 268435456 | bytes 8388608 | tf_op jit(solution)/shard_map/project/pallas_call | solution.py:541
  46.6 0.7 %collective-permute-done.15.yo = f32[12,16,128]{2,1,0:T(8,128)S(1)} collective-permute-done((f32[12,16,128]{2,1,0:T(8,128)S(1)}, f32[12,16,128]{2,1,0:T(8,128)S(1)}, u32[]{:S(2)}, u32[]{:S(2)}) %collective-permute-start.15) | collective-permute-done | bytes 98336 | tf_op jit(solution)/shard_map/ppermute | solution.py:469
  47.3 0.6 %project_faces.1 = f32[32,4,128]{2,1,0:T(4,128)S(1)} custom-call(s32[4,24]{1,0:T(4,128)S(4)} %get-tuple-element.54.rows, s32[6]{0:T(128)S(4)} %get-tuple-element.55.flags, bf16[64,32,128]{2,1,0:T(8,128)(2,1)S(1)} %get-tuple-element.95.v2, bf16[2,12,32,128]{3,2,1,0:T(8,128)(2,1)S(1)} %get-tuple-element.97.over, ...), custom_call_target="tpu_custom_call" | custom-call | tf_op jit(solution)/shard_map/project_faces/pallas_call | solution.py:547
  48.0 11.8 %all_to_all.5.sums = f32[32,4,128]{2,1,0:T(4,128)S(1)} all-to-all(f32[32,4,128]{2,1,0:T(4,128)S(1)} %project_faces.1), channel_id=1, replica_groups=mesh['gx'=4,'gy'=8] {'gx','gy'}, dimensions={0} | all-to-all | bytes 131072 | tf_op jit(solution)/shard_map/all_to_all | solution.py:550
  59.7 2.5 %end.1 = (f32[64,16,128]{2,1,0:T(8,128)}, f32[16,16]{1,0:T(8,128)}) custom-call(f32[32,4,128]{2,1,0:T(4,128)S(1)} %all_to_all.5.sums, bf16[64,32,128]{2,1,0:T(8,128)(2,1)S(1)} %get-tuple-element.95.v2), custom_call_target="tpu_custom_call" | custom-call | tf_op jit(solution)/shard_map/end/pallas_call | solution.py:551
  (21 shorter events, 0.3 us)
Async XLA Ops:
  4.1 13.3 %collective-permute-start = (f32[24,16,128]{2,1,0:T(8,128)S(1)}, f32[24,16,128]{2,1,0:T(8,128)S(1)}, u32[]{:S(2)}, u32[]{:S(2)}) collective-permute-start(f32[24,16,128]{2,1,0:T(8,128)S(1)} %get-tuple-element.65), channel_id=1, source_target_pairs={{0,8},{1,9},{2,10},{3,11},{4,12},{5,13},{6,14},{7,15},{8,0},{9,1},... | collective-permute-start | bytes 589832 | tf_op jit(solution)/shard_map/ppermute | solution.py:469
  7.2 10.2 %collective-permute-start.1 = (f32[24,16,128]{2,1,0:T(8,128)S(1)}, f32[24,16,128]{2,1,0:T(8,128)S(1)}, u32[]{:S(2)}, u32[]{:S(2)}) collective-permute-start(f32[24,16,128]{2,1,0:T(8,128)S(1)} %get-tuple-element.66), channel_id=1, source_target_pairs={{0,1},{1,0},{2,3},{3,2},{4,5},{5,4},{6,7},{7,6},{8,16},{9,17},{10,... | collective-permute-start | bytes 589832 | tf_op jit(solution)/shard_map/ppermute | solution.py:469
  7.2 10.2 %collective-permute-start.2 = (f32[24,16,128]{2,1,0:T(8,128)S(1)}, f32[24,16,128]{2,1,0:T(8,128)S(1)}, u32[]{:S(2)}, u32[]{:S(2)}) collective-permute-start(f32[24,16,128]{2,1,0:T(8,128)S(1)} %get-tuple-element.67), channel_id=1, source_target_pairs={{0,1},{1,0},{2,3},{3,2},{4,5},{5,4},{6,7},{7,6},{8,9},{9,8},{10,11... | collective-permute-start | bytes 589832 | tf_op jit(solution)/shard_map/ppermute | solution.py:469
  7.7 9.7 %collective-permute-start.3 = (f32[24,16,128]{2,1,0:T(8,128)S(1)}, f32[24,16,128]{2,1,0:T(8,128)S(1)}, u32[]{:S(2)}, u32[]{:S(2)}) collective-permute-start(f32[24,16,128]{2,1,0:T(8,128)S(1)} %get-tuple-element.68), channel_id=1, source_target_pairs={{0,8},{1,2},{2,1},{3,4},{4,3},{5,6},{6,5},{7,15},{8,0},{9,10},{10,... | collective-permute-start | bytes 589832 | tf_op jit(solution)/shard_map/ppermute | solution.py:469
  10.3 7.1 %copy-start = (f32[1,1,64,128]{3,2,1,0:T(8,128)S(1)}, f32[1,1,64,128]{3,2,1,0:T(8,128)}, u32[]{:S(2)}) copy-start(f32[1,1,64,128]{3,2,1,0:T(8,128)} %param.10) | copy-start | bytes 98308
  19.6 7.8 %collective-permute-start.4 = (f32[24,16,128]{2,1,0:T(8,128)S(1)}, f32[24,16,128]{2,1,0:T(8,128)S(1)}, u32[]{:S(2)}, u32[]{:S(2)}) collective-permute-start(f32[24,16,128]{2,1,0:T(8,128)S(1)} %get-tuple-element.82), channel_id=1, source_target_pairs={{0,8},{1,9},{2,10},{3,11},{4,12},{5,13},{6,14},{7,15},{8,0},{9,1},... | collective-permute-start | bytes 589832 | tf_op jit(solution)/shard_map/ppermute | solution.py:469
  19.7 7.7 %collective-permute-start.5 = (f32[24,16,128]{2,1,0:T(8,128)S(1)}, f32[24,16,128]{2,1,0:T(8,128)S(1)}, u32[]{:S(2)}, u32[]{:S(2)}) collective-permute-start(f32[24,16,128]{2,1,0:T(8,128)S(1)} %get-tuple-element.83), channel_id=1, source_target_pairs={{0,1},{1,0},{2,3},{3,2},{4,5},{5,4},{6,7},{7,6},{8,16},{9,17},{10,... | collective-permute-start | bytes 589832 | tf_op jit(solution)/shard_map/ppermute | solution.py:469
  21.0 6.4 %collective-permute-start.6 = (f32[24,16,128]{2,1,0:T(8,128)S(1)}, f32[24,16,128]{2,1,0:T(8,128)S(1)}, u32[]{:S(2)}, u32[]{:S(2)}) collective-permute-start(f32[24,16,128]{2,1,0:T(8,128)S(1)} %get-tuple-element.84), channel_id=1, source_target_pairs={{0,1},{1,0},{2,3},{3,2},{4,5},{5,4},{6,7},{7,6},{8,9},{9,8},{10,11... | collective-permute-start | bytes 589832 | tf_op jit(solution)/shard_map/ppermute | solution.py:469
  21.0 7.4 %collective-permute-start.7 = (f32[24,16,128]{2,1,0:T(8,128)S(1)}, f32[24,16,128]{2,1,0:T(8,128)S(1)}, u32[]{:S(2)}, u32[]{:S(2)}) collective-permute-start(f32[24,16,128]{2,1,0:T(8,128)S(1)} %get-tuple-element.85), channel_id=1, source_target_pairs={{0,8},{1,2},{2,1},{3,4},{4,3},{5,6},{6,5},{7,15},{8,0},{9,10},{10,... | collective-permute-start | bytes 589832 | tf_op jit(solution)/shard_map/ppermute | solution.py:469
  30.6 9.0 %collective-permute-start.8 = (f32[24,16,128]{2,1,0:T(8,128)S(1)}, f32[24,16,128]{2,1,0:T(8,128)S(1)}, u32[]{:S(2)}, u32[]{:S(2)}) collective-permute-start(f32[24,16,128]{2,1,0:T(8,128)S(1)} %get-tuple-element.91), channel_id=1, source_target_pairs={{0,8},{1,9},{2,10},{3,11},{4,12},{5,13},{6,14},{7,15},{8,0},{9,1},... | collective-permute-start | bytes 589832 | tf_op jit(solution)/shard_map/ppermute | solution.py:469
  31.8 7.8 %collective-permute-start.9 = (f32[24,16,128]{2,1,0:T(8,128)S(1)}, f32[24,16,128]{2,1,0:T(8,128)S(1)}, u32[]{:S(2)}, u32[]{:S(2)}) collective-permute-start(f32[24,16,128]{2,1,0:T(8,128)S(1)} %get-tuple-element.92), channel_id=1, source_target_pairs={{0,1},{1,0},{2,3},{3,2},{4,5},{5,4},{6,7},{7,6},{8,16},{9,17},{10,... | collective-permute-start | bytes 589832 | tf_op jit(solution)/shard_map/ppermute | solution.py:469
  31.8 7.8 %collective-permute-start.10 = (f32[24,16,128]{2,1,0:T(8,128)S(1)}, f32[24,16,128]{2,1,0:T(8,128)S(1)}, u32[]{:S(2)}, u32[]{:S(2)}) collective-permute-start(f32[24,16,128]{2,1,0:T(8,128)S(1)} %get-tuple-element.93), channel_id=1, source_target_pairs={{0,1},{1,0},{2,3},{3,2},{4,5},{5,4},{6,7},{7,6},{8,9},{9,8},{10,11... | collective-permute-start | bytes 589832 | tf_op jit(solution)/shard_map/ppermute | solution.py:469
  32.3 7.3 %collective-permute-start.11 = (f32[24,16,128]{2,1,0:T(8,128)S(1)}, f32[24,16,128]{2,1,0:T(8,128)S(1)}, u32[]{:S(2)}, u32[]{:S(2)}) collective-permute-start(f32[24,16,128]{2,1,0:T(8,128)S(1)} %get-tuple-element.94), channel_id=1, source_target_pairs={{0,8},{1,2},{2,1},{3,4},{4,3},{5,6},{6,5},{7,15},{8,0},{9,10},{10,... | collective-permute-start | bytes 589832 | tf_op jit(solution)/shard_map/ppermute | solution.py:469
  41.2 5.3 %collective-permute-start.12 = (f32[12,16,128]{2,1,0:T(8,128)S(1)}, f32[12,16,128]{2,1,0:T(8,128)S(1)}, u32[]{:S(2)}, u32[]{:S(2)}) collective-permute-start(f32[12,16,128]{2,1,0:T(8,128)S(1)} %get-tuple-element.98), channel_id=1, source_target_pairs={{0,8},{1,9},{2,10},{3,11},{4,12},{5,13},{6,14},{7,15},{8,0},{9,1},... | collective-permute-start | bytes 294920 | tf_op jit(solution)/shard_map/ppermute | solution.py:469
  42.2 4.4 %collective-permute-start.13 = (f32[12,16,128]{2,1,0:T(8,128)S(1)}, f32[12,16,128]{2,1,0:T(8,128)S(1)}, u32[]{:S(2)}, u32[]{:S(2)}) collective-permute-start(f32[12,16,128]{2,1,0:T(8,128)S(1)} %get-tuple-element.99), channel_id=1, source_target_pairs={{0,1},{1,0},{2,3},{3,2},{4,5},{5,4},{6,7},{7,6},{8,16},{9,17},{10,... | collective-permute-start | bytes 294920 | tf_op jit(solution)/shard_map/ppermute | solution.py:469
  42.6 4.0 %collective-permute-start.14 = (f32[12,16,128]{2,1,0:T(8,128)S(1)}, f32[12,16,128]{2,1,0:T(8,128)S(1)}, u32[]{:S(2)}, u32[]{:S(2)}) collective-permute-start(f32[12,16,128]{2,1,0:T(8,128)S(1)} %get-tuple-element.100), channel_id=1, source_target_pairs={{0,1},{1,0},{2,3},{3,2},{4,5},{5,4},{6,7},{7,6},{8,9},{9,8},{10,11... | collective-permute-start | bytes 294920 | tf_op jit(solution)/shard_map/ppermute | solution.py:469
  42.7 4.6 %collective-permute-start.15 = (f32[12,16,128]{2,1,0:T(8,128)S(1)}, f32[12,16,128]{2,1,0:T(8,128)S(1)}, u32[]{:S(2)}, u32[]{:S(2)}) collective-permute-start(f32[12,16,128]{2,1,0:T(8,128)S(1)} %get-tuple-element.101), channel_id=1, source_target_pairs={{0,8},{1,2},{2,1},{3,4},{4,3},{5,6},{6,5},{7,15},{8,0},{9,10},{10,... | collective-permute-start | bytes 294920 | tf_op jit(solution)/shard_map/ppermute | solution.py:469
